TPU v7x, 32 devices: a whole 2x2x4 slice. The times are simulated.
32 devices in a mesh: group: 2 (over y), skill: 4 (over z), tensor: 2 (over core), dp: 2 (over x).
Axes of the slice: x: 2, y: 2, z: 4, core: 2. Of those that a mesh axis runs over, the one named last changes fastest.
Arguments:
- tokens: bfloat16 [12288, 8192], P(('group', 'skill'), ('tensor', 'dp')), parts along dimension 0, may hold values from -6 to 6
- base_weight: bfloat16 [8192, 1024], P(('tensor', 'dp')), may hold values from -0.0625 to 0.0625
- skill_down: bfloat16 [512, 8192, 16], P('skill', ('tensor', 'dp')), may hold values from -0.0625 to 0.0625
- skill_up: bfloat16 [512, 16, 1024], P('skill', None, ('tensor', 'dp')), may hold values from -1.5 to 1.5
- alloc: float32 [64, 512], P('group', 'skill'), parts along dimension 0, may hold values from -0.25 to 0.25
- block_tenant: int32 [96], P(('group', 'skill')), parts along dimension 0, may hold values from 0 to 31
- block_len: int32 [96], P(('group', 'skill')), parts along dimension 0, may hold values from 1 to 128, as said below
Outputs:
- values_out: bfloat16 [12288, 1024], P(('group', 'skill'), ('tensor', 'dp')), parts along dimension 0
There are 2 independent parts, one for each index of `group`. A program takes and returns all parts, laid end to end along the dimension named above; an argument that names none is the same for every part. Nothing has to cross between parts.
Inputs may be any that keep to these rules, and one draw needn't show every extreme that they name: `block_len`: each block holds between 1 and 128 live rows; some block is full in every draw.
All inputs are finite; a program needn't handle non-finite values.
Results may differ from a plain program's by a relative error of at most 0.015.
Values may be sent and summed in bfloat16 or wider, within the bound.
No kernel may reach another device: no remote copies, remote signals or barrier semaphores. Data moves between devices by JAX's collectives and lax.ppermute only.
A program may use at most 128 MiB of HBM per device.

v0:
```python
import jax
import jax.numpy as jnp
from jax import lax
from jax.sharding import PartitionSpec as P


def body(tokens, base_weight, skill_down, skill_up, alloc, block_tenant, block_len):
    rows, width = tokens.shape
    blocks = block_len.shape[0]
    block_rows = rows // blocks
    local_skills, slice_width, rank = skill_down.shape
    slice_out = skill_up.shape[2]
    down_size = slice_width * rank
    stacked = jnp.concatenate(
        [
            skill_down.reshape(local_skills, down_size),
            skill_up.reshape(local_skills, rank * slice_out),
        ],
        1,
    ).astype(jnp.float32)
    partial_sum = jnp.dot(alloc, stacked, precision=lax.Precision.HIGHEST)
    composed = lax.psum(partial_sum.astype(jnp.bfloat16), "skill")
    factors = jnp.take(composed, block_tenant, axis=0)
    down_part = factors[:, :down_size].reshape(blocks, slice_width, rank)
    up_part = factors[:, down_size:].reshape(blocks, rank, slice_out).astype(jnp.float32)
    grouped = tokens.reshape(blocks, block_rows, width)
    projected = jnp.einsum("bnd,bdr->bnr", grouped, down_part, preferred_element_type=jnp.float32)
    base_term = jnp.dot(tokens, base_weight, preferred_element_type=jnp.float32)
    lowrank = lax.psum(projected.astype(jnp.bfloat16), ("tensor", "dp")).astype(jnp.float32)
    base = lax.psum_scatter(
        base_term.astype(jnp.bfloat16), ("tensor", "dp"), scatter_dimension=1, tiled=True
    ).astype(jnp.float32)
    adapter = jnp.einsum("bnr,bro->bno", lowrank, up_part, precision=lax.Precision.HIGHEST)
    total = base.reshape(blocks, block_rows, slice_out) + adapter
    live = (jnp.arange(block_rows, dtype=jnp.int32)[None, :] < block_len[:, None])[:, :, None]
    return jnp.where(live, total, 0.0).astype(jnp.bfloat16).reshape(rows, slice_out)


def solution(mesh):
    placed = (
        P(("group", "skill"), ("tensor", "dp")),
        P(("tensor", "dp"), None),
        P("skill", ("tensor", "dp"), None),
        P("skill", None, ("tensor", "dp")),
        P("group", "skill"),
        P(("group", "skill")),
        P(("group", "skill")),
    )
    return jax.shard_map(
        body,
        mesh=mesh,
        in_specs=placed,
        out_specs=P(("group", "skill"), ("tensor", "dp")),
        check_vma=False,
    )
```

profile of v0, /device:TPU:0, one launch (start us, length us, event | category | flops | bytes accessed | tf_op | source)
XLA Modules:
  0.0 186.4 jit_solution(17813197591540322716)
XLA Ops:
  7.4 0.0 copy-start
  7.4 0.0 copy-start.1
  7.4 0.0 all-reduce.2.cloned.1.call-start
  7.4 13.5 %copy.8 = bf16[128,2048,16]{0,2,1:T(8,128)(2,1)} copy(bf16[128,2048,16]{1,2,0:T(8,128)(2,1)} %param.9) | data formatting | bytes 16777216 | tf_op args[2]
  20.9 0.0 copy-done.1
  20.9 1.0 copy.9
  21.8 0.0 copy-done
  21.9 26.1 %fusion = bf16[32,36864]{1,0:T(8,128)(2,1)} fusion(f32[32,128]{1,0:T(8,128)S(1)} %copy-done, bf16[128,4096]{0,1:T(8,128)(2,1)S(1)} %bitcast.21, bf16[128,32768]{0,1:T(8,128)(2,1)} %bitcast.19), kind=kOutput, calls=%fused_computation.2 | convolution fusion | flops 1831993344 | bytes 11812864 | tf_op jit(solution)/shard_map/dot_general | solution.py:21
  48.0 0.0 all-reduce.2.cloned.1.call-update
  48.0 0.0 copy-start.3
  48.0 0.0 copy-start.2
  48.0 0.0 reduce-scatter.2.cloned.1.call-start
  48.1 11.4 %convolution_convert_fusion.1 = bf16[1536,1024]{1,0:T(8,128)(2,1)} fusion(bf16[1536,2048]{1,0:T(8,128)(2,1)} %param.7, bf16[2048,1024]{1,0:T(8,128)(2,1)} %param.8), kind=kOutput, calls=%fused_computation.6 | convolution fusion | flops 6444023808 | bytes 13631488 | tf_op jit(solution)/shard_map/dot_general | solution.py:28
  59.5 0.0 reduce-scatter.2.cloned.1.call-update
  59.5 0.0 copy-done.3
  59.6 0.0 copy-done.2
  59.6 0.1 iota_compare_fusion
  59.6 86.9 %all-reduce.2.cloned.1.call-done = bf16[32,36864]{1,0:T(8,128)(2,1)} async-done(((bf16[32,36864]{1,0:T(8,128)(2,1)}), bf16[32,36864]{1,0:T(8,128)(2,1)}) %all-reduce.2.cloned.1.call-update) | async-done | bytes 2359312 | tf_op jit(solution)/shard_map/psum | solution.py:22
  146.5 3.9 %gather_fusion = bf16[12,36864]{1,0:T(8,128)(2,1)S(1)} fusion(bf16[32,36864]{1,0:T(8,128)(2,1)} %all-reduce.2.cloned.1.call-done, s32[1024]{0:T(1024)S(1)} %pad_clamp_fusion), kind=kCustom, calls=%fused_computation | custom fusion | bytes 1769520 | tf_op jit(solution)/shard_map/jit(_take)/gather | solution.py:23
  150.4 0.2 broadcast_select_fusion
  150.5 0.1 slice.10
  150.6 6.2 %reshape.54 = bf16[12,2048,16]{2,1,0:T(8,128)(2,1)} reshape(bf16[12,32768]{1,0:T(8,128)(2,1)S(1)} %slice.10) | data formatting | bytes 1572864 | tf_op jit(solution)/shard_map/reshape | solution.py:24
  156.8 6.5 %fusion.6 = bf16[12,128,16]{1,2,0:T(8,128)(2,1)S(1)} fusion(bf16[12,2048,16]{2,1,0:T(8,128)(2,1)} %reshape.54, bf16[12,128,2048]{2,1,0:T(8,128)(2,1)} %bitcast.20), kind=kOutput, calls=%fused_computation.12 | convolution fusion | flops 100687872 | bytes 7127040 | tf_op jit(solution)/shard_map/bnd,bdr->bnr/dot_general | solution.py:27
  163.3 13.2 %psum.15 = bf16[12,128,16]{1,2,0:T(8,128)(2,1)S(1)} all-reduce(bf16[12,128,16]{1,2,0:T(8,128)(2,1)S(1)} %fusion.6), channel_id=1, replica_groups=mesh['group'=2,'skill'=4,'tensor'=2,'dp'=2] {'tensor','dp'}, use_global_device_ids=true, to_apply=%region_2.3 | all-reduce | flops 24576 | bytes 98304 | tf_op jit(solution)/shard_map/psum | solution.py:29
  176.5 0.0 reduce-scatter.2.cloned.1.call-done
  176.5 2.5 %fusion.5 = bf16[12,128,256]{2,1,0:T(8,128)(2,1)} fusion(bf16[12,128,256]{2,1,0:T(8,128)(2,1)} %bitcast.24, bf16[12,128,16]{1,2,0:T(8,128)(2,1)S(1)} %psum.15, pred[12,128]{1,0:T(8,128)(4,1)S(1)} %iota_compare_fusion, bf16[16,16,256]{2,1,0:T(8,128)(2,1)S(1)} %bitcast.23), kind=kOutput, calls=%fused_computation.9 | convolution fusion | flops 14155776 | bytes 1722368 | tf_op jit(solution)/shard_map/bnr,bro->bno/dot_general | solution.py:33
  (5 shorter events, 0.1 us)
Async XLA Ops:
  7.4 14.5 %copy-start = (f32[32,128]{1,0:T(8,128)S(1)}, f32[32,128]{1,0:T(8,128)}, u32[]{:S(2)}) copy-start(f32[32,128]{1,0:T(8,128)} %param.11) | copy-start | bytes 49156
  7.4 13.5 %copy-start.1 = (bf16[128,16,256]{2,1,0:T(8,128)(2,1)S(1)}, bf16[128,16,256]{2,1,0:T(8,128)(2,1)}, u32[]{:S(2)}) copy-start(bf16[128,16,256]{2,1,0:T(8,128)(2,1)} %param.10) | copy-start | bytes 3145732
  7.4 139.1 %all-reduce.2.cloned.1.call-start = ((), (), s32[]{:S(2)}) async-start(), calls=%async_computation.2 | async-start | bytes 4718592 | tf_op jit(solution)/shard_map/psum | solution.py:22
  48.0 11.5 %copy-start.3 = (s32[12]{0:T(128)S(1)}, s32[12]{0:T(128)}, u32[]{:S(2)}) copy-start(s32[12]{0:T(128)} %param.12) | copy-start | bytes 148
  48.0 11.5 %copy-start.2 = (s32[12]{0:T(128)S(1)}, s32[12]{0:T(128)}, u32[]{:S(2)}) copy-start(s32[12]{0:T(128)} %param.13) | copy-start | bytes 148
  48.0 128.5 %reduce-scatter.2.cloned.1.call-start = ((), (), s32[]{:S(2)}) async-start(), calls=%async_computation.1 | async-start | bytes 3932160 | tf_op jit(solution)/shard_map/reduce_scatter | solution.py:30
Sparse Core Ops, SparseCore 0:
  48.1 98.3 all-reduce.1
Sparse Core Ops, SparseCore 1:
  59.6 40.5 reduce-scatter.1
where the time goes:
time: 187 us; the launch traced here: 186 us
  waiting for transfers between devices  86.9 us (46%)
  matrix products  46.5 us (25%)
  local copies, waits for them, and re-layouts  24.6 us (13%)
  between operations  15 us (8%)
  blocking collectives  13.2 us (7%)
    psum x1, waiting for transfers between devices, body(): composed = lax.psum(partial_sum.astype(jnp.bfloat16), 'skill')  86.9 us
    dot_general x1, matrix products, body(): partial_sum = jnp.dot(alloc, stacked, precision=lax.Precision.HIGHEST)  26.1 us
    unnamed x11, local copies, waits for them, and re-layouts  14.5 us
    psum x1, blocking collectives, body(): lax.psum(projected.astype(jnp.bfloat16), ('tensor', 'dp'))  13.2 us
    dot_general x1, matrix products, body(): base_term = jnp.dot(tokens, base_weight, preferred_element_type=jnp.float32)  11.4 us
    dot_general x1, matrix products, body(): jnp.einsum('bnd,bdr->bnr', grouped, down_part, preferred_element_type=jnp...  6.49 us
    reshape x1, local copies, waits for them, and re-layouts, body(): down_part = factors[:, :down_size].reshape(blocks, slice_width, rank)  6.16 us
    gather x1, local copies, waits for them, and re-layouts, body(): factors = jnp.take(composed, block_tenant, axis=0)  3.85 us
  transfers between devices with their start and end apart: 2, of which 1 were waited for; matrix products, arithmetic and copies ran while one was open for 15% of the time, Pallas kernels for 0%

commit v1 on v0

v1 whole, which is shorter than its diff:
```python
import functools

import jax
import jax.numpy as jnp
from jax import lax
from jax.experimental import pallas as pl
from jax.experimental.pallas import tpu as pltpu
from jax.sharding import PartitionSpec as P

F32, BF16, I32 = jnp.float32, jnp.bfloat16, jnp.int32
MIB = 1 << 20
VMEM = pl.BlockSpec(memory_space=pltpu.VMEM)
SMEM = pl.BlockSpec(memory_space=pltpu.SMEM)
LANES = 128
NT = (((1,), (1,)), ((), ()))
TN = (((0,), (0,)), ((), ()))


def call(kernel, *, vmem=32, flops=0, nbytes=0, **kwargs):
    return pl.pallas_call(
        kernel,
        compiler_params=pltpu.CompilerParams(vmem_limit_bytes=vmem * MIB),
        cost_estimate=pl.CostEstimate(flops=flops, bytes_accessed=nbytes, transcendentals=0),
        **kwargs,
    )


def tables_kernel(n, tenants, place_ref, *refs):
    arrays, tab_ref = refs[:n], refs[n]
    me = place_ref[0]
    blocks = arrays[0].shape[1]
    sub = lax.broadcasted_iota(I32, (tenants, tenants), 0)
    lane = lax.broadcasted_iota(I32, (tenants, tenants), 1)
    wide = lax.broadcasted_iota(I32, (tenants, LANES), 1)
    tenant = lax.broadcasted_iota(I32, (tenants, LANES), 0)
    one = lax.broadcasted_iota(I32, (tenants, blocks), 0)
    zs = [lax.rem(me - k + n, n) for k in range(n)]
    present = [
        jnp.max(jnp.where(one == arrays[k][0:1, :], 1.0, 0.0), axis=1, keepdims=True)
        for k in range(n)
    ]

    def union(keep):
        total = jnp.zeros((tenants, 1), F32)
        for z, here in zip(zs, present):
            total = jnp.maximum(total, here * jnp.where(keep(z), 1.0, 0.0))
        return total

    def positions(held):
        across = jnp.sum(jnp.where(sub == lane, held, 0.0), axis=0, keepdims=True)
        return jnp.sum(jnp.where(lane < sub, across, 0.0), axis=1, keepdims=True)

    def pack(held, value):
        slot = positions(held).astype(I32)
        chosen = jnp.logical_and(slot == wide, held > 0.5)
        return jnp.sum(jnp.where(chosen, value, 0.0), axis=0, keepdims=True)

    send_right, send_left = union(lambda z: z > me), union(lambda z: z < me)
    from_left, from_right = positions(union(lambda z: z >= me)), positions(union(lambda z: z <= me))
    number = tenant.astype(F32)
    right = pack(send_right, number), pack(send_right, from_left)
    left = pack(send_left, number), pack(send_left, from_right)
    own = jnp.concatenate([arrays[0][0:1, :], jnp.zeros((1, LANES - blocks), I32)], axis=1)
    mine = own == tenant

    def at(place, rows, otherwise):
        return jnp.where(me == place, rows, otherwise)

    none = jnp.zeros((1, LANES), F32)
    final_right = jnp.sum(jnp.where(mine, from_left, 0.0), axis=0, keepdims=True)
    final_left = jnp.sum(jnp.where(mine, from_right, 0.0), axis=0, keepdims=True)
    rows = []
    for part in (0, 1):
        for hop in range(n - 1):
            rows.append(at(hop, right[part], at(n - 1 - hop, left[part], none)))
    for hop in range(n - 1):
        rows.append(at(hop + 1, final_right, at(n - 2 - hop, final_left, none)))
    for row, value in enumerate(rows):
        tab_ref[row : row + 1, :] = value.astype(I32)
    tab_ref[len(rows) : len(rows) + 1, :] = own


def make_tables(n, tenants, place, arrays):
    rows = -(-(3 * (n - 1) + 1) // 8) * 8
    return call(
        functools.partial(tables_kernel, n, tenants),
        out_shape=jax.ShapeDtypeStruct((rows, LANES), I32),
        in_specs=[SMEM] + [VMEM] * n,
        out_specs=VMEM,
    )(place, *arrays)


def compose_kernel(rank, alloc_ref, skills_ref, own_ref, kron):
    tenants, skills = alloc_ref.shape
    depth = skills * rank

    @pl.when(pl.program_id(0) == 0)
    def _():
        at = lax.broadcasted_iota(I32, (skills, depth), 1)
        row = lax.broadcasted_iota(I32, (skills, depth), 0)
        inside = jnp.logical_and(at >= row * rank, at < (row + 1) * rank)
        repeat = jnp.where(inside, 1.0, 0.0).astype(BF16)
        spread = jnp.dot(alloc_ref[...].astype(BF16), repeat, preferred_element_type=F32)
        lane = lax.rem(lax.broadcasted_iota(I32, (rank, depth), 1), rank)
        diagonal = lane == lax.broadcasted_iota(I32, (rank, depth), 0)
        for t in range(tenants):
            kron[t * rank : (t + 1) * rank, :] = jnp.where(diagonal, spread[t : t + 1, :], 0.0).astype(BF16)

    own_ref[...] = jnp.dot(kron[...], skills_ref[...], preferred_element_type=F32).astype(BF16)


def compose(alloc, library, rank, tile):
    tenants, skills = alloc.shape
    depth, width = library.shape
    return call(
        functools.partial(compose_kernel, rank),
        vmem=24,
        flops=2 * tenants * rank * depth * width,
        nbytes=2 * (depth + tenants * rank) * width,
        grid=(width // tile,),
        in_specs=[
            pl.BlockSpec((tenants, skills), lambda j: (0, 0)),
            pl.BlockSpec((depth, tile), lambda j: (0, j)),
        ],
        out_specs=pl.BlockSpec((tenants * rank, tile), lambda j: (0, j)),
        out_shape=jax.ShapeDtypeStruct((tenants * rank, width), BF16),
        scratch_shapes=[pltpu.VMEM((tenants * rank, depth), BF16)],
    )(alloc, library)


def relay_kernel(hop, n, slots, tab_ref, own_ref, *refs):
    out_ref = refs[-1]

    def one(slot, carry):
        block = own_ref[tab_ref[hop, slot]]
        if hop:
            passed = refs[0][tab_ref[n - 1 + hop, slot]]
            block = (block.astype(F32) + passed.astype(F32)).astype(BF16)
        out_ref[slot] = block
        return carry

    lax.fori_loop(0, slots, one, 0, unroll=4)


def relay(hop, n, slots, tab, own, part, arrived):
    tenants, rank, _ = own.shape
    start, size = part
    at = start // size
    ins = [tab, own] + ([arrived] if hop else [])
    return call(
        functools.partial(relay_kernel, hop, n, slots),
        vmem=16,
        nbytes=2 * rank * size * (tenants + 2 * slots),
        grid=(1,),
        in_specs=[SMEM, pl.BlockSpec((tenants, rank, size), lambda j: (0, 0, at))] + [VMEM] * (1 if hop else 0),
        out_specs=VMEM,
        out_shape=jax.ShapeDtypeStruct((slots, rank, size), BF16),
    )(*ins)


def project_kernel(n, last, tab_ref, tokens_ref, own_ref, *refs):
    arrived, total_ref, out_ref = refs[: n - 1], refs[n - 1], refs[n]
    rank = own_ref.shape[1]
    blocks = tokens_ref.shape[0] // LANES

    for b in range(blocks):
        factor = own_ref[tab_ref[3 * (n - 1), b]].astype(F32)
        for hop in range(n - 1):
            factor = factor + arrived[hop][tab_ref[2 * (n - 1) + hop, b]].astype(F32)
        rows = tokens_ref[b * LANES : (b + 1) * LANES, :]
        part = lax.dot_general(factor.astype(BF16), rows, NT, preferred_element_type=F32)
        at = slice(b * LANES, (b + 1) * LANES)
        out_ref[:, at] = (total_ref[:, at] + part).astype(out_ref.dtype)


def project(n, tab, tokens, own, part, arrived, total, last):
    tenants, rank, _ = own.shape
    rows = tokens.shape[0]
    start, size = part
    at = start // size
    return call(
        functools.partial(project_kernel, n, last),
        vmem=24,
        flops=2 * rows * size * rank,
        nbytes=2 * size * (rows + 2 * tenants * rank),
        grid=(1,),
        in_specs=[
            SMEM,
            pl.BlockSpec((rows, size), lambda j: (0, at)),
            pl.BlockSpec((tenants, rank, size), lambda j: (0, 0, at)),
        ]
        + [VMEM] * n,
        out_specs=VMEM,
        out_shape=jax.ShapeDtypeStruct((rank, rows), BF16 if last else F32),
    )(tab, tokens, own, *arrived, total)


def base_kernel(order_ref, tokens_ref, weight_ref, away_ref, keep_ref):
    q = pl.program_id(0)
    product = jnp.dot(tokens_ref[...], weight_ref[...], preferred_element_type=F32).astype(BF16)

    @pl.when(q < 2)
    def _():
        away_ref[0] = product

    @pl.when(q >= 2)
    def _():
        keep_ref[0] = product


def base_product(order, tokens, weight):
    rows, width = tokens.shape
    out = weight.shape[1] // 4
    return pl.pallas_call(
        base_kernel,
        grid_spec=pltpu.PrefetchScalarGridSpec(
            num_scalar_prefetch=1,
            grid=(4,),
            in_specs=[
                pl.BlockSpec((rows, width), lambda q, order: (0, 0), pipeline_mode=pl.Buffered(1)),
                pl.BlockSpec((width, out), lambda q, order: (0, order[q])),
            ],
            out_specs=[
                pl.BlockSpec((1, rows, out), lambda q, order: (jnp.minimum(q, 1), 0, 0)),
                pl.BlockSpec((1, rows, out), lambda q, order: (jnp.maximum(q - 2, 0), 0, 0)),
            ],
        ),
        out_shape=[jax.ShapeDtypeStruct((2, rows, out), BF16)] * 2,
        compiler_params=pltpu.CompilerParams(vmem_limit_bytes=32 * MIB),
        cost_estimate=pl.CostEstimate(
            flops=8 * rows * width * out, bytes_accessed=2 * rows * (width + 4 * out) + 8 * width * out, transcendentals=0
        ),
    )(order, tokens, weight)


def finish_kernel(n, per, tab_ref, len_ref, own_ref, *refs):
    arrived, lows, bases, out_ref = refs[: n - 1], refs[n - 1 : n + 3], refs[n + 3 : n + 6], refs[n + 6]
    step = pl.program_id(0)
    width = out_ref.shape[1]
    for j in range(per):
        b = step * per + j
        up = own_ref[tab_ref[3 * (n - 1), b]].astype(F32)
        for hop in range(n - 1):
            up = up + arrived[hop][tab_ref[2 * (n - 1) + hop, b]].astype(F32)
        up = up.astype(BF16)
        at = slice(j * LANES, (j + 1) * LANES)
        low = lows[0][:, at].astype(F32)
        for other in lows[1:]:
            low = low + other[:, at].astype(F32)
        high = low.astype(BF16)
        rest = (low - high.astype(F32)).astype(BF16)
        adapter = lax.dot_general(high, up, TN, preferred_element_type=F32)
        adapter = adapter + lax.dot_general(rest, up, TN, preferred_element_type=F32)
        total = adapter
        for base in bases:
            total = total + base[at, :].astype(F32)
        live = lax.broadcasted_iota(I32, (LANES, width), 0) < len_ref[b]
        out_ref[at, :] = jnp.where(live, total, 0.0).astype(out_ref.dtype)


def finish(n, tab, lens, own, arrived, lows, bases, per):
    rank, rows = lows[0].shape
    width = bases[0].shape[1]
    blocks = rows // LANES
    return call(
        functools.partial(finish_kernel, n, per),
        vmem=24,
        flops=4 * rows * rank * width,
        nbytes=8 * rows * width,
        grid=(blocks // per,),
        in_specs=[SMEM, SMEM, VMEM]
        + [VMEM] * (n - 1)
        + [pl.BlockSpec((rank, per * LANES), lambda j: (0, j))] * 4
        + [pl.BlockSpec((per * LANES, width), lambda j: (j, 0))] * 3,
        out_specs=pl.BlockSpec((per * LANES, width), lambda j: (j, 0)),
        out_shape=jax.ShapeDtypeStruct((rows, width), BF16),
    )(tab, lens, own, *arrived, *lows, *bases)


def swap(x, axis):
    return lax.ppermute(x, axis, [(0, 1), (1, 0)])


def line_body(n, tokens, base_weight, skill_down, skill_up, alloc, block_tenant, block_len):
    rows, width = tokens.shape
    tenants, local_skills = alloc.shape
    rank = skill_down.shape[2]
    slice_out = skill_up.shape[2]
    blocks = block_len.shape[0]
    me = lax.axis_index("skill")
    tensor, dp = lax.axis_index("tensor"), lax.axis_index("dp")
    hops = [[(h, h + 1), (n - 1 - h, n - 2 - h)] for h in range(n - 1)]
    sizes = [min(tenants, blocks * (n - 1 - h)) for h in range(n - 1)]

    own_t = block_tenant.reshape(1, blocks)
    seen = [own_t] + [
        lax.ppermute(own_t, "skill", [(j, (j + k) % n) for j in range(n)]) for k in range(1, n)
    ]
    up = compose(alloc, skill_up.reshape(local_skills * rank, slice_out), rank, slice_out)
    up = up.reshape(tenants, rank, slice_out)
    library = jnp.transpose(skill_down, (0, 2, 1)).reshape(local_skills * rank, width)
    down = compose(alloc, library, rank, 256).reshape(tenants, rank, width)
    tab = make_tables(n, tenants, me.reshape(1).astype(I32), seen)

    def chain(own, part):
        arrived = []
        for h in range(n - 1):
            message = relay(h, n, sizes[h], tab, own, part, arrived[-1] if h else None)
            arrived.append(lax.ppermute(message, "skill", hops[h]))
        return arrived

    other, mine = (1 - tensor) * 2, tensor * 2
    order = jnp.stack([other + 1 - dp, other + dp, mine + 1 - dp, mine + dp]).astype(I32)
    away, keep = base_product(order, tokens, base_weight)
    from_core = swap(away, "tensor")
    across = swap((keep[0].astype(F32) + from_core[0].astype(F32)).astype(BF16), "dp")

    up_arrived = chain(up, (0, slice_out))
    size = 512
    parts = [(s, size) for s in range(0, width, size)]
    down_arrived = [chain(down, part) for part in parts]
    low = jnp.zeros((rank, rows), F32)
    for part, arrived in zip(parts, down_arrived):
        low = project(n, tab, tokens, down, part, arrived, low, part is parts[-1])
    lows = [low, swap(low, "tensor"), swap(low, "dp")]
    lows.append(lax.ppermute(low, ("tensor", "dp"), [(0, 3), (1, 2), (2, 1), (3, 0)]))
    return finish(n, tab, block_len, up, up_arrived, lows, [keep[1], from_core[1], across], 3)


def plain_body(tokens, base_weight, skill_down, skill_up, alloc, block_tenant, block_len):
    rows, width = tokens.shape
    blocks = block_len.shape[0]
    block_rows = rows // blocks
    local_skills, slice_width, rank = skill_down.shape
    slice_out = skill_up.shape[2]
    down_size = slice_width * rank
    stacked = jnp.concatenate(
        [
            skill_down.reshape(local_skills, down_size),
            skill_up.reshape(local_skills, rank * slice_out),
        ],
        1,
    ).astype(F32)
    partial_sum = jnp.dot(alloc, stacked, precision=lax.Precision.HIGHEST)
    composed = lax.psum(partial_sum.astype(BF16), "skill")
    factors = jnp.take(composed, block_tenant, axis=0)
    down_part = factors[:, :down_size].reshape(blocks, slice_width, rank)
    up_part = factors[:, down_size:].reshape(blocks, rank, slice_out).astype(F32)
    grouped = tokens.reshape(blocks, block_rows, width)
    projected = jnp.einsum("bnd,bdr->bnr", grouped, down_part, preferred_element_type=F32)
    base_term = jnp.dot(tokens, base_weight, preferred_element_type=F32)
    lowrank = lax.psum(projected.astype(BF16), ("tensor", "dp")).astype(F32)
    base = lax.psum_scatter(
        base_term.astype(BF16), ("tensor", "dp"), scatter_dimension=1, tiled=True
    ).astype(F32)
    adapter = jnp.einsum("bnr,bro->bno", lowrank, up_part, precision=lax.Precision.HIGHEST)
    total = base.reshape(blocks, block_rows, slice_out) + adapter
    live = (jnp.arange(block_rows, dtype=I32)[None, :] < block_len[:, None])[:, :, None]
    return jnp.where(live, total, 0.0).astype(BF16).reshape(rows, slice_out)


def solution(mesh):
    placed = (
        P(("group", "skill"), ("tensor", "dp")),
        P(("tensor", "dp"), None),
        P("skill", ("tensor", "dp"), None),
        P("skill", None, ("tensor", "dp")),
        P("group", "skill"),
        P(("group", "skill")),
        P(("group", "skill")),
    )
    n = mesh.shape["skill"]
    if n == 4 and mesh.shape["tensor"] == 2 and mesh.shape["dp"] == 2:
        body = functools.partial(line_body, n)
    else:
        body = plain_body
    return jax.shard_map(
        body,
        mesh=mesh,
        in_specs=placed,
        out_specs=P(("group", "skill"), ("tensor", "dp")),
        check_vma=False,
    )
```

time: 187 us -> 130 us (0.70)
  the two profiles are of different devices: /device:TPU:0 before, /device:TPU:9 now
where the time goes in v1:
time: 130 us; the launch traced here: 129 us
  waiting for transfers between devices  44 us (34%)
  starting transfers between devices  36.9 us (28%)
  Pallas kernels  36.9 us (28%)
  local copies, waits for them, and re-layouts  9.63 us (7%)
  other arithmetic  1.41 us (1%)
    ppermute x15, waiting for transfers between devices, chain(): arrived.append(lax.ppermute(message, 'skill', hops[h]))  37.9 us
    ppermute x15, starting transfers between devices, chain(): arrived.append(lax.ppermute(message, 'skill', hops[h]))  24.3 us
    pallas_call x15, Pallas kernels, relay(): call(functools.partial(relay_kernel, hop, n, slots), vmem=16, nbytes=2 *...  11.5 us
    pallas_call x1, Pallas kernels, base_product(): pl.pallas_call(base_kernel, grid_spec=pltpu.PrefetchScalarGridSpec(num_sc...  8.68 us
    pallas_call x2, Pallas kernels, compose(): call(functools.partial(compose_kernel, rank), vmem=24, flops=2 * tenants...  8.56 us
    unnamed x18, local copies, waits for them, and re-layouts  8.39 us
    ppermute x4, starting transfers between devices, swap(): return lax.ppermute(x, axis, [(0, 1), (1, 0)])  7.38 us
    ppermute x1, waiting for transfers between devices, line_body(): lax.ppermute(low, ('tensor', 'dp'), [(0, 3), (1, 2), (2, 1), (3, 0)])  5.13 us
  transfers between devices with their start and end apart: 23, of which 8 were waited for; matrix products, arithmetic and copies ran while one was open for 2% of the time, Pallas kernels for 26%

profile of v1, /device:TPU:9, one launch (start us, length us, event | category | flops | bytes accessed | tf_op | source)
XLA Modules:
  0.0 129.3 jit_solution(12061605476986543681)
XLA Ops:
  0.0 1.3 %collective-permute-start = (s32[1,12]{1,0:T(1,128)}, s32[1,12]{1,0:T(1,128)S(1)}, u32[]{:S(2)}, u32[]{:S(2)}) collective-permute-start(s32[1,12]{1,0:T(1,128)} %bitcast.40), channel_id=1, source_target_pairs={{0,4},{4,8},{8,12},{12,0},{1,5},{5,9},{9,13},{13,1},{2,6},{6,10},{... | collective-permute-start | bytes 152 | tf_op jit(solution)/shard_map/ppermute | solution.py:297
  1.3 1.0 collective-permute-start.1
  2.3 1.5 %collective-permute-start.2 = (s32[1,12]{1,0:T(1,128)}, s32[1,12]{1,0:T(1,128)S(1)}, u32[]{:S(2)}, u32[]{:S(2)}) collective-permute-start(s32[1,12]{1,0:T(1,128)} %bitcast.42), channel_id=1, source_target_pairs={{0,12},{4,0},{8,4},{12,8},{1,13},{5,1},{9,5},{13,9},{2,14},{6,2},{... | collective-permute-start | bytes 152 | tf_op jit(solution)/shard_map/ppermute | solution.py:297
  3.8 0.1 pad_add_fusion.order_ref
  3.9 2.8 %copy-done = bf16[1536,2048]{1,0:T(8,128)(2,1)S(1)} copy-done((bf16[1536,2048]{1,0:T(8,128)(2,1)S(1)}, bf16[1536,2048]{1,0:T(8,128)(2,1)}, u32[]{:S(2)}) %copy-start) | copy-done | bytes 6291480
  6.6 2.2 %copy-done.4 = bf16[2048,1024]{1,0:T(8,128)(2,1)S(1)} copy-done((bf16[2048,1024]{1,0:T(8,128)(2,1)S(1)}, bf16[2048,1024]{1,0:T(8,128)(2,1)}, u32[]{:S(2)}) %copy-start.4) | copy-done | bytes 4194328
  8.8 8.7 %shard_map.95 = (bf16[2,1536,256]{2,1,0:T(8,128)(2,1)S(1)}, bf16[2,1536,256]{2,1,0:T(8,128)(2,1)S(1)}) custom-call(s32[4]{0:T(128)S(1)} %pad_add_fusion.order_ref, bf16[1536,2048]{1,0:T(8,128)(2,1)S(1)} %copy-done, bf16[2048,1024]{1,0:T(8,128)(2,1)S(1)} %copy-done.4), custom_call_target="tpu_custom_call" | custom-call | flops 6442450944 | bytes 13631488 | tf_op jit(solution)/shard_map/pallas_call | solution.py:214
  17.5 1.6 %collective-permute-start.21 = (bf16[2,1536,256]{2,1,0:T(8,128)(2,1)S(1)}, bf16[2,1536,256]{2,1,0:T(8,128)(2,1)}, u32[]{:S(2)}, u32[]{:S(2)}) collective-permute-start(bf16[2,1536,256]{2,1,0:T(8,128)(2,1)S(1)} %get-tuple-element.8), channel_id=1, source_target_pairs={{0,2},{2,0},{1,3},{3,1},{4,6},{6,4},{5,7},{7,5},{8,10},{10,8},{9,1... | collective-permute-start | bytes 4718600 | tf_op jit(solution)/shard_map/ppermute | solution.py:281
  19.1 3.4 %copy-done.3 = bf16[128,2048,16]{1,2,0:T(8,128)(2,1)S(1)} copy-done((bf16[128,2048,16]{1,2,0:T(8,128)(2,1)S(1)}, bf16[128,2048,16]{1,2,0:T(8,128)(2,1)}, u32[]{:S(2)}) %copy-start.3) | copy-done | bytes 8388632
  22.5 7.7 %shard_map.78 = bf16[512,2048]{1,0:T(8,128)(2,1)S(1)} custom-call(f32[32,128]{1,0:T(8,128)S(1)} %copy-done.6, bf16[2048,2048]{1,0:T(8,128)(2,1)S(1)} %bitcast.44), custom_call_target="tpu_custom_call" | custom-call | flops 4294967296 | bytes 10485760 | tf_op jit(solution)/shard_map/pallas_call | solution.py:115
  30.2 0.2 shard_map.73.tab_ref
  30.5 0.7 shard_map.88
  31.2 1.3 collective-permute-start.15
  32.5 0.7 shard_map.85
  33.3 1.3 collective-permute-start.12
  34.6 0.7 shard_map.82
  35.3 1.4 %collective-permute-start.9 = (bf16[32,16,512]{2,1,0:T(8,128)(2,1)S(1)}, bf16[32,16,512]{2,1,0:T(8,128)(2,1)S(1)}, u32[]{:S(2)}, u32[]{:S(2)}) collective-permute-start(bf16[32,16,512]{2,1,0:T(8,128)(2,1)S(1)} %shard_map.82), channel_id=1, source_target_pairs={{0,4},{12,8},{1,5},{13,9},{2,6},{14,10},{3,7},{15,11},{16,20},{28,... | collective-permute-start | bytes 1572872 | tf_op jit(solution)/shard_map/ppermute | solution.py:309
  36.8 0.7 shard_map.79
  37.5 1.3 collective-permute-start.6
  38.8 0.9 shard_map.74
  39.7 0.7 shard_map.75
  40.4 6.2 %collective-permute-done.15.refs_0_ = bf16[32,16,512]{2,1,0:T(8,128)(2,1)S(1)} collective-permute-done((bf16[32,16,512]{2,1,0:T(8,128)(2,1)S(1)}, bf16[32,16,512]{2,1,0:T(8,128)(2,1)S(1)}, u32[]{:S(2)}, u32[]{:S(2)}) %collective-permute-start.15) | collective-permute-done | bytes 524320 | tf_op jit(solution)/shard_map/ppermute | solution.py:309
  46.6 1.3 collective-permute-start.3
  47.9 0.8 shard_map.89
  48.7 9.1 %collective-permute-done.12.refs_0_ = bf16[32,16,512]{2,1,0:T(8,128)(2,1)S(1)} collective-permute-done((bf16[32,16,512]{2,1,0:T(8,128)(2,1)S(1)}, bf16[32,16,512]{2,1,0:T(8,128)(2,1)S(1)}, u32[]{:S(2)}, u32[]{:S(2)}) %collective-permute-start.12) | collective-permute-done | bytes 524320 | tf_op jit(solution)/shard_map/ppermute | solution.py:309
  57.9 1.9 %collective-permute-start.16 = (bf16[24,16,512]{2,1,0:T(8,128)(2,1)S(1)}, bf16[24,16,512]{2,1,0:T(8,128)(2,1)S(1)}, u32[]{:S(2)}, u32[]{:S(2)}) collective-permute-start(bf16[24,16,512]{2,1,0:T(8,128)(2,1)S(1)} %shard_map.89), channel_id=1, source_target_pairs={{4,8},{8,4},{5,9},{9,5},{6,10},{10,6},{7,11},{11,7},{20,24},{24,20... | collective-permute-start | bytes 1179656 | tf_op jit(solution)/shard_map/ppermute | solution.py:309
  59.8 0.8 shard_map.86
  60.6 8.5 %collective-permute-done.9.refs_0_ = bf16[32,16,512]{2,1,0:T(8,128)(2,1)S(1)} collective-permute-done((bf16[32,16,512]{2,1,0:T(8,128)(2,1)S(1)}, bf16[32,16,512]{2,1,0:T(8,128)(2,1)S(1)}, u32[]{:S(2)}, u32[]{:S(2)}) %collective-permute-start.9) | collective-permute-done | bytes 524320 | tf_op jit(solution)/shard_map/ppermute | solution.py:309
  69.1 1.9 %collective-permute-start.13 = (bf16[24,16,512]{2,1,0:T(8,128)(2,1)S(1)}, bf16[24,16,512]{2,1,0:T(8,128)(2,1)S(1)}, u32[]{:S(2)}, u32[]{:S(2)}) collective-permute-start(bf16[24,16,512]{2,1,0:T(8,128)(2,1)S(1)} %shard_map.86), channel_id=1, source_target_pairs={{4,8},{8,4},{5,9},{9,5},{6,10},{10,6},{7,11},{11,7},{20,24},{24,20... | collective-permute-start | bytes 1179656 | tf_op jit(solution)/shard_map/ppermute | solution.py:309
  71.0 0.8 shard_map.83
  71.8 8.5 %collective-permute-done.6.refs_0_ = bf16[32,16,512]{2,1,0:T(8,128)(2,1)S(1)} collective-permute-done((bf16[32,16,512]{2,1,0:T(8,128)(2,1)S(1)}, bf16[32,16,512]{2,1,0:T(8,128)(2,1)S(1)}, u32[]{:S(2)}, u32[]{:S(2)}) %collective-permute-start.6) | collective-permute-done | bytes 524320 | tf_op jit(solution)/shard_map/ppermute | solution.py:309
  80.3 1.9 %collective-permute-start.10 = (bf16[24,16,512]{2,1,0:T(8,128)(2,1)S(1)}, bf16[24,16,512]{2,1,0:T(8,128)(2,1)S(1)}, u32[]{:S(2)}, u32[]{:S(2)}) collective-permute-start(bf16[24,16,512]{2,1,0:T(8,128)(2,1)S(1)} %shard_map.83), channel_id=1, source_target_pairs={{4,8},{8,4},{5,9},{9,5},{6,10},{10,6},{7,11},{11,7},{20,24},{24,20... | collective-permute-start | bytes 1179656 | tf_op jit(solution)/shard_map/ppermute | solution.py:309
  82.3 0.8 shard_map.80
  83.1 2.9 %collective-permute-done.3.refs_0_ = bf16[32,16,256]{2,1,0:T(8,128)(2,1)S(1)} collective-permute-done((bf16[32,16,256]{2,1,0:T(8,128)(2,1)S(1)}, bf16[32,16,256]{2,1,0:T(8,128)(2,1)S(1)}, u32[]{:S(2)}, u32[]{:S(2)}) %collective-permute-start.3) | collective-permute-done | bytes 262176 | tf_op jit(solution)/shard_map/ppermute | solution.py:309
  86.0 1.9 %collective-permute-start.7 = (bf16[24,16,512]{2,1,0:T(8,128)(2,1)S(1)}, bf16[24,16,512]{2,1,0:T(8,128)(2,1)S(1)}, u32[]{:S(2)}, u32[]{:S(2)}) collective-permute-start(bf16[24,16,512]{2,1,0:T(8,128)(2,1)S(1)} %shard_map.80), channel_id=1, source_target_pairs={{4,8},{8,4},{5,9},{9,5},{6,10},{10,6},{7,11},{11,7},{20,24},{24,20... | collective-permute-start | bytes 1179656 | tf_op jit(solution)/shard_map/ppermute | solution.py:309
  87.9 0.8 shard_map.76
  88.7 3.4 %collective-permute-start.4 = (bf16[24,16,256]{2,1,0:T(8,128)(2,1)S(1)}, bf16[24,16,256]{2,1,0:T(8,128)(2,1)S(1)}, u32[]{:S(2)}, u32[]{:S(2)}) collective-permute-start(bf16[24,16,256]{2,1,0:T(8,128)(2,1)S(1)} %shard_map.76), channel_id=1, source_target_pairs={{4,8},{8,4},{5,9},{9,5},{6,10},{10,6},{7,11},{11,7},{20,24},{24,20... | collective-permute-start | bytes 589832 | tf_op jit(solution)/shard_map/ppermute | solution.py:309
  92.1 0.0 slice-start
  92.1 0.7 shard_map.90
  92.8 1.4 %collective-permute-start.17 = (bf16[12,16,512]{2,1,0:T(8,128)(2,1)S(1)}, bf16[12,16,512]{2,1,0:T(8,128)(2,1)S(1)}, u32[]{:S(2)}, u32[]{:S(2)}) collective-permute-start(bf16[12,16,512]{2,1,0:T(8,128)(2,1)S(1)} %shard_map.90), channel_id=1, source_target_pairs={{8,12},{4,0},{9,13},{5,1},{10,14},{6,2},{11,15},{7,3},{24,28},{20,... | collective-permute-start | bytes 589832 | tf_op jit(solution)/shard_map/ppermute | solution.py:309
  94.3 0.7 shard_map.87
  95.0 0.0 slice-start.1
  95.1 1.4 %collective-permute-start.14 = (bf16[12,16,512]{2,1,0:T(8,128)(2,1)S(1)}, bf16[12,16,512]{2,1,0:T(8,128)(2,1)S(1)}, u32[]{:S(2)}, u32[]{:S(2)}) collective-permute-start(bf16[12,16,512]{2,1,0:T(8,128)(2,1)S(1)} %shard_map.87), channel_id=1, source_target_pairs={{8,12},{4,0},{9,13},{5,1},{10,14},{6,2},{11,15},{7,3},{24,28},{20,... | collective-permute-start | bytes 589832 | tf_op jit(solution)/shard_map/ppermute | solution.py:309
  96.5 0.7 shard_map.84
  97.3 2.8 %collective-permute-done.7.refs_0_.refs_1_ = bf16[24,16,512]{2,1,0:T(8,128)(2,1)S(1)} collective-permute-done((bf16[24,16,512]{2,1,0:T(8,128)(2,1)S(1)}, bf16[24,16,512]{2,1,0:T(8,128)(2,1)S(1)}, u32[]{:S(2)}, u32[]{:S(2)}) %collective-permute-start.7) | collective-permute-done | bytes 393248 | tf_op jit(solution)/shard_map/ppermute | solution.py:309
  100.0 1.3 collective-permute-start.11
  101.3 0.7 shard_map.81
  102.1 1.3 %collective-permute-start.8 = (bf16[12,16,512]{2,1,0:T(8,128)(2,1)S(1)}, bf16[12,16,512]{2,1,0:T(8,128)(2,1)S(1)}, u32[]{:S(2)}, u32[]{:S(2)}) collective-permute-start(bf16[12,16,512]{2,1,0:T(8,128)(2,1)S(1)} %shard_map.81), channel_id=1, source_target_pairs={{8,12},{4,0},{9,13},{5,1},{10,14},{6,2},{11,15},{7,3},{24,28},{20,... | collective-permute-start | bytes 589832 | tf_op jit(solution)/shard_map/ppermute | solution.py:309
  103.4 1.3 %fusion = bf16[1536,256]{1,0:T(8,128)(2,1)S(1)} fusion(bf16[2,1536,256]{2,1,0:T(8,128)(2,1)} %collective-permute-done.21, bf16[2,1536,256]{2,1,0:T(8,128)(2,1)S(1)} %get-tuple-element.7), kind=kLoop, calls=%fused_computation.1 | loop fusion | flops 1572864 | bytes 2359296 | tf_op jit(solution)/shard_map/convert_element_type | solution.py:316
  104.7 1.3 collective-permute-start.22
  106.0 0.1 slice_bitcast_fusion.1.refs_7_
  106.1 0.7 shard_map.77
  106.8 1.3 %collective-permute-start.5 = (bf16[12,16,256]{2,1,0:T(8,128)(2,1)S(1)}, bf16[12,16,256]{2,1,0:T(8,128)(2,1)S(1)}, u32[]{:S(2)}, u32[]{:S(2)}) collective-permute-start(bf16[12,16,256]{2,1,0:T(8,128)(2,1)S(1)} %shard_map.77), channel_id=1, source_target_pairs={{8,12},{4,0},{9,13},{5,1},{10,14},{6,2},{11,15},{7,3},{24,28},{20,... | collective-permute-start | bytes 294920 | tf_op jit(solution)/shard_map/ppermute | solution.py:309
  108.2 1.2 shard_map.91.refs_3_
  109.3 1.2 shard_map.92.refs_3_
  110.6 1.2 shard_map.93.refs_3_
  111.8 1.2 shard_map.94.refs_3_
  113.0 4.2 %collective-permute-start.18 = (bf16[16,1536]{1,0:T(8,128)(2,1)S(1)}, bf16[16,1536]{1,0:T(8,128)(2,1)S(1)}, u32[]{:S(2)}, u32[]{:S(2)}) collective-permute-start(bf16[16,1536]{1,0:T(8,128)(2,1)S(1)} %shard_map.94.refs_3_), channel_id=1, source_target_pairs={{0,2},{2,0},{1,3},{3,1},{4,6},{6,4},{5,7},{7,5},{8,10},{10,8},{9,1... | collective-permute-start | bytes 147464 | tf_op jit(solution)/shard_map/ppermute | solution.py:281
  117.2 0.3 collective-permute-start.19
  117.5 1.4 %collective-permute-start.20 = (bf16[16,1536]{1,0:T(8,128)(2,1)S(1)}, bf16[16,1536]{1,0:T(8,128)(2,1)S(1)}, u32[]{:S(2)}, u32[]{:S(2)}) collective-permute-start(bf16[16,1536]{1,0:T(8,128)(2,1)S(1)} %shard_map.94.refs_3_), channel_id=1, source_target_pairs={{0,3},{1,2},{2,1},{3,0},{4,7},{5,6},{6,5},{7,4},{8,11},{9,10},{10,... | collective-permute-start | bytes 147464 | tf_op jit(solution)/shard_map/ppermute | solution.py:326
  118.9 1.2 slice_bitcast_fusion.refs_8_
  120.1 0.9 collective-permute-done.19.refs_5_
  121.0 5.1 %collective-permute-done.20.refs_6_ = bf16[16,1536]{1,0:T(8,128)(2,1)S(1)} collective-permute-done((bf16[16,1536]{1,0:T(8,128)(2,1)S(1)}, bf16[16,1536]{1,0:T(8,128)(2,1)S(1)}, u32[]{:S(2)}, u32[]{:S(2)}) %collective-permute-start.20) | collective-permute-done | bytes 49184 | tf_op jit(solution)/shard_map/ppermute | solution.py:326
  126.2 3.1 %shard_map.96 = bf16[1536,256]{1,0:T(8,128)(2,1)} custom-call(s32[16,128]{1,0:T(8,128)S(1)} %shard_map.73.tab_ref, s32[12]{0:T(128)S(1)} %copy-done.1, bf16[32,16,256]{2,1,0:T(8,128)(2,1)S(1)} %bitcast.39, bf16[32,16,256]{2,1,0:T(8,128)(2,1)S(1)} %collective-permute-done.3.refs_0_, bf16[24,16,256]{2,1,0:T(8,128)(2,1)S(1)} %collective-permute-done.4.refs_0_.refs_1_, ...), custom_call_target="tpu_custom_call" | custom-call | flops 25165824 | bytes 3145728 | tf_op jit(solution)/shard_map/pallas_call | solution.py:265
  (30 shorter events, 0.1 us)
Async XLA Ops:
  0.0 30.2 %collective-permute-start = (s32[1,12]{1,0:T(1,128)}, s32[1,12]{1,0:T(1,128)S(1)}, u32[]{:S(2)}, u32[]{:S(2)}) collective-permute-start(s32[1,12]{1,0:T(1,128)} %bitcast.40), channel_id=1, source_target_pairs={{0,4},{4,8},{8,12},{12,0},{1,5},{5,9},{9,13},{13,1},{2,6},{6,10},{... | collective-permute-start | bytes 152 | tf_op jit(solution)/shard_map/ppermute | solution.py:297
  1.3 28.9 %collective-permute-start.1 = (s32[1,12]{1,0:T(1,128)}, s32[1,12]{1,0:T(1,128)S(1)}, u32[]{:S(2)}, u32[]{:S(2)}) collective-permute-start(s32[1,12]{1,0:T(1,128)} %bitcast.41), channel_id=1, source_target_pairs={{0,8},{4,12},{8,0},{12,4},{1,9},{5,13},{9,1},{13,5},{2,10},{6,14},... | collective-permute-start | bytes 152 | tf_op jit(solution)/shard_map/ppermute | solution.py:297
  2.3 27.9 %collective-permute-start.2 = (s32[1,12]{1,0:T(1,128)}, s32[1,12]{1,0:T(1,128)S(1)}, u32[]{:S(2)}, u32[]{:S(2)}) collective-permute-start(s32[1,12]{1,0:T(1,128)} %bitcast.42), channel_id=1, source_target_pairs={{0,12},{4,0},{8,4},{12,8},{1,13},{5,1},{9,5},{13,9},{2,14},{6,2},{... | collective-permute-start | bytes 152 | tf_op jit(solution)/shard_map/ppermute | solution.py:297
  3.9 2.8 %copy-start = (bf16[1536,2048]{1,0:T(8,128)(2,1)S(1)}, bf16[1536,2048]{1,0:T(8,128)(2,1)}, u32[]{:S(2)}) copy-start(bf16[1536,2048]{1,0:T(8,128)(2,1)} %tokens_ref.9) | copy-start | bytes 18874372
  6.6 2.2 %copy-start.4 = (bf16[2048,1024]{1,0:T(8,128)(2,1)S(1)}, bf16[2048,1024]{1,0:T(8,128)(2,1)}, u32[]{:S(2)}) copy-start(bf16[2048,1024]{1,0:T(8,128)(2,1)} %weight_ref.1) | copy-start | bytes 12582916
  8.8 10.3 %copy-start.6 = (f32[32,128]{1,0:T(8,128)S(1)}, f32[32,128]{1,0:T(8,128)}, u32[]{:S(2)}) copy-start(f32[32,128]{1,0:T(8,128)} %alloc_ref.3) | copy-start | bytes 49156
  17.5 84.5 %collective-permute-start.21 = (bf16[2,1536,256]{2,1,0:T(8,128)(2,1)S(1)}, bf16[2,1536,256]{2,1,0:T(8,128)(2,1)}, u32[]{:S(2)}, u32[]{:S(2)}) collective-permute-start(bf16[2,1536,256]{2,1,0:T(8,128)(2,1)S(1)} %get-tuple-element.8), channel_id=1, source_target_pairs={{0,2},{2,0},{1,3},{3,1},{4,6},{6,4},{5,7},{7,5},{8,10},{10,8},{9,1... | collective-permute-start | bytes 4718600 | tf_op jit(solution)/shard_map/ppermute | solution.py:281
  19.1 3.4 %copy-start.3 = (bf16[128,2048,16]{1,2,0:T(8,128)(2,1)S(1)}, bf16[128,2048,16]{1,2,0:T(8,128)(2,1)}, u32[]{:S(2)}) copy-start(bf16[128,2048,16]{1,2,0:T(8,128)(2,1)} %param.9) | copy-start | bytes 25165828
  22.5 7.7 %copy-start.2 = (s32[12]{0:T(128)S(1)}, s32[12]{0:T(128)}, u32[]{:S(2)}) copy-start(s32[12]{0:T(128)} %param.12) | copy-start | bytes 148
  31.2 15.4 %collective-permute-start.15 = (bf16[32,16,512]{2,1,0:T(8,128)(2,1)S(1)}, bf16[32,16,512]{2,1,0:T(8,128)(2,1)S(1)}, u32[]{:S(2)}, u32[]{:S(2)}) collective-permute-start(bf16[32,16,512]{2,1,0:T(8,128)(2,1)S(1)} %shard_map.88), channel_id=1, source_target_pairs={{0,4},{12,8},{1,5},{13,9},{2,6},{14,10},{3,7},{15,11},{16,20},{28,... | collective-permute-start | bytes 1572872 | tf_op jit(solution)/shard_map/ppermute | solution.py:309
  33.3 24.6 %collective-permute-start.12 = (bf16[32,16,512]{2,1,0:T(8,128)(2,1)S(1)}, bf16[32,16,512]{2,1,0:T(8,128)(2,1)S(1)}, u32[]{:S(2)}, u32[]{:S(2)}) collective-permute-start(bf16[32,16,512]{2,1,0:T(8,128)(2,1)S(1)} %shard_map.85), channel_id=1, source_target_pairs={{0,4},{12,8},{1,5},{13,9},{2,6},{14,10},{3,7},{15,11},{16,20},{28,... | collective-permute-start | bytes 1572872 | tf_op jit(solution)/shard_map/ppermute | solution.py:309
  35.3 3.5 %copy-start.5 = (bf16[128,16,256]{2,1,0:T(8,128)(2,1)S(1)}, bf16[128,16,256]{2,1,0:T(8,128)(2,1)}, u32[]{:S(2)}) copy-start(bf16[128,16,256]{2,1,0:T(8,128)(2,1)} %param.10) | copy-start | bytes 3145732
  35.3 33.8 %collective-permute-start.9 = (bf16[32,16,512]{2,1,0:T(8,128)(2,1)S(1)}, bf16[32,16,512]{2,1,0:T(8,128)(2,1)S(1)}, u32[]{:S(2)}, u32[]{:S(2)}) collective-permute-start(bf16[32,16,512]{2,1,0:T(8,128)(2,1)S(1)} %shard_map.82), channel_id=1, source_target_pairs={{0,4},{12,8},{1,5},{13,9},{2,6},{14,10},{3,7},{15,11},{16,20},{28,... | collective-permute-start | bytes 1572872 | tf_op jit(solution)/shard_map/ppermute | solution.py:309
  37.5 42.8 %collective-permute-start.6 = (bf16[32,16,512]{2,1,0:T(8,128)(2,1)S(1)}, bf16[32,16,512]{2,1,0:T(8,128)(2,1)S(1)}, u32[]{:S(2)}, u32[]{:S(2)}) collective-permute-start(bf16[32,16,512]{2,1,0:T(8,128)(2,1)S(1)} %shard_map.79), channel_id=1, source_target_pairs={{0,4},{12,8},{1,5},{13,9},{2,6},{14,10},{3,7},{15,11},{16,20},{28,... | collective-permute-start | bytes 1572872 | tf_op jit(solution)/shard_map/ppermute | solution.py:309
  46.6 39.3 %collective-permute-start.3 = (bf16[32,16,256]{2,1,0:T(8,128)(2,1)S(1)}, bf16[32,16,256]{2,1,0:T(8,128)(2,1)S(1)}, u32[]{:S(2)}, u32[]{:S(2)}) collective-permute-start(bf16[32,16,256]{2,1,0:T(8,128)(2,1)S(1)} %shard_map.75), channel_id=1, source_target_pairs={{0,4},{12,8},{1,5},{13,9},{2,6},{14,10},{3,7},{15,11},{16,20},{28,... | collective-permute-start | bytes 786440 | tf_op jit(solution)/shard_map/ppermute | solution.py:309
  57.9 30.8 %collective-permute-start.16 = (bf16[24,16,512]{2,1,0:T(8,128)(2,1)S(1)}, bf16[24,16,512]{2,1,0:T(8,128)(2,1)S(1)}, u32[]{:S(2)}, u32[]{:S(2)}) collective-permute-start(bf16[24,16,512]{2,1,0:T(8,128)(2,1)S(1)} %shard_map.89), channel_id=1, source_target_pairs={{4,8},{8,4},{5,9},{9,5},{6,10},{10,6},{7,11},{11,7},{20,24},{24,20... | collective-permute-start | bytes 1179656 | tf_op jit(solution)/shard_map/ppermute | solution.py:309
  69.1 23.7 %collective-permute-start.13 = (bf16[24,16,512]{2,1,0:T(8,128)(2,1)S(1)}, bf16[24,16,512]{2,1,0:T(8,128)(2,1)S(1)}, u32[]{:S(2)}, u32[]{:S(2)}) collective-permute-start(bf16[24,16,512]{2,1,0:T(8,128)(2,1)S(1)} %shard_map.86), channel_id=1, source_target_pairs={{4,8},{8,4},{5,9},{9,5},{6,10},{10,6},{7,11},{11,7},{20,24},{24,20... | collective-permute-start | bytes 1179656 | tf_op jit(solution)/shard_map/ppermute | solution.py:309
  80.3 14.7 %collective-permute-start.10 = (bf16[24,16,512]{2,1,0:T(8,128)(2,1)S(1)}, bf16[24,16,512]{2,1,0:T(8,128)(2,1)S(1)}, u32[]{:S(2)}, u32[]{:S(2)}) collective-permute-start(bf16[24,16,512]{2,1,0:T(8,128)(2,1)S(1)} %shard_map.83), channel_id=1, source_target_pairs={{4,8},{8,4},{5,9},{9,5},{6,10},{10,6},{7,11},{11,7},{20,24},{24,20... | collective-permute-start | bytes 1179656 | tf_op jit(solution)/shard_map/ppermute | solution.py:309
  86.0 14.1 %collective-permute-start.7 = (bf16[24,16,512]{2,1,0:T(8,128)(2,1)S(1)}, bf16[24,16,512]{2,1,0:T(8,128)(2,1)S(1)}, u32[]{:S(2)}, u32[]{:S(2)}) collective-permute-start(bf16[24,16,512]{2,1,0:T(8,128)(2,1)S(1)} %shard_map.80), channel_id=1, source_target_pairs={{4,8},{8,4},{5,9},{9,5},{6,10},{10,6},{7,11},{11,7},{20,24},{24,20... | collective-permute-start | bytes 1179656 | tf_op jit(solution)/shard_map/ppermute | solution.py:309
  88.7 16.0 %collective-permute-start.4 = (bf16[24,16,256]{2,1,0:T(8,128)(2,1)S(1)}, bf16[24,16,256]{2,1,0:T(8,128)(2,1)S(1)}, u32[]{:S(2)}, u32[]{:S(2)}) collective-permute-start(bf16[24,16,256]{2,1,0:T(8,128)(2,1)S(1)} %shard_map.76), channel_id=1, source_target_pairs={{4,8},{8,4},{5,9},{9,5},{6,10},{10,6},{7,11},{11,7},{20,24},{24,20... | collective-permute-start | bytes 589832 | tf_op jit(solution)/shard_map/ppermute | solution.py:309
  92.1 16.1 %slice-start = ((s8[6291456]{0:T(1024)(128)(4,1)}), s8[4194304]{0:T(1024)(128)(4,1)S(1)}, s32[]{:S(2)}) async-start(s8[6291456]{0:T(1024)(128)(4,1)} %bitcast.34), calls=%async_computation | async-start | bytes 8388608
  92.8 14.0 %collective-permute-start.17 = (bf16[12,16,512]{2,1,0:T(8,128)(2,1)S(1)}, bf16[12,16,512]{2,1,0:T(8,128)(2,1)S(1)}, u32[]{:S(2)}, u32[]{:S(2)}) collective-permute-start(bf16[12,16,512]{2,1,0:T(8,128)(2,1)S(1)} %shard_map.90), channel_id=1, source_target_pairs={{8,12},{4,0},{9,13},{5,1},{10,14},{6,2},{11,15},{7,3},{24,28},{20,... | collective-permute-start | bytes 589832 | tf_op jit(solution)/shard_map/ppermute | solution.py:309
  95.0 13.1 %slice-start.1 = ((s8[6291456]{0:T(1024)(128)(4,1)}), s8[2097152]{0:T(1024)(128)(4,1)S(1)}, s32[]{:S(2)}) async-start(s8[6291456]{0:T(1024)(128)(4,1)} %bitcast.34), calls=%async_computation.1 | async-start | bytes 4194304
  95.1 14.3 %collective-permute-start.14 = (bf16[12,16,512]{2,1,0:T(8,128)(2,1)S(1)}, bf16[12,16,512]{2,1,0:T(8,128)(2,1)S(1)}, u32[]{:S(2)}, u32[]{:S(2)}) collective-permute-start(bf16[12,16,512]{2,1,0:T(8,128)(2,1)S(1)} %shard_map.87), channel_id=1, source_target_pairs={{8,12},{4,0},{9,13},{5,1},{10,14},{6,2},{11,15},{7,3},{24,28},{20,... | collective-permute-start | bytes 589832 | tf_op jit(solution)/shard_map/ppermute | solution.py:309
  100.0 10.5 %collective-permute-start.11 = (bf16[12,16,512]{2,1,0:T(8,128)(2,1)S(1)}, bf16[12,16,512]{2,1,0:T(8,128)(2,1)S(1)}, u32[]{:S(2)}, u32[]{:S(2)}) collective-permute-start(bf16[12,16,512]{2,1,0:T(8,128)(2,1)S(1)} %shard_map.84), channel_id=1, source_target_pairs={{8,12},{4,0},{9,13},{5,1},{10,14},{6,2},{11,15},{7,3},{24,28},{20,... | collective-permute-start | bytes 589832 | tf_op jit(solution)/shard_map/ppermute | solution.py:309
  102.1 9.7 %collective-permute-start.8 = (bf16[12,16,512]{2,1,0:T(8,128)(2,1)S(1)}, bf16[12,16,512]{2,1,0:T(8,128)(2,1)S(1)}, u32[]{:S(2)}, u32[]{:S(2)}) collective-permute-start(bf16[12,16,512]{2,1,0:T(8,128)(2,1)S(1)} %shard_map.81), channel_id=1, source_target_pairs={{8,12},{4,0},{9,13},{5,1},{10,14},{6,2},{11,15},{7,3},{24,28},{20,... | collective-permute-start | bytes 589832 | tf_op jit(solution)/shard_map/ppermute | solution.py:309
  104.7 21.4 %collective-permute-start.22 = (bf16[1536,256]{1,0:T(8,128)(2,1)S(1)}, bf16[1536,256]{1,0:T(8,128)(2,1)S(1)}, u32[]{:S(2)}, u32[]{:S(2)}) collective-permute-start(bf16[1536,256]{1,0:T(8,128)(2,1)S(1)} %fusion), channel_id=1, source_target_pairs={{0,1},{1,0},{2,3},{3,2},{4,5},{5,4},{6,7},{7,6},{8,9},{9,8},{10,11... | collective-permute-start | bytes 2359304 | tf_op jit(solution)/shard_map/ppermute | solution.py:281
  106.8 13.3 %collective-permute-start.5 = (bf16[12,16,256]{2,1,0:T(8,128)(2,1)S(1)}, bf16[12,16,256]{2,1,0:T(8,128)(2,1)S(1)}, u32[]{:S(2)}, u32[]{:S(2)}) collective-permute-start(bf16[12,16,256]{2,1,0:T(8,128)(2,1)S(1)} %shard_map.77), channel_id=1, source_target_pairs={{8,12},{4,0},{9,13},{5,1},{10,14},{6,2},{11,15},{7,3},{24,28},{20,... | collective-permute-start | bytes 294920 | tf_op jit(solution)/shard_map/ppermute | solution.py:309
  113.0 13.2 %copy-start.1 = (s32[12]{0:T(128)S(1)}, s32[12]{0:T(128)}, u32[]{:S(2)}) copy-start(s32[12]{0:T(128)} %len_ref.1) | copy-start | bytes 148
  113.0 7.2 %collective-permute-start.18 = (bf16[16,1536]{1,0:T(8,128)(2,1)S(1)}, bf16[16,1536]{1,0:T(8,128)(2,1)S(1)}, u32[]{:S(2)}, u32[]{:S(2)}) collective-permute-start(bf16[16,1536]{1,0:T(8,128)(2,1)S(1)} %shard_map.94.refs_3_), channel_id=1, source_target_pairs={{0,2},{2,0},{1,3},{3,1},{4,6},{6,4},{5,7},{7,5},{8,10},{10,8},{9,1... | collective-permute-start | bytes 147464 | tf_op jit(solution)/shard_map/ppermute | solution.py:281
  117.2 3.8 %collective-permute-start.19 = (bf16[16,1536]{1,0:T(8,128)(2,1)S(1)}, bf16[16,1536]{1,0:T(8,128)(2,1)S(1)}, u32[]{:S(2)}, u32[]{:S(2)}) collective-permute-start(bf16[16,1536]{1,0:T(8,128)(2,1)S(1)} %shard_map.94.refs_3_), channel_id=1, source_target_pairs={{0,1},{1,0},{2,3},{3,2},{4,5},{5,4},{6,7},{7,6},{8,9},{9,8},{10,11... | collective-permute-start | bytes 147464 | tf_op jit(solution)/shard_map/ppermute | solution.py:281
  117.5 8.7 %collective-permute-start.20 = (bf16[16,1536]{1,0:T(8,128)(2,1)S(1)}, bf16[16,1536]{1,0:T(8,128)(2,1)S(1)}, u32[]{:S(2)}, u32[]{:S(2)}) collective-permute-start(bf16[16,1536]{1,0:T(8,128)(2,1)S(1)} %shard_map.94.refs_3_), channel_id=1, source_target_pairs={{0,3},{1,2},{2,1},{3,0},{4,7},{5,6},{6,5},{7,4},{8,11},{9,10},{10,... | collective-permute-start | bytes 147464 | tf_op jit(solution)/shard_map/ppermute | solution.py:326

commit v2 on v0

v2 whole, which is shorter than its diff:
```python
import functools

import jax
import jax.numpy as jnp
from jax import lax
from jax.experimental import pallas as pl
from jax.experimental.pallas import tpu as pltpu
from jax.sharding import PartitionSpec as P

F32, BF16, I32 = jnp.float32, jnp.bfloat16, jnp.int32
MIB = 1 << 20
LANES = 128
LARGE = 1 << 21
SHARE = 1.0
VMEM = pl.BlockSpec(memory_space=pltpu.VMEM)
SMEM = pl.BlockSpec(memory_space=pltpu.SMEM)
ANY = pl.BlockSpec(memory_space=pl.ANY)
NT = (((1,), (1,)), ((), ()))
TN = (((0,), (0,)), ((), ()))
PLANS = ((18, 16, 12), (20, 18, 12), (23, 21, 12))


def call(kernel, ins, specs, outs, out_specs, *, after=(), vmem=24, flops=0, nbytes=0, **kwargs):
    return pl.pallas_call(
        functools.partial(kernel, len(ins)),
        in_specs=specs + [ANY] * len(after),
        out_specs=out_specs,
        out_shape=outs,
        compiler_params=pltpu.CompilerParams(vmem_limit_bytes=vmem * MIB),
        cost_estimate=pl.CostEstimate(flops=int(SHARE * flops), bytes_accessed=int(SHARE * nbytes), transcendentals=0),
        **kwargs,
    )(*[placed(x) for x in ins], *after)


def placed(x):
    if x.dtype != BF16:
        return x
    return pltpu.with_memory_space_constraint(x, pltpu.HBM if x.size >= LARGE else pltpu.VMEM)


def shape(*dims, dtype=BF16):
    return jax.ShapeDtypeStruct(dims, dtype)


def kron_kernel(rank, ins, alloc_ref, kron_ref):
    tenants, skills = alloc_ref.shape
    depth = skills * rank
    at = lax.broadcasted_iota(I32, (skills, depth), 1)
    row = lax.broadcasted_iota(I32, (skills, depth), 0)
    inside = jnp.logical_and(at >= row * rank, at < (row + 1) * rank)
    repeat = jnp.where(inside, 1.0, 0.0).astype(BF16)
    spread = jnp.dot(alloc_ref[...].astype(BF16), repeat, preferred_element_type=F32)
    lane = lax.rem(lax.broadcasted_iota(I32, (rank, depth), 1), rank)
    diagonal = lane == lax.broadcasted_iota(I32, (rank, depth), 0)
    for t in range(tenants):
        kron_ref[t * rank : (t + 1) * rank, :] = jnp.where(diagonal, spread[t : t + 1, :], 0.0).astype(BF16)


def make_kron(alloc, rank):
    tenants, skills = alloc.shape
    return call(
        functools.partial(kron_kernel, rank), [alloc], [VMEM], shape(tenants * rank, skills * rank), VMEM, vmem=16
    )


def compose_kernel(slots, ins, *refs):
    kron_ref, library_ref = refs[:2] if not slots else refs[1:3]
    own_ref = refs[-2] if slots else refs[-1]
    tenants, rank, size = own_ref.shape
    made = jnp.dot(kron_ref[...], library_ref[...], preferred_element_type=F32).astype(BF16)
    own_ref[...] = made.reshape(tenants, rank, size)
    if slots:
        copy_slots(refs[0], own_ref, refs[-1], slots)


def copy_slots(tab_ref, own_ref, out_ref, slots):
    def one(slot, carry):
        out_ref[slot] = own_ref[tab_ref[0, slot]]
        return carry

    lax.fori_loop(0, slots, one, 0, unroll=2)


def compose(kron, library, rank, part, tile, slots=0, tab=None, after=()):
    rows, depth = kron.shape
    tenants = rows // rank
    start, size = part
    at = start // tile
    outs, out_specs = [shape(tenants, rank, size)], [pl.BlockSpec((tenants, rank, tile), lambda j: (0, 0, j))]
    if slots:
        outs.append(shape(slots, rank, size))
        out_specs.append(pl.BlockSpec((slots, rank, tile), lambda j: (0, 0, j)))
    made = call(
        functools.partial(compose_kernel, slots),
        ([tab] if slots else []) + [kron, library],
        ([SMEM] if slots else []) + [VMEM, pl.BlockSpec((depth, tile), lambda j: (0, at + j))],
        outs,
        out_specs,
        after=after,
        grid=(size // tile,),
        flops=2 * rows * depth * size,
        nbytes=2 * (depth + rows) * size,
    )
    return made if slots else made[0]


def tables_kernel(n, tenants, plans, ins, place_ref, *refs):
    arrays, tab_ref, plan_ref = refs[:-2], refs[-2], refs[-1]
    me = place_ref[0]
    blocks = arrays[0].shape[1]
    sub = lax.broadcasted_iota(I32, (tenants, tenants), 0)
    lane = lax.broadcasted_iota(I32, (tenants, tenants), 1)
    wide = lax.broadcasted_iota(I32, (tenants, LANES), 1)
    tenant = lax.broadcasted_iota(I32, (tenants, LANES), 0)
    one = lax.broadcasted_iota(I32, (tenants, blocks), 0)
    zs = [lax.rem(me - k + n, n) for k in range(n)]
    groups = len(arrays)
    present = [
        [
            jnp.max(jnp.where(one == arrays[g][k : k + 1, :], 1.0, 0.0), axis=1, keepdims=True)
            for k in range(n)
        ]
        for g in range(groups)
    ]

    def union(keep, group=0):
        total = jnp.zeros((tenants, 1), F32)
        for z, here in zip(zs, present[group]):
            total = jnp.maximum(total, here * jnp.where(keep(z), 1.0, 0.0))
        return total

    def positions(held):
        across = jnp.sum(jnp.where(sub == lane, held, 0.0), axis=0, keepdims=True)
        return jnp.sum(jnp.where(lane < sub, across, 0.0), axis=1, keepdims=True)

    def pack(held, value):
        slot = positions(held).astype(I32)
        chosen = jnp.logical_and(slot == wide, held > 0.5)
        return jnp.sum(jnp.where(chosen, value, 0.0), axis=0, keepdims=True)

    send_right, send_left = union(lambda z: z > me), union(lambda z: z < me)
    from_left, from_right = positions(union(lambda z: z >= me)), positions(union(lambda z: z <= me))
    number = tenant.astype(F32)
    right = pack(send_right, number), pack(send_right, from_left)
    left = pack(send_left, number), pack(send_left, from_right)
    own = jnp.concatenate([arrays[0][0:1, :], jnp.zeros((1, LANES - blocks), I32)], axis=1)
    mine = own == tenant

    def at(place, rows, otherwise):
        return jnp.where(me == place, rows, otherwise)

    none = jnp.zeros((1, LANES), F32)
    final_right = jnp.sum(jnp.where(mine, from_left, 0.0), axis=0, keepdims=True)
    final_left = jnp.sum(jnp.where(mine, from_right, 0.0), axis=0, keepdims=True)
    rows = []
    for part in (0, 1):
        for hop in range(n - 1):
            rows.append(at(hop, right[part], at(n - 1 - hop, left[part], none)))
    for hop in range(n - 1):
        rows.append(at(hop + 1, final_right, at(n - 2 - hop, final_left, none)))
    for row, value in enumerate(rows):
        tab_ref[row : row + 1, :] = value.astype(I32)
    tab_ref[len(rows) : len(rows) + 1, :] = own
    ends_here = jnp.logical_or(me == 0, me == n - 1)
    tab_ref[len(rows) + 1 : len(rows) + 2, :] = jnp.where(ends_here, jnp.ones_like(own), jnp.zeros_like(own))

    held = jnp.zeros((tenants, LANES), F32)
    hop_of = lax.broadcasted_iota(I32, (1, LANES), 1)
    limits = [jnp.full((1, LANES), float(tenants), F32) for _ in plans]
    column = 0
    for group in range(groups):
        for hop in range(n - 1):
            for keep in (lambda z: z > hop, lambda z: z < n - 1 - hop):
                held = jnp.where(wide == column, union(keep, group), held)
                limits = [jnp.where(hop_of == column, float(p[hop]), l) for p, l in zip(plans, limits)]
                column += 1
    counts = jnp.sum(held, axis=0, keepdims=True)
    plan = jnp.int32(0)
    for limit in limits[:-1]:
        plan = plan + jnp.where(jnp.max(counts - limit) > 0.5, 1, 0)
    plan_ref[0] = plan


def make_tables(n, tenants, plans, place, arrays):
    rows = -(-(3 * (n - 1) + 2) // 8) * 8
    return call(
        functools.partial(tables_kernel, n, tenants, plans),
        [place, *arrays],
        [SMEM] + [VMEM] * len(arrays),
        [shape(rows, LANES, dtype=I32), shape(1, dtype=I32)],
        [VMEM, SMEM],
    )


def step_kernel(n, jobs, passed, ins, *refs):
    tab_ref = refs[0]
    ins -= 1
    given, outs = list(refs[1 : 1 + ins]), refs[1 + ins + passed : 1 + ins + passed + len(jobs)]
    for (hop, slots, by_tenant), out_ref in zip(jobs, outs):
        own_ref = given.pop(0)
        in_ref = given.pop(0) if hop else None

        def one(slot, carry, hop=hop, by_tenant=by_tenant, own_ref=own_ref, in_ref=in_ref, out_ref=out_ref):
            tenant = tab_ref[hop, slot]
            block = own_ref[tenant]
            if hop:
                index = tenant if by_tenant else tab_ref[n - 1 + hop, slot]
                block = (block.astype(F32) + in_ref[index].astype(F32)).astype(BF16)
            out_ref[slot] = block
            return carry

        lax.fori_loop(0, slots, one, 0, unroll=4)


def step(n, tab, jobs, after=(), through=()):
    ins, shapes, plan = [], [], []
    for hop, slots, own, arrived, by_tenant in jobs:
        plan.append((hop, slots, by_tenant))
        ins += [own, arrived] if hop else [own]
        shapes.append(jax.ShapeDtypeStruct((slots,) + own.shape[1:], BF16))
    return call(
        functools.partial(step_kernel, n, plan, len(after) + len(through)),
        [tab, *ins],
        [SMEM] + [VMEM] * len(ins),
        shapes + [shape(*x.shape) for x in through],
        [VMEM] * len(shapes) + [ANY] * len(through),
        after=list(after) + list(through),
        input_output_aliases={1 + len(ins) + len(after) + i: len(shapes) + i for i in range(len(through))},
        nbytes=sum(2 * 3 * x.size for x in shapes),
    )


def factor_of(n, b, by_tenant, tab_ref, own_ref, arrived):
    tenant = tab_ref[3 * (n - 1), b]
    factor = own_ref[tenant].astype(F32)
    outer = tab_ref[3 * (n - 1) + 1, 0] > 0
    for hop in range(n - 1):
        index = tenant if by_tenant and hop == 0 else tab_ref[2 * (n - 1) + hop, b]
        came = arrived[hop][index].astype(F32)
        used = jnp.where(outer, 1, 0) if hop == n - 2 else jnp.where(outer, 0, 1)
        factor = jnp.where(used > 0, factor + came, factor)
    return factor.astype(BF16)


def project_kernel(n, first, out, ins, tab_ref, tokens_ref, own_ref, *refs):
    arrived = refs[: n - 1]
    total_ref = None if first else refs[ins - 4]
    outs = refs[-2:] if out else refs[-1:]
    size = tokens_ref.shape[1]

    def one(b, carry):
        factor = factor_of(n, b, False, tab_ref, own_ref, arrived)
        at = pl.ds(pl.multiple_of(b * LANES, LANES), LANES)
        part = lax.dot_general(factor, tokens_ref[at, :], NT, preferred_element_type=F32)
        if not first:
            part = total_ref[:, at] + part
        outs[0][:, at] = part.astype(outs[0].dtype)
        if out:
            outs[1][b] = factor_of(n, b, True, tab_ref, refs[n - 1], refs[n : 2 * n - 1])
        return carry

    lax.fori_loop(0, tokens_ref.shape[0] // LANES, one, 0, unroll=4)


def project(n, tab, tokens, own, part, arrived, total, last, up=None, after=()):
    tenants, rank, size = own.shape
    rows = tokens.shape[0]
    at = part[0] // size
    outs = [shape(rank, rows, dtype=BF16 if last else F32)]
    ins = [tab, tokens, own, *arrived]
    if up:
        outs.append(shape(rows // LANES, rank, up[0].shape[2]))
        ins += [up[0], *up[1]]
    if total is not None:
        ins.append(total)
    return call(
        functools.partial(project_kernel, n, total is None, up is not None),
        ins,
        [SMEM, pl.BlockSpec((rows, size), lambda j: (0, at))] + [VMEM] * (len(ins) - 2),
        outs,
        [VMEM] * len(outs),
        after=after,
        grid=(1,),
        flops=2 * rows * size * rank,
        nbytes=2 * size * (rows + 2 * tenants * rank),
    )


def base_kernel(order_ref, tokens_ref, weight_ref, *refs):
    refs[-1][0] = jnp.dot(tokens_ref[...], weight_ref[...], preferred_element_type=F32).astype(BF16)


def base_product(order, tokens, weight, out, after):
    rows, width = tokens.shape
    flops, nbytes = 4 * rows * width * out, 2 * (rows * (width + 2 * out) + 2 * width * out)
    return pl.pallas_call(
        base_kernel,
        grid_spec=pltpu.PrefetchScalarGridSpec(
            num_scalar_prefetch=1,
            grid=(2, 2),
            in_specs=[
                pl.BlockSpec((rows // 2, width), lambda q, m, order: ((q + m) % 2, 0)),
                pl.BlockSpec((width, out), lambda q, m, order: (0, order[q])),
            ]
            + [ANY] * len(after),
            out_specs=pl.BlockSpec((1, rows // 2, out), lambda q, m, order: (q, (q + m) % 2, 0)),
        ),
        out_shape=shape(2, rows, out),
        compiler_params=pltpu.CompilerParams(vmem_limit_bytes=24 * MIB),
        cost_estimate=pl.CostEstimate(flops=int(SHARE * flops), bytes_accessed=int(SHARE * nbytes), transcendentals=0),
    )(order, placed(tokens), placed(weight), *after)


def gather_kernel(ins, a_ref, b_ref, c_ref, out_ref):
    out_ref[...] = (a_ref[0].astype(F32) + b_ref[0].astype(F32) + c_ref[...].astype(F32)).astype(out_ref.dtype)


def gather_base(keep, from_core, across):
    rows, width = across.shape
    half = pl.BlockSpec((1, rows, width), lambda j: (1, 0, 0))
    whole = pl.BlockSpec((rows, width), lambda j: (0, 0))
    return call(
        gather_kernel,
        [keep, from_core, across],
        [half, half, whole],
        shape(rows, width),
        whole,
        nbytes=8 * rows * width,
        grid=(1,),
    )


def finish_kernel(per, ins, len_ref, up_ref, *refs):
    lows, base_ref, out_ref = refs[:4], refs[4], refs[5]
    width = out_ref.shape[1]
    for j in range(per):
        b = pl.program_id(0) * per + j
        at = slice(j * LANES, (j + 1) * LANES)
        low = lows[0][:, at].astype(F32)
        for other in lows[1:]:
            low = low + other[:, at].astype(F32)
        high = low.astype(BF16)
        rest = (low - high.astype(F32)).astype(BF16)
        total = lax.dot_general(high, up_ref[b], TN, preferred_element_type=F32)
        total = total + lax.dot_general(rest, up_ref[b], TN, preferred_element_type=F32)
        total = total + base_ref[at, :].astype(F32)
        live = lax.broadcasted_iota(I32, (LANES, width), 0) < len_ref[b]
        out_ref[at, :] = jnp.where(live, total, 0.0).astype(out_ref.dtype)


def finish(lens, up, lows, base, per):
    rank, rows = lows[0].shape
    width = base.shape[1]
    blocks = rows // LANES
    whole = pl.BlockSpec((per * LANES, width), lambda j: (j, 0))
    return call(
        functools.partial(finish_kernel, per),
        [lens, up, *lows, base],
        [SMEM, VMEM] + [pl.BlockSpec((rank, per * LANES), lambda j: (0, j))] * 4 + [whole],
        shape(rows, width),
        whole,
        grid=(blocks // per,),
        flops=4 * rows * rank * width,
        nbytes=8 * rows * width,
    )


def swap(x, axis):
    return lax.ppermute(x, axis, [(0, 1), (1, 0)])


def ends(x):
    return lax.ppermute(x, "skill", [(0, 1), (1, 0), (2, 3), (3, 2)])


def middle(x):
    pairs = [(2 + c, 4 + c) for c in (0, 1)] + [(0, 1), (6, 7)]
    return lax.ppermute(x, ("skill", "tensor"), pairs + [(b, a) for a, b in pairs])


def line_body(tokens, base_weight, skill_down, skill_up, alloc, block_tenant, block_len):
    n = 4
    rows, width = tokens.shape
    tenants, local_skills = alloc.shape
    rank = skill_down.shape[2]
    out = skill_up.shape[2]
    blocks = block_len.shape[0]
    me = lax.axis_index("skill")
    tensor, dp = lax.axis_index("tensor"), lax.axis_index("dp")
    hops = [ends, middle, ends]
    full = [min(tenants, blocks * (n - 1 - h)) for h in range(n - 1)]
    plans = [[min(f, p) for f, p in zip(full, plan)] for plan in PLANS] + [full]
    tile = width // 8
    parts = [(0, 3 * tile), (3 * tile, 3 * tile), (6 * tile, 2 * tile)]

    own_t = block_tenant.reshape(1, blocks)
    seen = jnp.concatenate(
        [own_t]
        + [lax.ppermute(own_t, "skill", [(j, (j + k) % n) for j in range(n)]) for k in range(1, n)],
        axis=0,
    )
    seen = [seen, swap(seen, "group")]
    kron = make_kron(alloc, rank)
    library = jnp.transpose(skill_down, (0, 2, 1)).reshape(local_skills * rank, width)
    own_up = compose(kron, skill_up.reshape(local_skills * rank, out), rank, (0, out), out, after=[seen[0]])
    up_0 = ends(own_up)
    own_0 = compose(kron, library, rank, parts[0], tile, after=[own_up])
    tab, plan = make_tables(n, tenants, plans, me.reshape(1).astype(I32), seen)
    other, mine = (1 - tensor) * 2, tensor * 2
    order_away = jnp.stack([other + 1 - dp, other + dp]).astype(I32)
    order_keep = jnp.stack([mine + 1 - dp, mine + dp]).astype(I32)

    def planned(sizes):
        owns, arrived, up_came = [own_0], [[], [], []], [up_0]

        def job(h, k):
            return h, sizes[h], owns[k], arrived[k][h - 1] if h else None, False

        def up_job(h):
            return h, sizes[h], own_up, up_came[h - 1], h == 1

        first, up_1 = step(n, tab, [job(0, 0), up_job(1)])
        arrived[0].append(ends(first))
        up_came.append(middle(up_1))
        sent = []
        for k in (1, 2):
            own, message = compose(kron, library, rank, parts[k], tile, sizes[0], tab)
            owns.append(own)
            sent.append(message)
            arrived[k].append(ends(message))

        to_1, up_2 = step(n, tab, [job(1, 0), up_job(2)], sent)
        arrived[0].append(middle(to_1))
        up_came.append(ends(up_2))
        away = base_product(order_away, tokens, base_weight, out, [to_1])

        to_1, to_2, away = step(n, tab, [job(1, 1), job(2, 0)], [], [away])
        arrived[1].append(middle(to_1))
        arrived[0].append(ends(to_2))
        from_core = swap(away, "tensor")
        keep = base_product(order_keep, tokens, base_weight, out, [to_1])

        to_1, to_2, keep = step(n, tab, [job(1, 2), job(2, 1)], [from_core, up_came[2]], [keep])
        arrived[2].append(middle(to_1))
        arrived[1].append(ends(to_2))
        near = (keep[0].astype(F32) + from_core[0].astype(F32)).astype(BF16)
        across = swap(near, "dp")
        low, up = project(n, tab, tokens, owns[0], parts[0], arrived[0], None, False, (own_up, up_came), [to_1])

        (to_2,) = step(n, tab, [job(2, 2)], [low])
        arrived[2].append(ends(to_2))
        (low,) = project(n, tab, tokens, owns[1], parts[1], arrived[1], low, False)
        base = gather_base(keep, from_core, across)
        (low,) = project(n, tab, tokens, owns[2], parts[2], arrived[2], low, True, None, [base])
        return low, up, base

    low, up, base = lax.switch(plan[0], [functools.partial(planned, sizes) for sizes in plans])
    lows = [low, swap(low, "tensor"), swap(low, "dp")]
    lows.append(lax.ppermute(low, ("tensor", "dp"), [(0, 3), (1, 2), (2, 1), (3, 0)]))
    return finish(block_len, up, lows, base, 6)


def plain_body(tokens, base_weight, skill_down, skill_up, alloc, block_tenant, block_len):
    rows, width = tokens.shape
    blocks = block_len.shape[0]
    block_rows = rows // blocks
    local_skills, slice_width, rank = skill_down.shape
    slice_out = skill_up.shape[2]
    down_size = slice_width * rank
    stacked = jnp.concatenate(
        [
            skill_down.reshape(local_skills, down_size),
            skill_up.reshape(local_skills, rank * slice_out),
        ],
        1,
    ).astype(F32)
    partial_sum = jnp.dot(alloc, stacked, precision=lax.Precision.HIGHEST)
    composed = lax.psum(partial_sum.astype(BF16), "skill")
    factors = jnp.take(composed, block_tenant, axis=0)
    down_part = factors[:, :down_size].reshape(blocks, slice_width, rank)
    up_part = factors[:, down_size:].reshape(blocks, rank, slice_out).astype(F32)
    grouped = tokens.reshape(blocks, block_rows, width)
    projected = jnp.einsum("bnd,bdr->bnr", grouped, down_part, preferred_element_type=F32)
    base_term = jnp.dot(tokens, base_weight, preferred_element_type=F32)
    lowrank = lax.psum(projected.astype(BF16), ("tensor", "dp")).astype(F32)
    base = lax.psum_scatter(
        base_term.astype(BF16), ("tensor", "dp"), scatter_dimension=1, tiled=True
    ).astype(F32)
    adapter = jnp.einsum("bnr,bro->bno", lowrank, up_part, precision=lax.Precision.HIGHEST)
    total = base.reshape(blocks, block_rows, slice_out) + adapter
    live = (jnp.arange(block_rows, dtype=I32)[None, :] < block_len[:, None])[:, :, None]
    return jnp.where(live, total, 0.0).astype(BF16).reshape(rows, slice_out)


def solution(mesh):
    placed = (
        P(("group", "skill"), ("tensor", "dp")),
        P(("tensor", "dp"), None),
        P("skill", ("tensor", "dp"), None),
        P("skill", None, ("tensor", "dp")),
        P("group", "skill"),
        P(("group", "skill")),
        P(("group", "skill")),
    )
    fits = (mesh.shape["skill"], mesh.shape["tensor"], mesh.shape["dp"]) == (4, 2, 2)
    body = line_body if fits else plain_body
    return jax.shard_map(
        body,
        mesh=mesh,
        in_specs=placed,
        out_specs=P(("group", "skill"), ("tensor", "dp")),
        check_vma=False,
    )
```

time: 187 us -> 89.8 us (0.48)
  waiting for transfers between devices: 86.9 us -> 19.7 us
  matrix products: 46.5 us -> 0 us
  Pallas kernels: 0 us -> 43.9 us
  starting transfers between devices: 0.05 us -> 24.1 us
  local copies, waits for them, and re-layouts: 24.6 us -> 1.38 us
  between operations: 15 us -> 0.73 us
  blocking collectives: 13.2 us -> 0 us
    psum x1 -> x0, waiting for transfers between devices: 86.9 us -> none  [body(): composed = lax.psum(partial_sum.astype(jnp.bfloat16), 'skill')]
    dot_general x4 -> x0, matrix products: 46.5 us -> none  [the longest x1 26.1 us: body(): partial_sum = jnp.dot(alloc, stacked, precision=lax.Precision.HIGHEST)]
    pallas_call x0 -> x18, Pallas kernels: none -> 43.9 us  [the longest x16 28.5 us: call(): pl.pallas_call(functools.partial(kernel, len(ins)), in_specs=specs + [ANY...]
    ppermute x0 -> x21, starting transfers between devices: none -> 24.1 us  [the longest x8 12.3 us: ends(): return lax.ppermute(x, 'skill', [(0, 1), (1, 0), (2, 3), (3, 2)])]
    ppermute x0 -> x21, waiting for transfers between devices: none -> 19.7 us  [the longest x8 13.8 us: ends(): return lax.ppermute(x, 'skill', [(0, 1), (1, 0), (2, 3), (3, 2)])]
    psum x1 -> x0, blocking collectives: 13.2 us -> none  [body(): lax.psum(projected.astype(jnp.bfloat16), ('tensor', 'dp'))]
    unnamed x11 -> x8, local copies, waits for them, and re-layouts: 14.5 us -> 1.38 us
    reshape x1 -> x0, local copies, waits for them, and re-layouts: 6.16 us -> none  [body(): down_part = factors[:, :down_size].reshape(blocks, slice_width, rank)]
  transfers between devices with their start and end apart: 2 -> 21, of which waited for: 1 -> 9; matrix products, arithmetic and copies ran while one was open for 15% -> 0% of each run, Pallas kernels for 0% -> 39%
where the time goes in v2:
time: 89.8 us; the launch traced here: 90.6 us
  Pallas kernels  43.9 us (49%)
  starting transfers between devices  24.1 us (27%)
  waiting for transfers between devices  19.7 us (22%)
  local copies, waits for them, and re-layouts  1.38 us (2%)
    pallas_call x16, Pallas kernels, call(): pl.pallas_call(functools.partial(kernel, len(ins)), in_specs=specs + [ANY...  28.5 us
    pallas_call x2, Pallas kernels, base_product(): pl.pallas_call(base_kernel, grid_spec=pltpu.PrefetchScalarGridSpec(num_sc...  15.4 us
    ppermute x8, waiting for transfers between devices, ends(): return lax.ppermute(x, 'skill', [(0, 1), (1, 0), (2, 3), (3, 2)])  13.8 us
    ppermute x8, starting transfers between devices, ends(): return lax.ppermute(x, 'skill', [(0, 1), (1, 0), (2, 3), (3, 2)])  12.3 us
    ppermute x3, starting transfers between devices, line_body(): lax.ppermute(own_t, 'skill', [(j, (j + k) % n) for j in range(n)])  6.06 us
    ppermute x5, starting transfers between devices, swap(): return lax.ppermute(x, axis, [(0, 1), (1, 0)])  5.49 us
    ppermute x3, waiting for transfers between devices, line_body(): lax.ppermute(own_t, 'skill', [(j, (j + k) % n) for j in range(n)])  3.17 us
  transfers between devices with their start and end apart: 21, of which 9 were waited for; matrix products, arithmetic and copies ran while one was open for 0% of the time, Pallas kernels for 39%

profile of v2, /device:TPU:0, one launch (start us, length us, event | category | flops | bytes accessed | tf_op | source)
XLA Modules:
  0.0 90.6 jit_solution(7199293304512679424)
XLA Ops:
  0.0 5.0 %collective-permute-start.54 = (s32[1,12]{1,0:T(1,128)}, s32[1,12]{1,0:T(1,128)S(1)}, u32[]{:S(2)}, u32[]{:S(2)}) collective-permute-start(s32[1,12]{1,0:T(1,128)} %bitcast.25), channel_id=1, source_target_pairs={{0,12},{4,0},{8,4},{12,8},{1,13},{5,1},{9,5},{13,9},{2,14},{6,2},{... | collective-permute-start | bytes 152 | tf_op jit(solution)/shard_map/ppermute | solution.py:399
  5.1 0.0 collective-permute-start.53
  5.1 1.0 %collective-permute-start.52 = (s32[1,12]{1,0:T(1,128)}, s32[1,12]{1,0:T(1,128)S(1)}, u32[]{:S(2)}, u32[]{:S(2)}) collective-permute-start(s32[1,12]{1,0:T(1,128)} %bitcast.27), channel_id=1, source_target_pairs={{0,4},{4,8},{8,12},{12,0},{1,5},{5,9},{9,13},{13,1},{2,6},{6,10},{... | collective-permute-start | bytes 152 | tf_op jit(solution)/shard_map/ppermute | solution.py:399
  6.1 0.7 copy-done.1
  6.8 0.6 shard_map.74.refs_0_
  7.3 0.0 collective-permute-done.54
  7.4 2.3 %collective-permute-done.53 = s32[1,12]{1,0:T(1,128)S(1)} collective-permute-done((s32[1,12]{1,0:T(1,128)}, s32[1,12]{1,0:T(1,128)S(1)}, u32[]{:S(2)}, u32[]{:S(2)}) %collective-permute-start.53) | collective-permute-done | bytes 80 | tf_op jit(solution)/shard_map/ppermute | solution.py:399
  9.6 0.9 collective-permute-done.52
  10.6 0.7 shard_map.75.refs_2_
  11.3 0.1 collective-permute-start.56
  11.3 0.1 pad_add_fusion.1
  11.4 1.5 %collective-permute-start.55 = (s32[4,12]{1,0:T(4,128)S(1)}, s32[4,12]{1,0:T(4,128)S(1)}, u32[]{:S(2)}, u32[]{:S(2)}) collective-permute-start(s32[4,12]{1,0:T(4,128)S(1)} %pad_add_fusion.refs_0_.refs_2_), channel_id=1, source_target_pairs={{0,16},{16,0},{1,17},{17,1},{2,18},{18,2},{3,19},{19,3},{4,20},{20... | collective-permute-start | bytes 584 | tf_op jit(solution)/shard_map/ppermute | solution.py:369
  13.0 3.9 %shard_map.76 = bf16[32,16,768]{2,1,0:T(8,128)(2,1)S(1)} custom-call(bf16[512,2048]{1,0:T(8,128)(2,1)S(1)} %shard_map.74.refs_0_, bf16[2048,2048]{1,0:T(8,128)(2,1)} %bitcast.20, bf16[32,16,256]{2,1,0:T(8,128)(2,1)S(1)} %shard_map.75.refs_2_), custom_call_target="tpu_custom_call" | custom-call | flops 1610612736 | bytes 3932160 | tf_op jit(solution)/shard_map/pallas_call | solution.py:24
  16.9 0.0 collective-permute-done.55.refs_1_
  16.9 0.8 shard_map.73
  18.3 0.0 collective-permute-done.56
  18.3 64.3 %conditional.1 = (bf16[16,1536]{1,0:T(8,128)(2,1)S(1)}, bf16[12,16,256]{2,1,0:T(8,128)(2,1)S(1)}, bf16[1536,256]{1,0:T(8,128)(2,1)}) conditional(s32[]{:T(128)} %bitcast.6, (s32[16,128]{1,0:T(8,128)S(1)}, bf16[512,2048]{1,0:T(8,128)(2,1)S(1)}, bf16[2048,2048]{1,0:T(8,128)(2,1)}, bf16[32,16,768]{2,1,0:T(8,128)(2,1)S(1)}, ...), branch_computations={%region_0.0_spmd, %region_1.0_spmd, %region_2.0_spmd, %region_3.0_... | conditional | flops 9229041664 | bytes 81232416 | solution.py:457
  18.5 0.8 branch_1_fun.15
  19.4 2.1 %collective-permute-start.15 = (bf16[20,16,768]{2,1,0:T(8,128)(2,1)S(1)}, bf16[20,16,768]{2,1,0:T(8,128)(2,1)S(1)}, u32[]{:S(2)}, u32[]{:S(2)}) collective-permute-start(bf16[20,16,768]{2,1,0:T(8,128)(2,1)S(1)} %get-tuple-element.122), channel_id=1, source_target_pairs={{0,4},{4,0},{8,12},{12,8},{1,5},{5,1},{9,13},{13,9},{2,6},{6,2},{1... | collective-permute-start | bytes 1474568 | tf_op jit(solution)/shard_map/cond/branch_1_fun/ppermute | solution.py:373
  21.4 0.0 collective-permute-start.16
  21.4 4.1 %branch_1_fun.14 = (bf16[32,16,768]{2,1,0:T(8,128)(2,1)S(1)}, bf16[20,16,768]{2,1,0:T(8,128)(2,1)S(1)}) custom-call(s32[16,128]{1,0:T(8,128)S(1)} %get-tuple-element.111.refs_0_.tab_ref, bf16[512,2048]{1,0:T(8,128)(2,1)S(1)} %get-tuple-element.113.refs_1_, bf16[2048,2048]{1,0:T(8,128)(2,1)} %get-tuple-element.114.refs_2_), custom_call_target="tpu_custom_call" | custom-call | flops 1610612736 | bytes 3932160 | tf_op jit(solution)/shard_map/cond/branch_1_fun/pallas_call | solution.py:24
  25.6 1.7 %collective-permute-start.14 = (bf16[20,16,768]{2,1,0:T(8,128)(2,1)S(1)}, bf16[20,16,768]{2,1,0:T(8,128)(2,1)S(1)}, u32[]{:S(2)}, u32[]{:S(2)}) collective-permute-start(bf16[20,16,768]{2,1,0:T(8,128)(2,1)S(1)} %get-tuple-element.118.refs_5_), channel_id=1, source_target_pairs={{0,4},{4,0},{8,12},{12,8},{1,5},{5,1},{9,13},{13,9},{2,6},{6,2},{1... | collective-permute-start | bytes 1474568 | tf_op jit(solution)/shard_map/cond/branch_1_fun/ppermute | solution.py:373
  27.3 2.9 %branch_1_fun.13 = (bf16[32,16,512]{2,1,0:T(8,128)(2,1)S(1)}, bf16[20,16,512]{2,1,0:T(8,128)(2,1)S(1)}) custom-call(s32[16,128]{1,0:T(8,128)S(1)} %get-tuple-element.111.refs_0_.tab_ref, bf16[512,2048]{1,0:T(8,128)(2,1)S(1)} %get-tuple-element.113.refs_1_, bf16[2048,2048]{1,0:T(8,128)(2,1)} %get-tuple-element.114.refs_2_), custom_call_target="tpu_custom_call" | custom-call | flops 1073741824 | bytes 2621440 | tf_op jit(solution)/shard_map/cond/branch_1_fun/pallas_call | solution.py:24
  30.2 0.0 collective-permute-done.16.refs_4_.refs_5_
  30.2 2.9 %collective-permute-done.15.refs_2_.refs_0_ = bf16[20,16,768]{2,1,0:T(8,128)(2,1)S(1)} collective-permute-done((bf16[20,16,768]{2,1,0:T(8,128)(2,1)S(1)}, bf16[20,16,768]{2,1,0:T(8,128)(2,1)S(1)}, u32[]{:S(2)}, u32[]{:S(2)}) %collective-permute-start.15) | collective-permute-done | bytes 491552 | tf_op jit(solution)/shard_map/cond/branch_1_fun/ppermute | solution.py:373
  33.1 0.9 branch_1_fun.16
  34.0 0.1 collective-permute-start.17
  34.1 7.7 %branch_1_fun.17.refs_5_ = bf16[2,1536,256]{2,1,0:T(8,128)(2,1)S(1)} custom-call(s32[2]{0:T(128)S(1)} %get-tuple-element.125.order_ref, bf16[1536,2048]{1,0:T(8,128)(2,1)} %get-tuple-element.112.tokens_ref, bf16[2048,1024]{1,0:T(8,128)(2,1)} %get-tuple-element.126.weight_ref, bf16[18,16,768]{2,1,0:T(8,128)(2,1)S(1)} %get-tuple-element.124.refs_0_), custom_call_target="tpu_custom_call" | custom-call | flops 3221225472 | bytes 9961472 | tf_op jit(solution)/shard_map/cond/branch_1_fun/pallas_call | solution.py:296
  41.8 0.0 collective-permute-done.14.refs_2_.refs_0_
  41.8 0.0 collective-permute-done.17.refs_4_.refs_1_
  41.8 0.9 %branch_1_fun.18 = (bf16[18,16,768]{2,1,0:T(8,128)(2,1)S(1)}, bf16[12,16,768]{2,1,0:T(8,128)(2,1)S(1)}, bf16[2,1536,256]{2,1,0:T(8,128)(2,1)S(1)}) custom-call(s32[16,128]{1,0:T(8,128)S(1)} %get-tuple-element.111.refs_0_.tab_ref, bf16[32,16,768]{2,1,0:T(8,128)(2,1)S(1)} %get-tuple-element.117.refs_1_.refs_3_.own_ref, ...), custom_call_target="tpu_custom_call", output_to_operand_aliasing={{2}: (5, {})} | custom-call | bytes 2211840 | tf_op jit(solution)/shard_map/cond/branch_1_fun/pallas_call | solution.py:24
  42.8 0.6 collective-permute-start.19
  43.3 0.1 collective-permute-start.18
  43.4 4.0 %collective-permute-start.13 = (bf16[20,16,512]{2,1,0:T(8,128)(2,1)S(1)}, bf16[20,16,512]{2,1,0:T(8,128)(2,1)S(1)}, u32[]{:S(2)}, u32[]{:S(2)}) collective-permute-start(bf16[20,16,512]{2,1,0:T(8,128)(2,1)S(1)} %get-tuple-element.116.refs_6_), channel_id=1, source_target_pairs={{0,4},{4,0},{8,12},{12,8},{1,5},{5,1},{9,13},{13,9},{2,6},{6,2},{1... | collective-permute-start | bytes 983048 | tf_op jit(solution)/shard_map/cond/branch_1_fun/ppermute | solution.py:373
  47.4 0.0 collective-permute-start.20
  47.4 7.7 %branch_1_fun.19.refs_7_ = bf16[2,1536,256]{2,1,0:T(8,128)(2,1)S(1)} custom-call(s32[2]{0:T(128)S(1)} %get-tuple-element.130.order_ref, bf16[1536,2048]{1,0:T(8,128)(2,1)} %get-tuple-element.112.tokens_ref, bf16[2048,1024]{1,0:T(8,128)(2,1)} %get-tuple-element.126.weight_ref, bf16[18,16,768]{2,1,0:T(8,128)(2,1)S(1)} %get-tuple-element.127.refs_0_), custom_call_target="tpu_custom_call" | custom-call | flops 3221225472 | bytes 9961472 | tf_op jit(solution)/shard_map/cond/branch_1_fun/pallas_call | solution.py:296
  55.1 0.7 collective-permute-done.13.refs_2_.refs_0_
  55.9 1.7 %collective-permute-done.20.refs_6_ = bf16[12,16,256]{2,1,0:T(8,128)(2,1)S(1)} collective-permute-done((bf16[12,16,256]{2,1,0:T(8,128)(2,1)S(1)}, bf16[12,16,256]{2,1,0:T(8,128)(2,1)S(1)}, u32[]{:S(2)}, u32[]{:S(2)}) %collective-permute-start.20) | collective-permute-done | bytes 98336 | tf_op jit(solution)/shard_map/cond/branch_1_fun/ppermute | solution.py:373
  57.5 0.0 collective-permute-done.18.refs_4_.refs_1_
  57.5 0.0 collective-permute-done.19.refs_5_.b_ref
  57.5 0.9 branch_1_fun.20
  58.5 0.2 fusion.1
  58.7 1.6 %collective-permute-start.25 = (bf16[1536,256]{1,0:T(8,128)(2,1)S(1)}, bf16[1536,256]{1,0:T(8,128)(2,1)S(1)}, u32[]{:S(2)}, u32[]{:S(2)}) collective-permute-start(bf16[1536,256]{1,0:T(8,128)(2,1)S(1)} %fusion.1), channel_id=1, source_target_pairs={{0,1},{1,0},{2,3},{3,2},{4,5},{5,4},{6,7},{7,6},{8,9},{9,8},{10,11... | collective-permute-start | bytes 2359304 | tf_op jit(solution)/shard_map/cond/branch_1_fun/ppermute | solution.py:369
  60.2 1.7 %collective-permute-start.22 = (bf16[12,16,768]{2,1,0:T(8,128)(2,1)S(1)}, bf16[12,16,768]{2,1,0:T(8,128)(2,1)S(1)}, u32[]{:S(2)}, u32[]{:S(2)}) collective-permute-start(bf16[12,16,768]{2,1,0:T(8,128)(2,1)S(1)} %get-tuple-element.132), channel_id=1, source_target_pairs={{0,4},{4,0},{8,12},{12,8},{1,5},{5,1},{9,13},{13,9},{2,6},{6,2},{1... | collective-permute-start | bytes 884744 | tf_op jit(solution)/shard_map/cond/branch_1_fun/ppermute | solution.py:373
  62.0 0.0 collective-permute-start.21
  62.0 0.9 collective-permute-start.24
  62.8 7.3 %collective-permute-done.22.refs_2_ = bf16[12,16,768]{2,1,0:T(8,128)(2,1)S(1)} collective-permute-done((bf16[12,16,768]{2,1,0:T(8,128)(2,1)S(1)}, bf16[12,16,768]{2,1,0:T(8,128)(2,1)S(1)}, u32[]{:S(2)}, u32[]{:S(2)}) %collective-permute-start.22) | collective-permute-done | bytes 294944 | tf_op jit(solution)/shard_map/cond/branch_1_fun/ppermute | solution.py:373
  70.2 2.6 %branch_1_fun.21 = (f32[16,1536]{1,0:T(8,128)S(1)}, bf16[12,16,256]{2,1,0:T(8,128)(2,1)S(1)}) custom-call(s32[16,128]{1,0:T(8,128)S(1)} %get-tuple-element.111.refs_0_.tab_ref, bf16[1536,2048]{1,0:T(8,128)(2,1)} %get-tuple-element.112.tokens_ref, bf16[32,16,768]{2,1,0:T(8,128)(2,1)S(1)} %get-tuple-element.119.refs_1_.refs_3_.own_ref, ...), custom_call_target="tpu_custom_call" | custom-call | flops 37748736 | bytes 3932160 | tf_op jit(solution)/shard_map/cond/branch_1_fun/pallas_call | solution.py:24
  72.8 0.0 collective-permute-done.21.refs_2_.refs_1_
  72.8 0.8 branch_1_fun.22
  73.6 1.8 %collective-permute-start.23 = (bf16[12,16,512]{2,1,0:T(8,128)(2,1)S(1)}, bf16[12,16,512]{2,1,0:T(8,128)(2,1)S(1)}, u32[]{:S(2)}, u32[]{:S(2)}) collective-permute-start(bf16[12,16,512]{2,1,0:T(8,128)(2,1)S(1)} %branch_1_fun.22), channel_id=1, source_target_pairs={{0,4},{4,0},{8,12},{12,8},{1,5},{5,1},{9,13},{13,9},{2,6},{6,2},{1... | collective-permute-start | bytes 589832 | tf_op jit(solution)/shard_map/cond/branch_1_fun/ppermute | solution.py:373
  75.4 1.1 %collective-permute-done.24.refs_2_ = bf16[12,16,768]{2,1,0:T(8,128)(2,1)S(1)} collective-permute-done((bf16[12,16,768]{2,1,0:T(8,128)(2,1)S(1)}, bf16[12,16,768]{2,1,0:T(8,128)(2,1)S(1)}, u32[]{:S(2)}, u32[]{:S(2)}) %collective-permute-start.24) | collective-permute-done | bytes 294944 | tf_op jit(solution)/shard_map/cond/branch_1_fun/ppermute | solution.py:373
  76.5 2.6 %branch_1_fun.23.refs_3_ = f32[16,1536]{1,0:T(8,128)S(1)} custom-call(s32[16,128]{1,0:T(8,128)S(1)} %get-tuple-element.111.refs_0_.tab_ref, bf16[1536,2048]{1,0:T(8,128)(2,1)} %get-tuple-element.112.tokens_ref, bf16[32,16,768]{2,1,0:T(8,128)(2,1)S(1)} %get-tuple-element.117.refs_1_.refs_3_.own_ref, ...), custom_call_target="tpu_custom_call" | custom-call | flops 37748736 | bytes 3932160 | tf_op jit(solution)/shard_map/cond/branch_1_fun/pallas_call | solution.py:24
  79.1 0.0 collective-permute-done.25.c_ref
  79.1 1.2 %branch_1_fun.24.refs_4_ = bf16[1536,256]{1,0:T(8,128)(2,1)} custom-call(bf16[2,1536,256]{2,1,0:T(8,128)(2,1)S(1)} %get-tuple-element.135.a_ref, bf16[2,1536,256]{2,1,0:T(8,128)(2,1)S(1)} %collective-permute-done.19.refs_5_.b_ref, bf16[1536,256]{1,0:T(8,128)(2,1)S(1)} %collective-permute-done.25.c_ref), custom_call_target="tpu_custom_call" | custom-call | bytes 3145728 | tf_op jit(solution)/shard_map/cond/branch_1_fun/pallas_call | solution.py:24
  80.3 2.1 %branch_1_fun.25 = bf16[16,1536]{1,0:T(8,128)(2,1)S(1)} custom-call(s32[16,128]{1,0:T(8,128)S(1)} %get-tuple-element.111.refs_0_.tab_ref, bf16[1536,2048]{1,0:T(8,128)(2,1)} %get-tuple-element.112.tokens_ref, bf16[32,16,512]{2,1,0:T(8,128)(2,1)S(1)} %get-tuple-element.115.refs_1_.own_ref, bf16[20,16,512]{2,1,0:T(8,128)(2,1)S(1)} %collective-permute-done.13.refs_2_.refs_0_, ...), custom_call_target="tpu_custom_call" | custom-call | flops 25165824 | bytes 2621440 | tf_op jit(solution)/shard_map/cond/branch_1_fun/pallas_call | solution.py:24
  82.7 0.1 collective-permute-start.59
  82.7 0.6 collective-permute-start.58
  83.3 1.2 %collective-permute-start.57 = (bf16[16,1536]{1,0:T(8,128)(2,1)S(1)}, bf16[16,1536]{1,0:T(8,128)(2,1)S(1)}, u32[]{:S(2)}, u32[]{:S(2)}) collective-permute-start(bf16[16,1536]{1,0:T(8,128)(2,1)S(1)} %get-tuple-element.197.refs_0_), channel_id=1, source_target_pairs={{0,2},{2,0},{1,3},{3,1},{4,6},{6,4},{5,7},{7,5},{8,10},{10,8},{9,1... | collective-permute-start | bytes 147464 | tf_op jit(solution)/shard_map/ppermute | solution.py:369
  84.6 1.7 %collective-permute-done.59.refs_3_ = bf16[16,1536]{1,0:T(8,128)(2,1)S(1)} collective-permute-done((bf16[16,1536]{1,0:T(8,128)(2,1)S(1)}, bf16[16,1536]{1,0:T(8,128)(2,1)S(1)}, u32[]{:S(2)}, u32[]{:S(2)}) %collective-permute-start.59) | collective-permute-done | bytes 49184 | tf_op jit(solution)/shard_map/ppermute | solution.py:459
  86.2 1.1 %collective-permute-done.58.refs_2_ = bf16[16,1536]{1,0:T(8,128)(2,1)S(1)} collective-permute-done((bf16[16,1536]{1,0:T(8,128)(2,1)S(1)}, bf16[16,1536]{1,0:T(8,128)(2,1)S(1)}, u32[]{:S(2)}, u32[]{:S(2)}) %collective-permute-start.58) | collective-permute-done | bytes 49184 | tf_op jit(solution)/shard_map/ppermute | solution.py:369
  87.3 0.0 collective-permute-done.57.refs_1_
  87.3 0.7 copy-done.2
  88.0 2.6 %shard_map.77 = bf16[1536,256]{1,0:T(8,128)(2,1)} custom-call(s32[12]{0:T(128)S(1)} %copy-done.2, bf16[12,16,256]{2,1,0:T(8,128)(2,1)S(1)} %get-tuple-element.196.up_ref, bf16[16,1536]{1,0:T(8,128)(2,1)S(1)} %get-tuple-element.197.refs_0_, bf16[16,1536]{1,0:T(8,128)(2,1)S(1)} %collective-permute-done.57.refs_1_, ...), custom_call_target="tpu_custom_call" | custom-call | flops 25165824 | bytes 3145728 | tf_op jit(solution)/shard_map/pallas_call | solution.py:24
  (8 shorter events, 0.0 us)
Async XLA Ops:
  0.0 10.5 %copy-start.3 = (s32[12]{0:T(128)S(1)}, s32[12]{0:T(128)}, u32[]{:S(2)}) copy-start(s32[12]{0:T(128)} %param.16) | copy-start | bytes 148
  0.0 7.3 %collective-permute-start.54 = (s32[1,12]{1,0:T(1,128)}, s32[1,12]{1,0:T(1,128)S(1)}, u32[]{:S(2)}, u32[]{:S(2)}) collective-permute-start(s32[1,12]{1,0:T(1,128)} %bitcast.25), channel_id=1, source_target_pairs={{0,12},{4,0},{8,4},{12,8},{1,13},{5,1},{9,5},{13,9},{2,14},{6,2},{... | collective-permute-start | bytes 152 | tf_op jit(solution)/shard_map/ppermute | solution.py:399
  5.1 4.6 %collective-permute-start.53 = (s32[1,12]{1,0:T(1,128)}, s32[1,12]{1,0:T(1,128)S(1)}, u32[]{:S(2)}, u32[]{:S(2)}) collective-permute-start(s32[1,12]{1,0:T(1,128)} %bitcast.26), channel_id=1, source_target_pairs={{0,8},{4,12},{8,0},{12,4},{1,9},{5,13},{9,1},{13,5},{2,10},{6,14},... | collective-permute-start | bytes 152 | tf_op jit(solution)/shard_map/ppermute | solution.py:399
  5.1 5.5 %collective-permute-start.52 = (s32[1,12]{1,0:T(1,128)}, s32[1,12]{1,0:T(1,128)S(1)}, u32[]{:S(2)}, u32[]{:S(2)}) collective-permute-start(s32[1,12]{1,0:T(1,128)} %bitcast.27), channel_id=1, source_target_pairs={{0,4},{4,8},{8,12},{12,0},{1,5},{5,9},{9,13},{13,1},{2,6},{6,10},{... | collective-permute-start | bytes 152 | tf_op jit(solution)/shard_map/ppermute | solution.py:399
  6.1 0.7 copy-start.1
  6.8 3.8 %copy-start = (bf16[128,16,256]{2,1,0:T(8,128)(2,1)S(1)}, bf16[128,16,256]{2,1,0:T(8,128)(2,1)}, u32[]{:S(2)}) copy-start(bf16[128,16,256]{2,1,0:T(8,128)(2,1)} %param.14) | copy-start | bytes 3145732
  11.3 7.0 %collective-permute-start.56 = (bf16[32,16,256]{2,1,0:T(8,128)(2,1)S(1)}, bf16[32,16,256]{2,1,0:T(8,128)(2,1)S(1)}, u32[]{:S(2)}, u32[]{:S(2)}) collective-permute-start(bf16[32,16,256]{2,1,0:T(8,128)(2,1)S(1)} %shard_map.75.refs_2_), channel_id=1, source_target_pairs={{0,4},{4,0},{8,12},{12,8},{1,5},{5,1},{9,13},{13,9},{2,6},{6,2},{1... | collective-permute-start | bytes 786440 | tf_op jit(solution)/shard_map/ppermute | solution.py:373
  11.4 5.4 %collective-permute-start.55 = (s32[4,12]{1,0:T(4,128)S(1)}, s32[4,12]{1,0:T(4,128)S(1)}, u32[]{:S(2)}, u32[]{:S(2)}) collective-permute-start(s32[4,12]{1,0:T(4,128)S(1)} %pad_add_fusion.refs_0_.refs_2_), channel_id=1, source_target_pairs={{0,16},{16,0},{1,17},{17,1},{2,18},{18,2},{3,19},{19,3},{4,20},{20... | collective-permute-start | bytes 584 | tf_op jit(solution)/shard_map/ppermute | solution.py:369
  19.4 13.7 %collective-permute-start.15 = (bf16[20,16,768]{2,1,0:T(8,128)(2,1)S(1)}, bf16[20,16,768]{2,1,0:T(8,128)(2,1)S(1)}, u32[]{:S(2)}, u32[]{:S(2)}) collective-permute-start(bf16[20,16,768]{2,1,0:T(8,128)(2,1)S(1)} %get-tuple-element.122), channel_id=1, source_target_pairs={{0,4},{4,0},{8,12},{12,8},{1,5},{5,1},{9,13},{13,9},{2,6},{6,2},{1... | collective-permute-start | bytes 1474568 | tf_op jit(solution)/shard_map/cond/branch_1_fun/ppermute | solution.py:373
  21.4 8.8 %collective-permute-start.16 = (bf16[18,16,256]{2,1,0:T(8,128)(2,1)S(1)}, bf16[18,16,256]{2,1,0:T(8,128)(2,1)S(1)}, u32[]{:S(2)}, u32[]{:S(2)}) collective-permute-start(bf16[18,16,256]{2,1,0:T(8,128)(2,1)S(1)} %get-tuple-element.123), channel_id=1, source_target_pairs={{4,8},{6,10},{0,2},{12,14},{8,4},{10,6},{2,0},{14,12},{5,9},{7,11}... | collective-permute-start | bytes 442376 | tf_op jit(solution)/shard_map/cond/branch_1_fun/ppermute | solution.py:378
  25.6 16.3 %collective-permute-start.14 = (bf16[20,16,768]{2,1,0:T(8,128)(2,1)S(1)}, bf16[20,16,768]{2,1,0:T(8,128)(2,1)S(1)}, u32[]{:S(2)}, u32[]{:S(2)}) collective-permute-start(bf16[20,16,768]{2,1,0:T(8,128)(2,1)S(1)} %get-tuple-element.118.refs_5_), channel_id=1, source_target_pairs={{0,4},{4,0},{8,12},{12,8},{1,5},{5,1},{9,13},{13,9},{2,6},{6,2},{1... | collective-permute-start | bytes 1474568 | tf_op jit(solution)/shard_map/cond/branch_1_fun/ppermute | solution.py:373
  34.0 7.8 %collective-permute-start.17 = (bf16[18,16,768]{2,1,0:T(8,128)(2,1)S(1)}, bf16[18,16,768]{2,1,0:T(8,128)(2,1)S(1)}, u32[]{:S(2)}, u32[]{:S(2)}) collective-permute-start(bf16[18,16,768]{2,1,0:T(8,128)(2,1)S(1)} %get-tuple-element.124.refs_0_), channel_id=1, source_target_pairs={{4,8},{6,10},{0,2},{12,14},{8,4},{10,6},{2,0},{14,12},{5,9},{7,11}... | collective-permute-start | bytes 1327112 | tf_op jit(solution)/shard_map/cond/branch_1_fun/ppermute | solution.py:378
  42.8 14.8 %collective-permute-start.19 = (bf16[2,1536,256]{2,1,0:T(8,128)(2,1)S(1)}, bf16[2,1536,256]{2,1,0:T(8,128)(2,1)S(1)}, u32[]{:S(2)}, u32[]{:S(2)}) collective-permute-start(bf16[2,1536,256]{2,1,0:T(8,128)(2,1)S(1)} %get-tuple-element.128), channel_id=1, source_target_pairs={{0,2},{2,0},{1,3},{3,1},{4,6},{6,4},{5,7},{7,5},{8,10},{10,8},{9,1... | collective-permute-start | bytes 4718600 | tf_op jit(solution)/shard_map/cond/branch_1_fun/ppermute | solution.py:369
  43.3 14.2 %collective-permute-start.18 = (bf16[18,16,768]{2,1,0:T(8,128)(2,1)S(1)}, bf16[18,16,768]{2,1,0:T(8,128)(2,1)S(1)}, u32[]{:S(2)}, u32[]{:S(2)}) collective-permute-start(bf16[18,16,768]{2,1,0:T(8,128)(2,1)S(1)} %get-tuple-element.127.refs_0_), channel_id=1, source_target_pairs={{4,8},{6,10},{0,2},{12,14},{8,4},{10,6},{2,0},{14,12},{5,9},{7,11}... | collective-permute-start | bytes 1327112 | tf_op jit(solution)/shard_map/cond/branch_1_fun/ppermute | solution.py:378
  43.4 12.5 %collective-permute-start.13 = (bf16[20,16,512]{2,1,0:T(8,128)(2,1)S(1)}, bf16[20,16,512]{2,1,0:T(8,128)(2,1)S(1)}, u32[]{:S(2)}, u32[]{:S(2)}) collective-permute-start(bf16[20,16,512]{2,1,0:T(8,128)(2,1)S(1)} %get-tuple-element.116.refs_6_), channel_id=1, source_target_pairs={{0,4},{4,0},{8,12},{12,8},{1,5},{5,1},{9,13},{13,9},{2,6},{6,2},{1... | collective-permute-start | bytes 983048 | tf_op jit(solution)/shard_map/cond/branch_1_fun/ppermute | solution.py:373
  47.4 10.1 %collective-permute-start.20 = (bf16[12,16,256]{2,1,0:T(8,128)(2,1)S(1)}, bf16[12,16,256]{2,1,0:T(8,128)(2,1)S(1)}, u32[]{:S(2)}, u32[]{:S(2)}) collective-permute-start(bf16[12,16,256]{2,1,0:T(8,128)(2,1)S(1)} %get-tuple-element.129), channel_id=1, source_target_pairs={{0,4},{4,0},{8,12},{12,8},{1,5},{5,1},{9,13},{13,9},{2,6},{6,2},{1... | collective-permute-start | bytes 294920 | tf_op jit(solution)/shard_map/cond/branch_1_fun/ppermute | solution.py:373
  58.7 20.5 %collective-permute-start.25 = (bf16[1536,256]{1,0:T(8,128)(2,1)S(1)}, bf16[1536,256]{1,0:T(8,128)(2,1)S(1)}, u32[]{:S(2)}, u32[]{:S(2)}) collective-permute-start(bf16[1536,256]{1,0:T(8,128)(2,1)S(1)} %fusion.1), channel_id=1, source_target_pairs={{0,1},{1,0},{2,3},{3,2},{4,5},{5,4},{6,7},{7,6},{8,9},{9,8},{10,11... | collective-permute-start | bytes 2359304 | tf_op jit(solution)/shard_map/cond/branch_1_fun/ppermute | solution.py:369
  60.2 9.9 %collective-permute-start.22 = (bf16[12,16,768]{2,1,0:T(8,128)(2,1)S(1)}, bf16[12,16,768]{2,1,0:T(8,128)(2,1)S(1)}, u32[]{:S(2)}, u32[]{:S(2)}) collective-permute-start(bf16[12,16,768]{2,1,0:T(8,128)(2,1)S(1)} %get-tuple-element.132), channel_id=1, source_target_pairs={{0,4},{4,0},{8,12},{12,8},{1,5},{5,1},{9,13},{13,9},{2,6},{6,2},{1... | collective-permute-start | bytes 884744 | tf_op jit(solution)/shard_map/cond/branch_1_fun/ppermute | solution.py:373
  62.0 10.8 %collective-permute-start.21 = (bf16[18,16,512]{2,1,0:T(8,128)(2,1)S(1)}, bf16[18,16,512]{2,1,0:T(8,128)(2,1)S(1)}, u32[]{:S(2)}, u32[]{:S(2)}) collective-permute-start(bf16[18,16,512]{2,1,0:T(8,128)(2,1)S(1)} %get-tuple-element.131.refs_7_), channel_id=1, source_target_pairs={{4,8},{6,10},{0,2},{12,14},{8,4},{10,6},{2,0},{14,12},{5,9},{7,11}... | collective-permute-start | bytes 884744 | tf_op jit(solution)/shard_map/cond/branch_1_fun/ppermute | solution.py:378
  62.0 14.5 %collective-permute-start.24 = (bf16[12,16,768]{2,1,0:T(8,128)(2,1)S(1)}, bf16[12,16,768]{2,1,0:T(8,128)(2,1)S(1)}, u32[]{:S(2)}, u32[]{:S(2)}) collective-permute-start(bf16[12,16,768]{2,1,0:T(8,128)(2,1)S(1)} %get-tuple-element.134), channel_id=1, source_target_pairs={{0,4},{4,0},{8,12},{12,8},{1,5},{5,1},{9,13},{13,9},{2,6},{6,2},{1... | collective-permute-start | bytes 884744 | tf_op jit(solution)/shard_map/cond/branch_1_fun/ppermute | solution.py:373
  73.6 6.8 %collective-permute-start.23 = (bf16[12,16,512]{2,1,0:T(8,128)(2,1)S(1)}, bf16[12,16,512]{2,1,0:T(8,128)(2,1)S(1)}, u32[]{:S(2)}, u32[]{:S(2)}) collective-permute-start(bf16[12,16,512]{2,1,0:T(8,128)(2,1)S(1)} %branch_1_fun.22), channel_id=1, source_target_pairs={{0,4},{4,0},{8,12},{12,8},{1,5},{5,1},{9,13},{13,9},{2,6},{6,2},{1... | collective-permute-start | bytes 589832 | tf_op jit(solution)/shard_map/cond/branch_1_fun/ppermute | solution.py:373
  82.7 3.6 %collective-permute-start.59 = (bf16[16,1536]{1,0:T(8,128)(2,1)S(1)}, bf16[16,1536]{1,0:T(8,128)(2,1)S(1)}, u32[]{:S(2)}, u32[]{:S(2)}) collective-permute-start(bf16[16,1536]{1,0:T(8,128)(2,1)S(1)} %get-tuple-element.197.refs_0_), channel_id=1, source_target_pairs={{0,3},{1,2},{2,1},{3,0},{4,7},{5,6},{6,5},{7,4},{8,11},{9,10},{10,... | collective-permute-start | bytes 147464 | tf_op jit(solution)/shard_map/ppermute | solution.py:459
  82.7 4.6 %collective-permute-start.58 = (bf16[16,1536]{1,0:T(8,128)(2,1)S(1)}, bf16[16,1536]{1,0:T(8,128)(2,1)S(1)}, u32[]{:S(2)}, u32[]{:S(2)}) collective-permute-start(bf16[16,1536]{1,0:T(8,128)(2,1)S(1)} %get-tuple-element.197.refs_0_), channel_id=1, source_target_pairs={{0,1},{1,0},{2,3},{3,2},{4,5},{5,4},{6,7},{7,6},{8,9},{9,8},{10,11... | collective-permute-start | bytes 147464 | tf_op jit(solution)/shard_map/ppermute | solution.py:369
  83.3 4.0 %collective-permute-start.57 = (bf16[16,1536]{1,0:T(8,128)(2,1)S(1)}, bf16[16,1536]{1,0:T(8,128)(2,1)S(1)}, u32[]{:S(2)}, u32[]{:S(2)}) collective-permute-start(bf16[16,1536]{1,0:T(8,128)(2,1)S(1)} %get-tuple-element.197.refs_0_), channel_id=1, source_target_pairs={{0,2},{2,0},{1,3},{3,1},{4,6},{6,4},{5,7},{7,5},{8,10},{10,8},{9,1... | collective-permute-start | bytes 147464 | tf_op jit(solution)/shard_map/ppermute | solution.py:369
  87.3 0.7 copy-start.2

commit v3 on v2

--- a/solution.py
+++ b/solution.py
@@ -11,16 +11,17 @@
 MIB = 1 << 20
 LANES = 128
 LARGE = 1 << 21
+PER = 6
 SHARE = 1.0
 VMEM = pl.BlockSpec(memory_space=pltpu.VMEM)
 SMEM = pl.BlockSpec(memory_space=pltpu.SMEM)
 ANY = pl.BlockSpec(memory_space=pl.ANY)
 NT = (((1,), (1,)), ((), ()))
 TN = (((0,), (0,)), ((), ()))
-PLANS = ((18, 16, 12), (20, 18, 12), (23, 21, 12))
-
-
-def call(kernel, ins, specs, outs, out_specs, *, after=(), vmem=24, flops=0, nbytes=0, **kwargs):
+PLANS = ((17, 15, 10), (18, 16, 11), (20, 17, 12), (23, 20, 12))
+
+
+def call(kernel, ins, specs, outs, out_specs, *, after=(), free=None, vmem=24, flops=0, nbytes=0, **kwargs):
     return pl.pallas_call(
         functools.partial(kernel, len(ins)),
         in_specs=specs + [ANY] * len(after),
@@ -29,7 +30,7 @@
         compiler_params=pltpu.CompilerParams(vmem_limit_bytes=vmem * MIB),
         cost_estimate=pl.CostEstimate(flops=int(SHARE * flops), bytes_accessed=int(SHARE * nbytes), transcendentals=0),
         **kwargs,
-    )(*[placed(x) for x in ins], *after)
+    )(*[x if free is True or x is free else placed(x) for x in ins], *after)
 
 
 def placed(x):
@@ -56,10 +57,25 @@
         kron_ref[t * rank : (t + 1) * rank, :] = jnp.where(diagonal, spread[t : t + 1, :], 0.0).astype(BF16)
 
 
-def make_kron(alloc, rank):
+def first_kernel(rank, ins, alloc_ref, library_ref, own_ref, kron_ref):
+    kron_kernel(rank, 1, alloc_ref, kron_ref)
+    made = jnp.dot(kron_ref[...], library_ref[...], preferred_element_type=F32).astype(BF16)
+    own_ref[...] = made.reshape(own_ref.shape)
+
+
+def compose_first(alloc, library, rank):
     tenants, skills = alloc.shape
+    depth, out = library.shape
     return call(
-        functools.partial(kron_kernel, rank), [alloc], [VMEM], shape(tenants * rank, skills * rank), VMEM, vmem=16
+        functools.partial(first_kernel, rank),
+        [pltpu.with_memory_space_constraint(x, pltpu.HBM) for x in (alloc, library)],
+        [pl.BlockSpec(x.shape, lambda j: (0, 0)) for x in (alloc, library)],
+        [shape(tenants, rank, out), shape(tenants * rank, depth)],
+        [VMEM] * 2,
+        free=True,
+        grid=(1,),
+        flops=2 * tenants * rank * depth * out,
+        nbytes=2 * depth * out,
     )
 
 
@@ -104,7 +120,7 @@
     return made if slots else made[0]
 
 
-def tables_kernel(n, tenants, plans, ins, place_ref, *refs):
+def tables_kernel(n, tenants, plans, ins, place_ref, len_ref, *refs):
     arrays, tab_ref, plan_ref = refs[:-2], refs[-2], refs[-1]
     me = place_ref[0]
     blocks = arrays[0].shape[1]
@@ -161,6 +177,7 @@
     for row, value in enumerate(rows):
         tab_ref[row : row + 1, :] = value.astype(I32)
     tab_ref[len(rows) : len(rows) + 1, :] = own
+    tab_ref[len(rows) + 2 : len(rows) + 3, :] = jnp.concatenate([len_ref[...], jnp.zeros((1, LANES - blocks), I32)], axis=1)
     ends_here = jnp.logical_or(me == 0, me == n - 1)
     tab_ref[len(rows) + 1 : len(rows) + 2, :] = jnp.where(ends_here, jnp.ones_like(own), jnp.zeros_like(own))
 
@@ -181,43 +198,73 @@
     plan_ref[0] = plan
 
 
-def make_tables(n, tenants, plans, place, arrays):
-    rows = -(-(3 * (n - 1) + 2) // 8) * 8
+def make_tables(n, tenants, plans, place, lens, arrays):
+    rows = -(-(3 * (n - 1) + 3) // 8) * 8
     return call(
         functools.partial(tables_kernel, n, tenants, plans),
-        [place, *arrays],
-        [SMEM] + [VMEM] * len(arrays),
+        [place, lens, *arrays],
+        [SMEM] + [VMEM] * (1 + len(arrays)),
         [shape(rows, LANES, dtype=I32), shape(1, dtype=I32)],
         [VMEM, SMEM],
     )
 
 
-def step_kernel(n, jobs, passed, ins, *refs):
-    tab_ref = refs[0]
-    ins -= 1
-    given, outs = list(refs[1 : 1 + ins]), refs[1 + ins + passed : 1 + ins + passed + len(jobs)]
-    for (hop, slots, by_tenant), out_ref in zip(jobs, outs):
-        own_ref = given.pop(0)
-        in_ref = given.pop(0) if hop else None
-
-        def one(slot, carry, hop=hop, by_tenant=by_tenant, own_ref=own_ref, in_ref=in_ref, out_ref=out_ref):
+def step_kernel(n, jobs, passed, ins, tab_ref, *refs):
+    given, outs = list(refs[: ins - 1]), refs[ins - 1 + passed :]
+    for (hop, slots, pieces), out_ref in zip(jobs, outs):
+        both = slots is None
+        if both:
+            slots = out_ref.shape[0] // 2
+            fresh_ref = given.pop(0)
+
+            @pl.when(tab_ref[3 * (n - 1) + 1, 0] > 0)
+            def _(fresh_ref=fresh_ref, out_ref=out_ref):
+                out_ref[: fresh_ref.shape[0]] = fresh_ref[...]
+
+        held = [(given.pop(0), given.pop(0) if hop else None) for _ in pieces]
+
+        def one(slot, carry, hop=hop, pieces=pieces, held=held, out_ref=out_ref, both=both, slots=slots):
             tenant = tab_ref[hop, slot]
-            block = own_ref[tenant]
-            if hop:
-                index = tenant if by_tenant else tab_ref[n - 1 + hop, slot]
-                block = (block.astype(F32) + in_ref[index].astype(F32)).astype(BF16)
-            out_ref[slot] = block
+            at = 0
+            made = []
+            for by_tenant, (own_ref, in_ref) in zip(pieces, held):
+                block = own_ref[tenant]
+                if hop:
+                    index = tenant if by_tenant else tab_ref[n - 1 + hop, slot]
+                    block = (block.astype(F32) + in_ref[index].astype(F32)).astype(BF16)
+                made.append(block)
+            block = jnp.concatenate(made, axis=1) if len(made) > 1 else made[0]
+            if both:
+                half = out_ref.shape[2]
+                out_ref[slot] = block[:, :half]
+                out_ref[slots + slot] = block[:, half:]
+            else:
+                out_ref[slot] = block
             return carry
 
-        lax.fori_loop(0, slots, one, 0, unroll=4)
+        def all_slots(one=one, slots=slots):
+            lax.fori_loop(0, slots, one, 0, unroll=4)
+
+        if both:
+            pl.when(tab_ref[3 * (n - 1) + 1, 0] == 0)(all_slots)
+        else:
+            all_slots()
 
 
 def step(n, tab, jobs, after=(), through=()):
     ins, shapes, plan = [], [], []
-    for hop, slots, own, arrived, by_tenant in jobs:
-        plan.append((hop, slots, by_tenant))
-        ins += [own, arrived] if hop else [own]
-        shapes.append(jax.ShapeDtypeStruct((slots,) + own.shape[1:], BF16))
+    for hop, slots, pieces in jobs:
+        columns = sum(own.shape[2] for own, _, _ in pieces)
+        if isinstance(slots, tuple):
+            plan.append((hop, None, [by_tenant for _, _, by_tenant in pieces]))
+            ins.append(slots[1])
+            slots, columns = 2 * slots[0], columns // 2
+            assert slots >= ins[-1].shape[0] and columns == ins[-1].shape[2]
+        else:
+            plan.append((hop, slots, [by_tenant for _, _, by_tenant in pieces]))
+        for own, arrived, _ in pieces:
+            ins += [own, arrived] if hop else [own]
+        shapes.append(shape(slots, pieces[0][0].shape[1], columns))
     return call(
         functools.partial(step_kernel, n, plan, len(after) + len(through)),
         [tab, *ins],
@@ -230,13 +277,28 @@
     )
 
 
-def factor_of(n, b, by_tenant, tab_ref, own_ref, arrived):
+def read(ref, slot, start, size):
+    half = ref.shape[2]
+    if start + size <= half and start == 0 and size == half:
+        return ref[slot]
+    slots = ref.shape[0] // 2
+    pieces = []
+    while size:
+        part, at = divmod(start, half)
+        count = min(size, half - at)
+        pieces.append(ref[part * slots + slot, :, at : at + count])
+        start, size = start + count, size - count
+    return jnp.concatenate(pieces, axis=1) if len(pieces) > 1 else pieces[0]
+
+
+def factor_of(n, b, by_tenant, tab_ref, own_ref, arrived, lead=0):
     tenant = tab_ref[3 * (n - 1), b]
     factor = own_ref[tenant].astype(F32)
     outer = tab_ref[3 * (n - 1) + 1, 0] > 0
     for hop in range(n - 1):
         index = tenant if by_tenant and hop == 0 else tab_ref[2 * (n - 1) + hop, b]
-        came = arrived[hop][index].astype(F32)
+        came = read(arrived[hop], index, lead, own_ref.shape[2]) if hop == n - 2 else arrived[hop][index]
+        came = came.astype(F32)
         used = jnp.where(outer, 1, 0) if hop == n - 2 else jnp.where(outer, 0, 1)
         factor = jnp.where(used > 0, factor + came, factor)
     return factor.astype(BF16)
@@ -256,7 +318,7 @@
             part = total_ref[:, at] + part
         outs[0][:, at] = part.astype(outs[0].dtype)
         if out:
-            outs[1][b] = factor_of(n, b, True, tab_ref, refs[n - 1], refs[n : 2 * n - 1])
+            outs[1][b] = factor_of(n, b, True, tab_ref, refs[n - 1], refs[n : 2 * n - 1], own_ref.shape[2])
         return carry
 
     lax.fori_loop(0, tokens_ref.shape[0] // LANES, one, 0, unroll=4)
@@ -280,88 +342,97 @@
         outs,
         [VMEM] * len(outs),
         after=after,
+        free=tokens,
         grid=(1,),
         flops=2 * rows * size * rank,
         nbytes=2 * size * (rows + 2 * tenants * rank),
     )
 
 
-def base_kernel(order_ref, tokens_ref, weight_ref, *refs):
-    refs[-1][0] = jnp.dot(tokens_ref[...], weight_ref[...], preferred_element_type=F32).astype(BF16)
-
-
-def base_product(order, tokens, weight, out, after):
+def base_kernel(order_ref, tokens_ref, first_ref, second_ref, *refs):
+    for weight_ref, out_ref in ((first_ref, refs[-2]), (second_ref, refs[-1])):
+        out_ref[...] = jnp.dot(tokens_ref[...], weight_ref[...], preferred_element_type=F32).astype(BF16)
+
+
+def base_product(order, tokens, weight, out, after, strips=3):
     rows, width = tokens.shape
     flops, nbytes = 4 * rows * width * out, 2 * (rows * (width + 2 * out) + 2 * width * out)
     return pl.pallas_call(
         base_kernel,
         grid_spec=pltpu.PrefetchScalarGridSpec(
             num_scalar_prefetch=1,
-            grid=(2, 2),
+            grid=(strips,),
             in_specs=[
-                pl.BlockSpec((rows // 2, width), lambda q, m, order: ((q + m) % 2, 0)),
-                pl.BlockSpec((width, out), lambda q, m, order: (0, order[q])),
+                pl.BlockSpec((rows // strips, width), lambda m, order: (m, 0)),
+                pl.BlockSpec((width, out), lambda m, order: (0, order[0])),
+                pl.BlockSpec((width, out), lambda m, order: (0, order[1])),
             ]
             + [ANY] * len(after),
-            out_specs=pl.BlockSpec((1, rows // 2, out), lambda q, m, order: (q, (q + m) % 2, 0)),
+            out_specs=[pl.BlockSpec((rows // strips, out), lambda m, order: (m, 0))] * 2,
         ),
-        out_shape=shape(2, rows, out),
+        out_shape=[shape(rows, out)] * 2,
         compiler_params=pltpu.CompilerParams(vmem_limit_bytes=24 * MIB),
         cost_estimate=pl.CostEstimate(flops=int(SHARE * flops), bytes_accessed=int(SHARE * nbytes), transcendentals=0),
-    )(order, placed(tokens), placed(weight), *after)
-
-
-def gather_kernel(ins, a_ref, b_ref, c_ref, out_ref):
-    out_ref[...] = (a_ref[0].astype(F32) + b_ref[0].astype(F32) + c_ref[...].astype(F32)).astype(out_ref.dtype)
-
-
-def gather_base(keep, from_core, across):
-    rows, width = across.shape
-    half = pl.BlockSpec((1, rows, width), lambda j: (1, 0, 0))
-    whole = pl.BlockSpec((rows, width), lambda j: (0, 0))
+    )(order, tokens, placed(weight), placed(weight), *after)
+
+
+def near_kernel(ins, a_ref, b_ref, *outs):
+    rows = outs[0].shape[0]
+    for i, out_ref in enumerate(outs):
+        at = slice(i * rows, (i + 1) * rows)
+        out_ref[...] = (a_ref[at, :].astype(F32) + b_ref[at, :].astype(F32)).astype(BF16)
+
+
+def add_halves(a, b):
+    rows, width = a.shape
+    return call(near_kernel, [a, b], [VMEM] * 2, [shape(rows // 2, width)] * 2, [VMEM] * 2, nbytes=6 * rows * width)
+
+
+def gather_kernel(ins, a_ref, b_ref, *refs):
+    rows = refs[0].shape[0]
+    for i, part_ref in enumerate(refs[: ins - 2]):
+        at = slice(i * rows, (i + 1) * rows)
+        total = a_ref[at, :].astype(F32) + b_ref[at, :].astype(F32) + part_ref[...].astype(F32)
+        refs[-1][at, :] = total.astype(BF16)
+
+
+def gather_base(a, b, halves, after):
     return call(
-        gather_kernel,
-        [keep, from_core, across],
-        [half, half, whole],
-        shape(rows, width),
-        whole,
-        nbytes=8 * rows * width,
-        grid=(1,),
-    )
-
-
-def finish_kernel(per, ins, len_ref, up_ref, *refs):
+        gather_kernel, [a, b, *halves], [VMEM] * 4, shape(*a.shape), VMEM, after=after, nbytes=8 * a.size
+    )
+
+
+def finish_kernel(row, per, ins, tab_ref, up_ref, *refs):
     lows, base_ref, out_ref = refs[:4], refs[4], refs[5]
     width = out_ref.shape[1]
+    low = lows[0][...].astype(F32)
+    for other in lows[1:]:
+        low = low + other[...].astype(F32)
+    low = low.astype(BF16)
     for j in range(per):
         b = pl.program_id(0) * per + j
         at = slice(j * LANES, (j + 1) * LANES)
-        low = lows[0][:, at].astype(F32)
-        for other in lows[1:]:
-            low = low + other[:, at].astype(F32)
-        high = low.astype(BF16)
-        rest = (low - high.astype(F32)).astype(BF16)
-        total = lax.dot_general(high, up_ref[b], TN, preferred_element_type=F32)
-        total = total + lax.dot_general(rest, up_ref[b], TN, preferred_element_type=F32)
+        total = lax.dot_general(low[:, at], up_ref[b], TN, preferred_element_type=F32)
         total = total + base_ref[at, :].astype(F32)
-        live = lax.broadcasted_iota(I32, (LANES, width), 0) < len_ref[b]
+        live = lax.broadcasted_iota(I32, (LANES, width), 0) < tab_ref[row, b]
         out_ref[at, :] = jnp.where(live, total, 0.0).astype(out_ref.dtype)
 
 
-def finish(lens, up, lows, base, per):
+def finish(tab, row, up, lows, base, per):
     rank, rows = lows[0].shape
     width = base.shape[1]
     blocks = rows // LANES
     whole = pl.BlockSpec((per * LANES, width), lambda j: (j, 0))
     return call(
-        functools.partial(finish_kernel, per),
-        [lens, up, *lows, base],
+        functools.partial(finish_kernel, row, per),
+        [tab, up, *lows, pltpu.with_memory_space_constraint(base, pltpu.HBM)],
         [SMEM, VMEM] + [pl.BlockSpec((rank, per * LANES), lambda j: (0, j))] * 4 + [whole],
         shape(rows, width),
         whole,
+        free=True,
         grid=(blocks // per,),
-        flops=4 * rows * rank * width,
-        nbytes=8 * rows * width,
+        flops=2 * rows * rank * width,
+        nbytes=4 * rows * width,
     )
 
 
@@ -371,6 +442,14 @@
 
 def ends(x):
     return lax.ppermute(x, "skill", [(0, 1), (1, 0), (2, 3), (3, 2)])
+
+
+def inward(x):
+    return lax.ppermute(x, "skill", [(0, 1), (3, 2)])
+
+
+def outward(x):
+    return lax.ppermute(x, "skill", [(1, 0), (2, 3)])
 
 
 def middle(x):
@@ -399,65 +478,69 @@
         + [lax.ppermute(own_t, "skill", [(j, (j + k) % n) for j in range(n)]) for k in range(1, n)],
         axis=0,
     )
+    library = jnp.transpose(skill_down, (0, 2, 1)).reshape(local_skills * rank, width)
+    own_up, kron = compose_first(alloc, skill_up.reshape(local_skills * rank, out), rank)
+    own_up, seen = lax.optimization_barrier((own_up, seen))
+    up_0 = ends(own_up)
     seen = [seen, swap(seen, "group")]
-    kron = make_kron(alloc, rank)
-    library = jnp.transpose(skill_down, (0, 2, 1)).reshape(local_skills * rank, width)
-    own_up = compose(kron, skill_up.reshape(local_skills * rank, out), rank, (0, out), out, after=[seen[0]])
-    up_0 = ends(own_up)
     own_0 = compose(kron, library, rank, parts[0], tile, after=[own_up])
-    tab, plan = make_tables(n, tenants, plans, me.reshape(1).astype(I32), seen)
-    other, mine = (1 - tensor) * 2, tensor * 2
-    order_away = jnp.stack([other + 1 - dp, other + dp]).astype(I32)
-    order_keep = jnp.stack([mine + 1 - dp, mine + dp]).astype(I32)
+    tab, plan = make_tables(n, tenants, plans, me.reshape(1).astype(I32), block_len.reshape(1, blocks), seen)
+    theirs, ours = (1 - tensor) * 2, tensor * 2
+    order_cross = jnp.stack([theirs + 1 - dp, ours + 1 - dp]).astype(I32)
+    order_stay = jnp.stack([theirs + dp, ours + dp]).astype(I32)
 
     def planned(sizes):
         owns, arrived, up_came = [own_0], [[], [], []], [up_0]
 
         def job(h, k):
-            return h, sizes[h], owns[k], arrived[k][h - 1] if h else None, False
-
-        def up_job(h):
-            return h, sizes[h], own_up, up_came[h - 1], h == 1
-
-        first, up_1 = step(n, tab, [job(0, 0), up_job(1)])
+            return h, sizes[h], [(owns[k], arrived[k][h - 1] if h else None, False)]
+
+        up_piece = (own_up, up_0, True)
+        first, up_1 = step(n, tab, [job(0, 0), (1, sizes[1], [up_piece])])
         arrived[0].append(ends(first))
         up_came.append(middle(up_1))
-        sent = []
-        for k in (1, 2):
-            own, message = compose(kron, library, rank, parts[k], tile, sizes[0], tab)
-            owns.append(own)
-            sent.append(message)
-            arrived[k].append(ends(message))
-
-        to_1, up_2 = step(n, tab, [job(1, 0), up_job(2)], sent)
+        own, message = compose(kron, library, rank, parts[1], tile, sizes[0], tab)
+        owns.append(own)
+        arrived[1].append(ends(message))
+        away, keep = base_product(order_cross, tokens, base_weight, out, [message])
+
+        to_1, away = step(n, tab, [job(1, 0)], [keep, up_came[1]], [away])
         arrived[0].append(middle(to_1))
-        up_came.append(ends(up_2))
-        away = base_product(order_away, tokens, base_weight, out, [to_1])
-
-        to_1, to_2, away = step(n, tab, [job(1, 1), job(2, 0)], [], [away])
+        from_core = swap(away, "tensor")
+        own, message = compose(kron, library, rank, parts[2], tile, sizes[0], tab, [to_1])
+        owns.append(own)
+
+        first_and_up = 2, ((max(sizes[2], (sizes[0] + 1) // 2)), message), [(owns[0], arrived[0][1], False), (own_up, up_came[1], False)]
+        to_1, to_2, keep = step(n, tab, [job(1, 1), first_and_up], [from_core], [keep])
         arrived[1].append(middle(to_1))
-        arrived[0].append(ends(to_2))
+        exchanged = ends(to_2)
+        arrived[0].append(exchanged)
+        arrived[2].append(exchanged)
+        up_came.append(exchanged)
+        near = add_halves(keep, from_core)
+        across = [swap(near[0], "dp")]
+        away, keep = base_product(order_stay, tokens, base_weight, out, [owns[2]])
+
+        to_1, to_2, away, near_2 = step(
+            n, tab, [job(1, 2), job(2, 1)], [across[0], arrived[0][2], keep], [away, near[1]]
+        )
+        arrived[2].append(middle(to_1))
+        arrived[1].append(outward(to_2))
+        across.append(swap(near_2, "dp"))
         from_core = swap(away, "tensor")
-        keep = base_product(order_keep, tokens, base_weight, out, [to_1])
-
-        to_1, to_2, keep = step(n, tab, [job(1, 2), job(2, 1)], [from_core, up_came[2]], [keep])
-        arrived[2].append(middle(to_1))
-        arrived[1].append(ends(to_2))
-        near = (keep[0].astype(F32) + from_core[0].astype(F32)).astype(BF16)
-        across = swap(near, "dp")
         low, up = project(n, tab, tokens, owns[0], parts[0], arrived[0], None, False, (own_up, up_came), [to_1])
 
-        (to_2,) = step(n, tab, [job(2, 2)], [low])
-        arrived[2].append(ends(to_2))
-        (low,) = project(n, tab, tokens, owns[1], parts[1], arrived[1], low, False)
-        base = gather_base(keep, from_core, across)
+        (to_2,) = step(n, tab, [job(2, 2)], [low, from_core])
+        arrived[2].append(outward(to_2))
+        (low,) = project(n, tab, tokens, owns[1], parts[1], arrived[1], low, False, None, [to_2])
+        base = gather_base(keep, from_core, across, [low])
         (low,) = project(n, tab, tokens, owns[2], parts[2], arrived[2], low, True, None, [base])
         return low, up, base
 
     low, up, base = lax.switch(plan[0], [functools.partial(planned, sizes) for sizes in plans])
     lows = [low, swap(low, "tensor"), swap(low, "dp")]
     lows.append(lax.ppermute(low, ("tensor", "dp"), [(0, 3), (1, 2), (2, 1), (3, 0)]))
-    return finish(block_len, up, lows, base, 6)
+    return finish(tab, 3 * (n - 1) + 2, up, lows, base, PER)
 
 
 def plain_body(tokens, base_weight, skill_down, skill_up, alloc, block_tenant, block_len):

time: 89.8 us -> 84.1 us (0.937); the launches traced: 90.6 us -> 82.5 us
  Pallas kernels: 43.9 us -> 38.6 us
  starting transfers between devices: 24.1 us -> 19.7 us
  waiting for transfers between devices: 19.7 us -> 22 us
  local copies, waits for them, and re-layouts: 1.38 us -> 0.01 us
    ppermute x8 -> x4, starting transfers between devices: 12.3 us -> 4.69 us  [ends(): return lax.ppermute(x, 'skill', [(0, 1), (1, 0), (2, 3), (3, 2)])]
    ppermute x0 -> x2, waiting for transfers between devices: none -> 6.17 us  [outward(): return lax.ppermute(x, 'skill', [(1, 0), (2, 3)])]
    pallas_call x2, Pallas kernels: 15.4 us -> 11.8 us  [base_product(): pl.pallas_call(base_kernel, grid_spec=pltpu.PrefetchScalarGridSpec(num_sc...]
    ppermute x8 -> x4, waiting for transfers between devices: 13.8 us -> 11.1 us  [ends(): return lax.ppermute(x, 'skill', [(0, 1), (1, 0), (2, 3), (3, 2)])]
    ppermute x0 -> x2, starting transfers between devices: none -> 2.57 us  [outward(): return lax.ppermute(x, 'skill', [(1, 0), (2, 3)])]
    pallas_call x16, Pallas kernels: 28.5 us -> 26.8 us  [call(): pl.pallas_call(functools.partial(kernel, len(ins)), in_specs=specs + [ANY...]
    unnamed x8 -> x6, local copies, waits for them, and re-layouts: 1.38 us -> 0.01 us
    ppermute x3, waiting for transfers between devices: 3.17 us -> 1.97 us  [line_body(): lax.ppermute(own_t, 'skill', [(j, (j + k) % n) for j in range(n)])]
  transfers between devices with their start and end apart: 21 -> 21, of which waited for: 9 -> 9; matrix products, arithmetic and copies ran while one was open for 0% -> 0% of each run, Pallas kernels for 39% -> 38%
where the time goes in v3:
time: 84.1 us; the launch traced here: 82.5 us
  Pallas kernels  38.6 us (46%)
  waiting for transfers between devices  22 us (26%)
  starting transfers between devices  19.7 us (23%)
    pallas_call x16, Pallas kernels, call(): pl.pallas_call(functools.partial(kernel, len(ins)), in_specs=specs + [ANY...  26.8 us
    pallas_call x2, Pallas kernels, base_product(): pl.pallas_call(base_kernel, grid_spec=pltpu.PrefetchScalarGridSpec(num_sc...  11.8 us
    ppermute x4, waiting for transfers between devices, ends(): return lax.ppermute(x, 'skill', [(0, 1), (1, 0), (2, 3), (3, 2)])  11.1 us
    ppermute x2, waiting for transfers between devices, outward(): return lax.ppermute(x, 'skill', [(1, 0), (2, 3)])  6.17 us
    ppermute x3, starting transfers between devices, line_body(): lax.ppermute(own_t, 'skill', [(j, (j + k) % n) for j in range(n)])  6.06 us
    ppermute x7, starting transfers between devices, swap(): return lax.ppermute(x, axis, [(0, 1), (1, 0)])  5.61 us
    ppermute x4, starting transfers between devices, ends(): return lax.ppermute(x, 'skill', [(0, 1), (1, 0), (2, 3), (3, 2)])  4.69 us
    ppermute x2, starting transfers between devices, outward(): return lax.ppermute(x, 'skill', [(1, 0), (2, 3)])  2.57 us
  transfers between devices with their start and end apart: 21, of which 9 were waited for; matrix products, arithmetic and copies ran while one was open for 0% of the time, Pallas kernels for 38%

profile of v3, /device:TPU:0, one launch (start us, length us, event | category | flops | bytes accessed | tf_op | source)
XLA Modules:
  0.0 82.5 jit_solution(3188564870904096798)
XLA Ops:
  0.0 5.0 %collective-permute-start.67 = (s32[1,12]{1,0:T(1,128)}, s32[1,12]{1,0:T(1,128)S(1)}, u32[]{:S(2)}, u32[]{:S(2)}) collective-permute-start(s32[1,12]{1,0:T(1,128)} %bitcast.21), channel_id=1, source_target_pairs={{0,12},{4,0},{8,4},{12,8},{1,13},{5,1},{9,5},{13,9},{2,14},{6,2},{... | collective-permute-start | bytes 152 | tf_op jit(solution)/shard_map/ppermute | solution.py:478
  5.0 0.0 collective-permute-start.66
  5.1 1.0 %collective-permute-start.65 = (s32[1,12]{1,0:T(1,128)}, s32[1,12]{1,0:T(1,128)S(1)}, u32[]{:S(2)}, u32[]{:S(2)}) collective-permute-start(s32[1,12]{1,0:T(1,128)} %bitcast.23), channel_id=1, source_target_pairs={{0,4},{4,8},{8,12},{12,0},{1,5},{5,9},{9,13},{13,1},{2,6},{6,10},{... | collective-permute-start | bytes 152 | tf_op jit(solution)/shard_map/ppermute | solution.py:478
  6.1 2.5 %shard_map.73 = (bf16[32,16,256]{2,1,0:T(8,128)(2,1)S(1)}, bf16[512,2048]{1,0:T(8,128)(2,1)S(1)}) custom-call(f32[32,128]{1,0:T(8,128)} %alloc_ref.1, bf16[2048,256]{1,0:T(8,128)(2,1)} %bitcast.25), custom_call_target="tpu_custom_call" | custom-call | flops 536870912 | bytes 1048576 | tf_op jit(solution)/shard_map/pallas_call | solution.py:25
  8.6 0.0 collective-permute-done.67
  8.6 1.1 %collective-permute-done.66 = s32[1,12]{1,0:T(1,128)S(1)} collective-permute-done((s32[1,12]{1,0:T(1,128)}, s32[1,12]{1,0:T(1,128)S(1)}, u32[]{:S(2)}, u32[]{:S(2)}) %collective-permute-start.66) | collective-permute-done | bytes 80 | tf_op jit(solution)/shard_map/ppermute | solution.py:478
  9.6 0.9 %collective-permute-done.65 = s32[1,12]{1,0:T(1,128)S(1)} collective-permute-done((s32[1,12]{1,0:T(1,128)}, s32[1,12]{1,0:T(1,128)S(1)}, u32[]{:S(2)}, u32[]{:S(2)}) %collective-permute-start.65) | collective-permute-done | bytes 80 | tf_op jit(solution)/shard_map/ppermute | solution.py:478
  10.5 0.7 pad_add_fusion.refs_0_
  11.2 0.5 collective-permute-start.69
  11.7 0.1 pad_add_fusion.1
  11.8 1.5 %collective-permute-start.68 = (s32[4,12]{1,0:T(4,128)S(1)}, s32[4,12]{1,0:T(4,128)S(1)}, u32[]{:S(2)}, u32[]{:S(2)}) collective-permute-start(s32[4,12]{1,0:T(4,128)S(1)} %pad_add_fusion.refs_0_), channel_id=1, source_target_pairs={{0,16},{16,0},{1,17},{17,1},{2,18},{18,2},{3,19},{19,3},{4,20},{20... | collective-permute-start | bytes 584 | tf_op jit(solution)/shard_map/ppermute | solution.py:440
  13.3 4.1 %shard_map.75 = bf16[32,16,768]{2,1,0:T(8,128)(2,1)S(1)} custom-call(bf16[512,2048]{1,0:T(8,128)(2,1)S(1)} %get-tuple-element.283.refs_0_, bf16[2048,2048]{1,0:T(8,128)(2,1)} %bitcast.15, bf16[32,16,256]{2,1,0:T(8,128)(2,1)S(1)} %get-tuple-element.284.refs_2_), custom_call_target="tpu_custom_call" | custom-call | flops 1610612736 | bytes 3932160 | tf_op jit(solution)/shard_map/pallas_call | solution.py:25
  17.4 0.0 collective-permute-done.68.refs_1_
  17.4 0.0 copy-done
  17.4 0.8 shard_map.74
  18.8 0.0 collective-permute-done.69
  18.9 56.6 %conditional.1 = (bf16[16,1536]{1,0:T(8,128)(2,1)S(1)}, bf16[12,16,256]{2,1,0:T(8,128)(2,1)S(1)}, bf16[1536,256]{1,0:T(8,128)(2,1)}) conditional(s32[]{:T(128)} %bitcast.4, (s32[16,128]{1,0:T(8,128)S(1)}, bf16[32,16,768]{2,1,0:T(8,128)(2,1)S(1)}, bf16[32,16,256]{2,1,0:T(8,128)(2,1)S(1)}, ...), branch_computations={%region_0.0_spmd, %region_1.0_spmd, %region_2.0_spmd, %region_3.0_... | conditional | flops 9227468800 | bytes 80052768 | solution.py:540
  18.9 0.8 branch_0_fun.14
  19.7 0.1 collective-permute-start.1
  19.8 1.6 %collective-permute-start = (bf16[17,16,768]{2,1,0:T(8,128)(2,1)S(1)}, bf16[17,16,768]{2,1,0:T(8,128)(2,1)S(1)}, u32[]{:S(2)}, u32[]{:S(2)}) collective-permute-start(bf16[17,16,768]{2,1,0:T(8,128)(2,1)S(1)} %get-tuple-element.112), channel_id=1, source_target_pairs={{0,4},{4,0},{8,12},{12,8},{1,5},{5,1},{9,13},{13,9},{2,6},{6,2},{1... | collective-permute-start | bytes 1253384 | tf_op jit(solution)/shard_map/cond/branch_0_fun/ppermute | solution.py:444
  21.4 4.1 %branch_0_fun.15 = (bf16[32,16,768]{2,1,0:T(8,128)(2,1)S(1)}, bf16[17,16,768]{2,1,0:T(8,128)(2,1)S(1)}) custom-call(s32[16,128]{1,0:T(8,128)S(1)} %get-tuple-element.105.tab_ref.refs_0_, bf16[512,2048]{1,0:T(8,128)(2,1)S(1)} %get-tuple-element.107.refs_1_, bf16[2048,2048]{1,0:T(8,128)(2,1)} %get-tuple-element.108.refs_2_), custom_call_target="tpu_custom_call" | custom-call | flops 1610612736 | bytes 3932160 | tf_op jit(solution)/shard_map/cond/branch_0_fun/pallas_call | solution.py:25
  25.4 5.9 %branch_0_fun.16 = (bf16[1536,256]{1,0:T(8,128)(2,1)S(1)}, bf16[1536,256]{1,0:T(8,128)(2,1)S(1)}) custom-call(s32[2]{0:T(128)S(1)} %get-tuple-element.113.order_ref, bf16[1536,2048]{1,0:T(8,128)(2,1)S(1)} %get-tuple-element.106.tokens_ref, bf16[2048,1024]{1,0:T(8,128)(2,1)} %get-tuple-element.114.first_ref.second_ref, ...), custom_call_target="tpu_custom_call" | custom-call | flops 3221225472 | bytes 9961472 | tf_op jit(solution)/shard_map/cond/branch_0_fun/pallas_call | solution.py:360
  31.4 0.0 collective-permute-done.1.refs_3_.refs_6_.refs_5_
  31.4 0.5 collective-permute-done.refs_1_.refs_0_
  31.9 0.8 branch_0_fun.17
  32.7 0.1 collective-permute-start.4
  32.8 0.3 collective-permute-start.2
  33.1 0.2 collective-permute-start.3
  33.3 2.9 %branch_0_fun.18 = (bf16[32,16,512]{2,1,0:T(8,128)(2,1)S(1)}, bf16[17,16,512]{2,1,0:T(8,128)(2,1)S(1)}) custom-call(s32[16,128]{1,0:T(8,128)S(1)} %get-tuple-element.105.tab_ref.refs_0_, bf16[512,2048]{1,0:T(8,128)(2,1)S(1)} %get-tuple-element.107.refs_1_, bf16[2048,2048]{1,0:T(8,128)(2,1)} %get-tuple-element.108.refs_2_, ...), custom_call_target="tpu_custom_call" | custom-call | flops 1073741824 | bytes 2621440 | tf_op jit(solution)/shard_map/cond/branch_0_fun/pallas_call | solution.py:25
  36.1 8.7 %collective-permute-done.2.refs_1_.refs_0_ = bf16[17,16,768]{2,1,0:T(8,128)(2,1)S(1)} collective-permute-done((bf16[17,16,768]{2,1,0:T(8,128)(2,1)S(1)}, bf16[17,16,768]{2,1,0:T(8,128)(2,1)S(1)}, u32[]{:S(2)}, u32[]{:S(2)}) %collective-permute-start.2) | collective-permute-done | bytes 417824 | tf_op jit(solution)/shard_map/cond/branch_0_fun/ppermute | solution.py:444
  44.8 0.0 collective-permute-done.3.refs_4_.refs_1_
  44.8 0.0 collective-permute-done.4.refs_7_.b_ref
  44.8 0.8 %branch_0_fun.19 = (bf16[15,16,768]{2,1,0:T(8,128)(2,1)S(1)}, bf16[20,16,512]{2,1,0:T(8,128)(2,1)S(1)}, bf16[1536,256]{1,0:T(8,128)(2,1)S(1)}) custom-call(s32[16,128]{1,0:T(8,128)S(1)} %get-tuple-element.105.tab_ref.refs_0_, bf16[32,16,768]{2,1,0:T(8,128)(2,1)S(1)} %get-tuple-element.121.refs_0_.refs_2_.own_ref, ...), custom_call_target="tpu_custom_call", output_to_operand_aliasing={{2}: (9, {})} | custom-call | bytes 2088960 | tf_op jit(solution)/shard_map/cond/branch_0_fun/pallas_call | solution.py:25
  45.7 0.2 branch_0_fun.20
  45.9 1.6 %collective-permute-start.7 = (bf16[768,256]{1,0:T(8,128)(2,1)S(1)}, bf16[768,256]{1,0:T(8,128)(2,1)S(1)}, u32[]{:S(2)}, u32[]{:S(2)}) collective-permute-start(bf16[768,256]{1,0:T(8,128)(2,1)S(1)} %get-tuple-element.127), channel_id=1, source_target_pairs={{0,1},{1,0},{2,3},{3,2},{4,5},{5,4},{6,7},{7,6},{8,9},{9,8},{10,11... | collective-permute-start | bytes 1179656 | tf_op jit(solution)/shard_map/cond/branch_0_fun/ppermute | solution.py:440
  47.4 0.0 collective-permute-start.6
  47.4 2.3 %collective-permute-start.5 = (bf16[20,16,512]{2,1,0:T(8,128)(2,1)S(1)}, bf16[20,16,512]{2,1,0:T(8,128)(2,1)S(1)}, u32[]{:S(2)}, u32[]{:S(2)}) collective-permute-start(bf16[20,16,512]{2,1,0:T(8,128)(2,1)S(1)} %get-tuple-element.124), channel_id=1, source_target_pairs={{0,4},{4,0},{8,12},{12,8},{1,5},{5,1},{9,13},{13,9},{2,6},{6,2},{1... | collective-permute-start | bytes 983048 | tf_op jit(solution)/shard_map/cond/branch_0_fun/ppermute | solution.py:444
  49.7 5.9 %branch_0_fun.21 = (bf16[1536,256]{1,0:T(8,128)(2,1)S(1)}, bf16[1536,256]{1,0:T(8,128)(2,1)S(1)}) custom-call(s32[2]{0:T(128)S(1)} %get-tuple-element.128.order_ref, bf16[1536,2048]{1,0:T(8,128)(2,1)S(1)} %get-tuple-element.106.tokens_ref, bf16[2048,1024]{1,0:T(8,128)(2,1)} %get-tuple-element.114.first_ref.second_ref, ...), custom_call_target="tpu_custom_call" | custom-call | flops 3221225472 | bytes 9961472 | tf_op jit(solution)/shard_map/cond/branch_0_fun/pallas_call | solution.py:360
  55.6 1.9 %collective-permute-done.5.refs_1_.refs_5_.refs_2_.refs_6_.refs_0_ = bf16[20,16,512]{2,1,0:T(8,128)(2,1)S(1)} collective-permute-done((bf16[20,16,512]{2,1,0:T(8,128)(2,1)S(1)}, bf16[20,16,512]{2,1,0:T(8,128)(2,1)S(1)}, u32[]{:S(2)}, u32[]{:S(2)}) %collective-permute-start.5) | collective-permute-done | bytes 327712 | tf_op jit(solution)/shard_map/cond/branch_0_fun/ppermute | solution.py:444
  57.5 0.0 collective-permute-done.6.refs_3_.refs_1_
  57.5 0.0 collective-permute-done.7.refs_4_.refs_0_
  57.5 0.9 %branch_0_fun.22 = (bf16[15,16,512]{2,1,0:T(8,128)(2,1)S(1)}, bf16[10,16,768]{2,1,0:T(8,128)(2,1)S(1)}, bf16[1536,256]{1,0:T(8,128)(2,1)S(1)}, bf16[768,256]{1,0:T(8,128)(2,1)S(1)}) custom-call(s32[16,128]{1,0:T(8,128)S(1)} %get-tuple-element.105.tab_ref.refs_0_, ...), custom_call_target="tpu_custom_call", output_to_operand_aliasing={{2}: (8, {}), {3}: (9, {})} | custom-call | bytes 1474560 | tf_op jit(solution)/shard_map/cond/branch_0_fun/pallas_call | solution.py:25
  58.4 0.1 collective-permute-start.9
  58.5 0.5 collective-permute-start.8
  59.0 0.5 collective-permute-start.12
  59.6 1.3 %collective-permute-start.11 = (bf16[10,16,768]{2,1,0:T(8,128)(2,1)S(1)}, bf16[10,16,768]{2,1,0:T(8,128)(2,1)S(1)}, u32[]{:S(2)}, u32[]{:S(2)}) collective-permute-start(bf16[10,16,768]{2,1,0:T(8,128)(2,1)S(1)} %get-tuple-element.135), channel_id=1, source_target_pairs={{4,0},{8,12},{5,1},{9,13},{6,2},{10,14},{7,3},{11,15},{20,16},{24,... | collective-permute-start | bytes 737288 | tf_op jit(solution)/shard_map/cond/branch_0_fun/ppermute | solution.py:452
  60.8 1.6 %branch_0_fun.23 = (f32[16,1536]{1,0:T(8,128)S(1)}, bf16[12,16,256]{2,1,0:T(8,128)(2,1)S(1)}) custom-call(s32[16,128]{1,0:T(8,128)S(1)} %get-tuple-element.105.tab_ref.refs_0_, bf16[1536,2048]{1,0:T(8,128)(2,1)S(1)} %get-tuple-element.106.tokens_ref, bf16[32,16,768]{2,1,0:T(8,128)(2,1)S(1)} %get-tuple-element.109.refs_0_.refs_3_.own_ref, ...), custom_call_target="tpu_custom_call" | custom-call | flops 37748736 | bytes 3932160 | tf_op jit(solution)/shard_map/cond/branch_0_fun/pallas_call | solution.py:25
  62.5 0.0 collective-permute-done.8.refs_1_
  62.5 0.0 collective-permute-done.9.refs_3_.b_ref
  62.5 0.7 branch_0_fun.24.refs_4_
  63.3 1.3 %collective-permute-start.10 = (bf16[10,16,512]{2,1,0:T(8,128)(2,1)S(1)}, bf16[10,16,512]{2,1,0:T(8,128)(2,1)S(1)}, u32[]{:S(2)}, u32[]{:S(2)}) collective-permute-start(bf16[10,16,512]{2,1,0:T(8,128)(2,1)S(1)} %branch_0_fun.24.refs_4_), channel_id=1, source_target_pairs={{4,0},{8,12},{5,1},{9,13},{6,2},{10,14},{7,3},{11,15},{20,16},{24,... | collective-permute-start | bytes 491528 | tf_op jit(solution)/shard_map/cond/branch_0_fun/ppermute | solution.py:452
  64.6 4.5 %collective-permute-done.11.refs_2_ = bf16[10,16,768]{2,1,0:T(8,128)(2,1)S(1)} collective-permute-done((bf16[10,16,768]{2,1,0:T(8,128)(2,1)S(1)}, bf16[10,16,768]{2,1,0:T(8,128)(2,1)S(1)}, u32[]{:S(2)}, u32[]{:S(2)}) %collective-permute-start.11) | collective-permute-done | bytes 245792 | tf_op jit(solution)/shard_map/cond/branch_0_fun/ppermute | solution.py:452
  69.1 1.6 %branch_0_fun.25.refs_2_.refs_3_ = f32[16,1536]{1,0:T(8,128)S(1)} custom-call(s32[16,128]{1,0:T(8,128)S(1)} %get-tuple-element.105.tab_ref.refs_0_, bf16[1536,2048]{1,0:T(8,128)(2,1)S(1)} %get-tuple-element.106.tokens_ref, bf16[32,16,768]{2,1,0:T(8,128)(2,1)S(1)} %get-tuple-element.121.refs_0_.refs_2_.own_ref, ...), custom_call_target="tpu_custom_call" | custom-call | flops 37748736 | bytes 3932160 | tf_op jit(solution)/shard_map/cond/branch_0_fun/pallas_call | solution.py:25
  70.7 0.0 collective-permute-done.12.refs_1_
  70.7 1.2 %branch_0_fun.26.refs_4_ = bf16[1536,256]{1,0:T(8,128)(2,1)} custom-call(bf16[1536,256]{1,0:T(8,128)(2,1)S(1)} %get-tuple-element.129.refs_6_.a_ref, bf16[1536,256]{1,0:T(8,128)(2,1)S(1)} %collective-permute-done.9.refs_3_.b_ref, bf16[768,256]{1,0:T(8,128)(2,1)S(1)} %collective-permute-done.7.refs_4_.refs_0_, ...), custom_call_target="tpu_custom_call" | custom-call | bytes 3145728 | tf_op jit(solution)/shard_map/cond/branch_0_fun/pallas_call | solution.py:25
  71.9 1.7 %collective-permute-done.10.refs_2_ = bf16[10,16,512]{2,1,0:T(8,128)(2,1)S(1)} collective-permute-done((bf16[10,16,512]{2,1,0:T(8,128)(2,1)S(1)}, bf16[10,16,512]{2,1,0:T(8,128)(2,1)S(1)}, u32[]{:S(2)}, u32[]{:S(2)}) %collective-permute-start.10) | collective-permute-done | bytes 163872 | tf_op jit(solution)/shard_map/cond/branch_0_fun/ppermute | solution.py:452
  73.6 1.4 %branch_0_fun.27 = bf16[16,1536]{1,0:T(8,128)(2,1)S(1)} custom-call(s32[16,128]{1,0:T(8,128)S(1)} %get-tuple-element.105.tab_ref.refs_0_, bf16[1536,2048]{1,0:T(8,128)(2,1)S(1)} %get-tuple-element.106.tokens_ref, bf16[32,16,512]{2,1,0:T(8,128)(2,1)S(1)} %get-tuple-element.120.refs_0_.own_ref, ...), custom_call_target="tpu_custom_call" | custom-call | flops 25165824 | bytes 2621440 | tf_op jit(solution)/shard_map/cond/branch_0_fun/pallas_call | solution.py:25
  75.5 0.1 collective-permute-start.72
  75.6 0.7 collective-permute-start.71
  76.3 1.1 %collective-permute-start.70 = (bf16[16,1536]{1,0:T(8,128)(2,1)S(1)}, bf16[16,1536]{1,0:T(8,128)(2,1)S(1)}, u32[]{:S(2)}, u32[]{:S(2)}) collective-permute-start(bf16[16,1536]{1,0:T(8,128)(2,1)S(1)} %get-tuple-element.286.refs_0_), channel_id=1, source_target_pairs={{0,2},{2,0},{1,3},{3,1},{4,6},{6,4},{5,7},{7,5},{8,10},{10,8},{9,1... | collective-permute-start | bytes 147464 | tf_op jit(solution)/shard_map/ppermute | solution.py:440
  77.4 1.7 %collective-permute-done.72.refs_3_ = bf16[16,1536]{1,0:T(8,128)(2,1)S(1)} collective-permute-done((bf16[16,1536]{1,0:T(8,128)(2,1)S(1)}, bf16[16,1536]{1,0:T(8,128)(2,1)S(1)}, u32[]{:S(2)}, u32[]{:S(2)}) %collective-permute-start.72) | collective-permute-done | bytes 49184 | tf_op jit(solution)/shard_map/ppermute | solution.py:542
  79.1 1.1 %collective-permute-done.71.refs_2_ = bf16[16,1536]{1,0:T(8,128)(2,1)S(1)} collective-permute-done((bf16[16,1536]{1,0:T(8,128)(2,1)S(1)}, bf16[16,1536]{1,0:T(8,128)(2,1)S(1)}, u32[]{:S(2)}, u32[]{:S(2)}) %collective-permute-start.71) | collective-permute-done | bytes 49184 | tf_op jit(solution)/shard_map/ppermute | solution.py:440
  80.1 0.0 collective-permute-done.70.refs_1_
  80.1 2.4 %shard_map.76 = bf16[1536,256]{1,0:T(8,128)(2,1)} custom-call(s32[16,128]{1,0:T(8,128)S(1)} %get-tuple-element.281.tab_ref, bf16[12,16,256]{2,1,0:T(8,128)(2,1)S(1)} %get-tuple-element.285.up_ref, bf16[16,1536]{1,0:T(8,128)(2,1)S(1)} %get-tuple-element.286.refs_0_, bf16[16,1536]{1,0:T(8,128)(2,1)S(1)} %collective-permute-done.70.refs_1_, ...), custom_call_target="tpu_custom_call" | custom-call | flops 12582912 | bytes 1572864 | tf_op jit(solution)/shard_map/pallas_call | solution.py:25
  (6 shorter events, 0.0 us)
Async XLA Ops:
  0.0 8.6 %collective-permute-start.67 = (s32[1,12]{1,0:T(1,128)}, s32[1,12]{1,0:T(1,128)S(1)}, u32[]{:S(2)}, u32[]{:S(2)}) collective-permute-start(s32[1,12]{1,0:T(1,128)} %bitcast.21), channel_id=1, source_target_pairs={{0,12},{4,0},{8,4},{12,8},{1,13},{5,1},{9,5},{13,9},{2,14},{6,2},{... | collective-permute-start | bytes 152 | tf_op jit(solution)/shard_map/ppermute | solution.py:478
  5.0 4.6 %collective-permute-start.66 = (s32[1,12]{1,0:T(1,128)}, s32[1,12]{1,0:T(1,128)S(1)}, u32[]{:S(2)}, u32[]{:S(2)}) collective-permute-start(s32[1,12]{1,0:T(1,128)} %bitcast.22), channel_id=1, source_target_pairs={{0,8},{4,12},{8,0},{12,4},{1,9},{5,13},{9,1},{13,5},{2,10},{6,14},... | collective-permute-start | bytes 152 | tf_op jit(solution)/shard_map/ppermute | solution.py:478
  5.1 5.5 %collective-permute-start.65 = (s32[1,12]{1,0:T(1,128)}, s32[1,12]{1,0:T(1,128)S(1)}, u32[]{:S(2)}, u32[]{:S(2)}) collective-permute-start(s32[1,12]{1,0:T(1,128)} %bitcast.23), channel_id=1, source_target_pairs={{0,4},{4,8},{8,12},{12,0},{1,5},{5,9},{9,13},{13,1},{2,6},{6,10},{... | collective-permute-start | bytes 152 | tf_op jit(solution)/shard_map/ppermute | solution.py:478
  6.1 11.3 %copy-start = (s32[12]{0:T(128)S(1)}, s32[12]{0:T(128)}, u32[]{:S(2)}) copy-start(s32[12]{0:T(128)} %param.18) | copy-start | bytes 148
  6.1 12.8 %slice-start = ((s8[6291456]{0:T(1024)(128)(4,1)}), s8[4194304]{0:T(1024)(128)(4,1)S(1)}, s32[]{:S(2)}) async-start(s8[6291456]{0:T(1024)(128)(4,1)} %bitcast.13), calls=%async_computation | async-start | bytes 8388608
  11.2 7.7 %collective-permute-start.69 = (bf16[32,16,256]{2,1,0:T(8,128)(2,1)S(1)}, bf16[32,16,256]{2,1,0:T(8,128)(2,1)S(1)}, u32[]{:S(2)}, u32[]{:S(2)}) collective-permute-start(bf16[32,16,256]{2,1,0:T(8,128)(2,1)S(1)} %get-tuple-element.284.refs_2_), channel_id=1, source_target_pairs={{0,4},{4,0},{8,12},{12,8},{1,5},{5,1},{9,13},{13,9},{2,6},{6,2},{1... | collective-permute-start | bytes 786440 | tf_op jit(solution)/shard_map/ppermute | solution.py:444
  11.8 5.6 %collective-permute-start.68 = (s32[4,12]{1,0:T(4,128)S(1)}, s32[4,12]{1,0:T(4,128)S(1)}, u32[]{:S(2)}, u32[]{:S(2)}) collective-permute-start(s32[4,12]{1,0:T(4,128)S(1)} %pad_add_fusion.refs_0_), channel_id=1, source_target_pairs={{0,16},{16,0},{1,17},{17,1},{2,18},{18,2},{3,19},{19,3},{4,20},{20... | collective-permute-start | bytes 584 | tf_op jit(solution)/shard_map/ppermute | solution.py:440
  13.3 5.5 %slice-start.1 = ((s8[6291456]{0:T(1024)(128)(4,1)}), s8[2097152]{0:T(1024)(128)(4,1)S(1)}, s32[]{:S(2)}) async-start(s8[6291456]{0:T(1024)(128)(4,1)} %bitcast.13), calls=%async_computation.1 | async-start | bytes 4194304
  19.7 11.7 %collective-permute-start.1 = (bf16[15,16,256]{2,1,0:T(8,128)(2,1)S(1)}, bf16[15,16,256]{2,1,0:T(8,128)(2,1)S(1)}, u32[]{:S(2)}, u32[]{:S(2)}) collective-permute-start(bf16[15,16,256]{2,1,0:T(8,128)(2,1)S(1)} %get-tuple-element.117), channel_id=1, source_target_pairs={{4,8},{6,10},{0,2},{12,14},{8,4},{10,6},{2,0},{14,12},{5,9},{7,11}... | collective-permute-start | bytes 368648 | tf_op jit(solution)/shard_map/cond/branch_0_fun/ppermute | solution.py:457
  19.8 12.1 %collective-permute-start = (bf16[17,16,768]{2,1,0:T(8,128)(2,1)S(1)}, bf16[17,16,768]{2,1,0:T(8,128)(2,1)S(1)}, u32[]{:S(2)}, u32[]{:S(2)}) collective-permute-start(bf16[17,16,768]{2,1,0:T(8,128)(2,1)S(1)} %get-tuple-element.112), channel_id=1, source_target_pairs={{0,4},{4,0},{8,12},{12,8},{1,5},{5,1},{9,13},{13,9},{2,6},{6,2},{1... | collective-permute-start | bytes 1253384 | tf_op jit(solution)/shard_map/cond/branch_0_fun/ppermute | solution.py:444
  32.7 12.1 %collective-permute-start.4 = (bf16[1536,256]{1,0:T(8,128)(2,1)S(1)}, bf16[1536,256]{1,0:T(8,128)(2,1)S(1)}, u32[]{:S(2)}, u32[]{:S(2)}) collective-permute-start(bf16[1536,256]{1,0:T(8,128)(2,1)S(1)} %get-tuple-element.123), channel_id=1, source_target_pairs={{0,2},{2,0},{1,3},{3,1},{4,6},{6,4},{5,7},{7,5},{8,10},{10,8},{9,1... | collective-permute-start | bytes 2359304 | tf_op jit(solution)/shard_map/cond/branch_0_fun/ppermute | solution.py:440
  32.8 12.1 %collective-permute-start.2 = (bf16[17,16,768]{2,1,0:T(8,128)(2,1)S(1)}, bf16[17,16,768]{2,1,0:T(8,128)(2,1)S(1)}, u32[]{:S(2)}, u32[]{:S(2)}) collective-permute-start(bf16[17,16,768]{2,1,0:T(8,128)(2,1)S(1)} %get-tuple-element.115.refs_0_), channel_id=1, source_target_pairs={{0,4},{4,0},{8,12},{12,8},{1,5},{5,1},{9,13},{13,9},{2,6},{6,2},{1... | collective-permute-start | bytes 1253384 | tf_op jit(solution)/shard_map/cond/branch_0_fun/ppermute | solution.py:444
  33.1 11.7 %collective-permute-start.3 = (bf16[15,16,768]{2,1,0:T(8,128)(2,1)S(1)}, bf16[15,16,768]{2,1,0:T(8,128)(2,1)S(1)}, u32[]{:S(2)}, u32[]{:S(2)}) collective-permute-start(bf16[15,16,768]{2,1,0:T(8,128)(2,1)S(1)} %get-tuple-element.119.refs_3_), channel_id=1, source_target_pairs={{4,8},{6,10},{0,2},{12,14},{8,4},{10,6},{2,0},{14,12},{5,9},{7,11}... | collective-permute-start | bytes 1105928 | tf_op jit(solution)/shard_map/cond/branch_0_fun/ppermute | solution.py:457
  45.9 11.7 %collective-permute-start.7 = (bf16[768,256]{1,0:T(8,128)(2,1)S(1)}, bf16[768,256]{1,0:T(8,128)(2,1)S(1)}, u32[]{:S(2)}, u32[]{:S(2)}) collective-permute-start(bf16[768,256]{1,0:T(8,128)(2,1)S(1)} %get-tuple-element.127), channel_id=1, source_target_pairs={{0,1},{1,0},{2,3},{3,2},{4,5},{5,4},{6,7},{7,6},{8,9},{9,8},{10,11... | collective-permute-start | bytes 1179656 | tf_op jit(solution)/shard_map/cond/branch_0_fun/ppermute | solution.py:440
  47.4 10.1 %collective-permute-start.6 = (bf16[15,16,768]{2,1,0:T(8,128)(2,1)S(1)}, bf16[15,16,768]{2,1,0:T(8,128)(2,1)S(1)}, u32[]{:S(2)}, u32[]{:S(2)}) collective-permute-start(bf16[15,16,768]{2,1,0:T(8,128)(2,1)S(1)} %get-tuple-element.125), channel_id=1, source_target_pairs={{4,8},{6,10},{0,2},{12,14},{8,4},{10,6},{2,0},{14,12},{5,9},{7,11}... | collective-permute-start | bytes 1105928 | tf_op jit(solution)/shard_map/cond/branch_0_fun/ppermute | solution.py:457
  47.4 10.1 %collective-permute-start.5 = (bf16[20,16,512]{2,1,0:T(8,128)(2,1)S(1)}, bf16[20,16,512]{2,1,0:T(8,128)(2,1)S(1)}, u32[]{:S(2)}, u32[]{:S(2)}) collective-permute-start(bf16[20,16,512]{2,1,0:T(8,128)(2,1)S(1)} %get-tuple-element.124), channel_id=1, source_target_pairs={{0,4},{4,0},{8,12},{12,8},{1,5},{5,1},{9,13},{13,9},{2,6},{6,2},{1... | collective-permute-start | bytes 983048 | tf_op jit(solution)/shard_map/cond/branch_0_fun/ppermute | solution.py:444
  58.4 4.1 %collective-permute-start.9 = (bf16[1536,256]{1,0:T(8,128)(2,1)S(1)}, bf16[1536,256]{1,0:T(8,128)(2,1)S(1)}, u32[]{:S(2)}, u32[]{:S(2)}) collective-permute-start(bf16[1536,256]{1,0:T(8,128)(2,1)S(1)} %get-tuple-element.134), channel_id=1, source_target_pairs={{0,2},{2,0},{1,3},{3,1},{4,6},{6,4},{5,7},{7,5},{8,10},{10,8},{9,1... | collective-permute-start | bytes 2359304 | tf_op jit(solution)/shard_map/cond/branch_0_fun/ppermute | solution.py:440
  58.5 4.0 %collective-permute-start.8 = (bf16[15,16,512]{2,1,0:T(8,128)(2,1)S(1)}, bf16[15,16,512]{2,1,0:T(8,128)(2,1)S(1)}, u32[]{:S(2)}, u32[]{:S(2)}) collective-permute-start(bf16[15,16,512]{2,1,0:T(8,128)(2,1)S(1)} %get-tuple-element.132.refs_7_), channel_id=1, source_target_pairs={{4,8},{6,10},{0,2},{12,14},{8,4},{10,6},{2,0},{14,12},{5,9},{7,11}... | collective-permute-start | bytes 737288 | tf_op jit(solution)/shard_map/cond/branch_0_fun/ppermute | solution.py:457
  59.0 11.7 %collective-permute-start.12 = (bf16[768,256]{1,0:T(8,128)(2,1)S(1)}, bf16[768,256]{1,0:T(8,128)(2,1)S(1)}, u32[]{:S(2)}, u32[]{:S(2)}) collective-permute-start(bf16[768,256]{1,0:T(8,128)(2,1)S(1)} %get-tuple-element.136), channel_id=1, source_target_pairs={{0,1},{1,0},{2,3},{3,2},{4,5},{5,4},{6,7},{7,6},{8,9},{9,8},{10,11... | collective-permute-start | bytes 1179656 | tf_op jit(solution)/shard_map/cond/branch_0_fun/ppermute | solution.py:440
  59.6 9.5 %collective-permute-start.11 = (bf16[10,16,768]{2,1,0:T(8,128)(2,1)S(1)}, bf16[10,16,768]{2,1,0:T(8,128)(2,1)S(1)}, u32[]{:S(2)}, u32[]{:S(2)}) collective-permute-start(bf16[10,16,768]{2,1,0:T(8,128)(2,1)S(1)} %get-tuple-element.135), channel_id=1, source_target_pairs={{4,0},{8,12},{5,1},{9,13},{6,2},{10,14},{7,3},{11,15},{20,16},{24,... | collective-permute-start | bytes 737288 | tf_op jit(solution)/shard_map/cond/branch_0_fun/ppermute | solution.py:452
  63.3 10.3 %collective-permute-start.10 = (bf16[10,16,512]{2,1,0:T(8,128)(2,1)S(1)}, bf16[10,16,512]{2,1,0:T(8,128)(2,1)S(1)}, u32[]{:S(2)}, u32[]{:S(2)}) collective-permute-start(bf16[10,16,512]{2,1,0:T(8,128)(2,1)S(1)} %branch_0_fun.24.refs_4_), channel_id=1, source_target_pairs={{4,0},{8,12},{5,1},{9,13},{6,2},{10,14},{7,3},{11,15},{20,16},{24,... | collective-permute-start | bytes 491528 | tf_op jit(solution)/shard_map/cond/branch_0_fun/ppermute | solution.py:452
  75.5 3.6 %collective-permute-start.72 = (bf16[16,1536]{1,0:T(8,128)(2,1)S(1)}, bf16[16,1536]{1,0:T(8,128)(2,1)S(1)}, u32[]{:S(2)}, u32[]{:S(2)}) collective-permute-start(bf16[16,1536]{1,0:T(8,128)(2,1)S(1)} %get-tuple-element.286.refs_0_), channel_id=1, source_target_pairs={{0,3},{1,2},{2,1},{3,0},{4,7},{5,6},{6,5},{7,4},{8,11},{9,10},{10,... | collective-permute-start | bytes 147464 | tf_op jit(solution)/shard_map/ppermute | solution.py:542
  75.6 4.6 %collective-permute-start.71 = (bf16[16,1536]{1,0:T(8,128)(2,1)S(1)}, bf16[16,1536]{1,0:T(8,128)(2,1)S(1)}, u32[]{:S(2)}, u32[]{:S(2)}) collective-permute-start(bf16[16,1536]{1,0:T(8,128)(2,1)S(1)} %get-tuple-element.286.refs_0_), channel_id=1, source_target_pairs={{0,1},{1,0},{2,3},{3,2},{4,5},{5,4},{6,7},{7,6},{8,9},{9,8},{10,11... | collective-permute-start | bytes 147464 | tf_op jit(solution)/shard_map/ppermute | solution.py:440
  76.3 3.9 %collective-permute-start.70 = (bf16[16,1536]{1,0:T(8,128)(2,1)S(1)}, bf16[16,1536]{1,0:T(8,128)(2,1)S(1)}, u32[]{:S(2)}, u32[]{:S(2)}) collective-permute-start(bf16[16,1536]{1,0:T(8,128)(2,1)S(1)} %get-tuple-element.286.refs_0_), channel_id=1, source_target_pairs={{0,2},{2,0},{1,3},{3,1},{4,6},{6,4},{5,7},{7,5},{8,10},{10,8},{9,1... | collective-permute-start | bytes 147464 | tf_op jit(solution)/shard_map/ppermute | solution.py:440

commit v4 on v3

--- a/solution.py
+++ b/solution.py
@@ -12,6 +12,7 @@
 LANES = 128
 LARGE = 1 << 21
 PER = 6
+EARLY = 0
 SHARE = 1.0
 VMEM = pl.BlockSpec(memory_space=pltpu.VMEM)
 SMEM = pl.BlockSpec(memory_space=pltpu.SMEM)
@@ -129,7 +130,7 @@
     wide = lax.broadcasted_iota(I32, (tenants, LANES), 1)
     tenant = lax.broadcasted_iota(I32, (tenants, LANES), 0)
     one = lax.broadcasted_iota(I32, (tenants, blocks), 0)
-    zs = [lax.rem(me - k + n, n) for k in range(n)]
+    zs = [me ^ k for k in range(n)]
     groups = len(arrays)
     present = [
         [
@@ -354,21 +355,22 @@
         out_ref[...] = jnp.dot(tokens_ref[...], weight_ref[...], preferred_element_type=F32).astype(BF16)
 
 
-def base_product(order, tokens, weight, out, after, strips=3):
-    rows, width = tokens.shape
+def base_product(order, tokens, weight, out, after, first, last):
+    strip, width = tokens.shape[0] // 3, tokens.shape[1]
+    rows = (last - first) * strip
     flops, nbytes = 4 * rows * width * out, 2 * (rows * (width + 2 * out) + 2 * width * out)
     return pl.pallas_call(
         base_kernel,
         grid_spec=pltpu.PrefetchScalarGridSpec(
             num_scalar_prefetch=1,
-            grid=(strips,),
+            grid=(last - first,),
             in_specs=[
-                pl.BlockSpec((rows // strips, width), lambda m, order: (m, 0)),
+                pl.BlockSpec((strip, width), lambda m, order: (first + m, 0)),
                 pl.BlockSpec((width, out), lambda m, order: (0, order[0])),
                 pl.BlockSpec((width, out), lambda m, order: (0, order[1])),
             ]
             + [ANY] * len(after),
-            out_specs=[pl.BlockSpec((rows // strips, out), lambda m, order: (m, 0))] * 2,
+            out_specs=[pl.BlockSpec((strip, out), lambda m, order: (m, 0))] * 2,
         ),
         out_shape=[shape(rows, out)] * 2,
         compiler_params=pltpu.CompilerParams(vmem_limit_bytes=24 * MIB),
@@ -376,29 +378,26 @@
     )(order, tokens, placed(weight), placed(weight), *after)
 
 
-def near_kernel(ins, a_ref, b_ref, *outs):
-    rows = outs[0].shape[0]
-    for i, out_ref in enumerate(outs):
-        at = slice(i * rows, (i + 1) * rows)
-        out_ref[...] = (a_ref[at, :].astype(F32) + b_ref[at, :].astype(F32)).astype(BF16)
-
-
-def add_halves(a, b):
-    rows, width = a.shape
-    return call(near_kernel, [a, b], [VMEM] * 2, [shape(rows // 2, width)] * 2, [VMEM] * 2, nbytes=6 * rows * width)
-
-
-def gather_kernel(ins, a_ref, b_ref, *refs):
-    rows = refs[0].shape[0]
-    for i, part_ref in enumerate(refs[: ins - 2]):
-        at = slice(i * rows, (i + 1) * rows)
-        total = a_ref[at, :].astype(F32) + b_ref[at, :].astype(F32) + part_ref[...].astype(F32)
-        refs[-1][at, :] = total.astype(BF16)
-
-
-def gather_base(a, b, halves, after):
+def rows_kernel(pieces, ins, *refs):
+    at = 0
+    for length, terms in pieces:
+        total = 0.0
+        for which, start in terms:
+            total = total + refs[which][start : start + length, :].astype(F32)
+        refs[-1][at : at + length, :] = total.astype(BF16)
+        at += length
+
+
+def add_rows(arrays, pieces, after=()):
+    rows, width = sum(length for length, _ in pieces), arrays[0].shape[1]
     return call(
-        gather_kernel, [a, b, *halves], [VMEM] * 4, shape(*a.shape), VMEM, after=after, nbytes=8 * a.size
+        functools.partial(rows_kernel, pieces),
+        list(arrays),
+        [VMEM] * len(arrays),
+        shape(rows, width),
+        VMEM,
+        after=after,
+        nbytes=8 * rows * width,
     )
 
 
@@ -475,7 +474,7 @@
     own_t = block_tenant.reshape(1, blocks)
     seen = jnp.concatenate(
         [own_t]
-        + [lax.ppermute(own_t, "skill", [(j, (j + k) % n) for j in range(n)]) for k in range(1, n)],
+        + [lax.ppermute(own_t, "skill", [(j, j ^ k) for j in range(n)]) for k in range(1, n)],
         axis=0,
     )
     library = jnp.transpose(skill_down, (0, 2, 1)).reshape(local_skills * rank, width)
@@ -502,38 +501,50 @@
         own, message = compose(kron, library, rank, parts[1], tile, sizes[0], tab)
         owns.append(own)
         arrived[1].append(ends(message))
-        away, keep = base_product(order_cross, tokens, base_weight, out, [message])
+        cut = rows // 3
+        away, keep = base_product(order_cross, tokens, base_weight, out, [message], 0, 1)
 
         to_1, away = step(n, tab, [job(1, 0)], [keep, up_came[1]], [away])
         arrived[0].append(middle(to_1))
-        from_core = swap(away, "tensor")
+        core = swap(away, "tensor")
         own, message = compose(kron, library, rank, parts[2], tile, sizes[0], tab, [to_1])
         owns.append(own)
-
-        first_and_up = 2, ((max(sizes[2], (sizes[0] + 1) // 2)), message), [(owns[0], arrived[0][1], False), (own_up, up_came[1], False)]
-        to_1, to_2, keep = step(n, tab, [job(1, 1), first_and_up], [from_core], [keep])
+        away_2, keep_2 = base_product(order_cross, tokens, base_weight, out, [own], 1, 3)
+        if EARLY:
+            stay, stay_keep = base_product(order_stay, tokens, base_weight, out, [keep_2], 0, 3)
+
+        first_and_up = 2, (max(sizes[2], (sizes[0] + 1) // 2), message), [
+            (owns[0], arrived[0][1], False),
+            (own_up, up_came[1], False),
+        ]
+        to_1, to_2, away_2 = step(n, tab, [job(1, 1), first_and_up], [core, keep_2] + ([stay] if EARLY else []), [away_2])
         arrived[1].append(middle(to_1))
         exchanged = ends(to_2)
         arrived[0].append(exchanged)
         arrived[2].append(exchanged)
         up_came.append(exchanged)
-        near = add_halves(keep, from_core)
-        across = [swap(near[0], "dp")]
-        away, keep = base_product(order_stay, tokens, base_weight, out, [owns[2]])
-
-        to_1, to_2, away, near_2 = step(
-            n, tab, [job(1, 2), job(2, 1)], [across[0], arrived[0][2], keep], [away, near[1]]
-        )
+        core_2 = swap(away_2, "tensor")
+        near = add_rows([keep, core], [(cut, [(0, 0), (1, 0)])], [to_1])
+        across = swap(near, "dp")
+        if not EARLY:
+            stay, stay_keep = base_product(order_stay, tokens, base_weight, out, [near], 0, 3)
+        near_2 = add_rows([keep_2, core_2], [(rows - cut, [(0, 0), (1, 0)])])
+
+        to_1, to_2, stay, near_2 = step(n, tab, [job(1, 2), job(2, 1)], [across, stay_keep], [stay, near_2])
         arrived[2].append(middle(to_1))
         arrived[1].append(outward(to_2))
-        across.append(swap(near_2, "dp"))
-        from_core = swap(away, "tensor")
+        across_2 = swap(near_2, "dp")
+        core = swap(stay, "tensor")
         low, up = project(n, tab, tokens, owns[0], parts[0], arrived[0], None, False, (own_up, up_came), [to_1])
 
-        (to_2,) = step(n, tab, [job(2, 2)], [low, from_core])
+        (to_2,) = step(n, tab, [job(2, 2)], [low, core])
         arrived[2].append(outward(to_2))
         (low,) = project(n, tab, tokens, owns[1], parts[1], arrived[1], low, False, None, [to_2])
-        base = gather_base(keep, from_core, across, [low])
+        base = add_rows(
+            [stay_keep, core, across, across_2],
+            [(cut, [(0, 0), (1, 0), (2, 0)]), (rows - cut, [(0, cut), (1, cut), (3, 0)])],
+            [low],
+        )
         (low,) = project(n, tab, tokens, owns[2], parts[2], arrived[2], low, True, None, [base])
         return low, up, base
 

time: 84.1 us -> 83.5 us (level)
  waiting for transfers between devices: 22 us -> 14.1 us
  starting transfers between devices: 19.7 us -> 24.9 us
  Pallas kernels: 38.6 us -> 40.7 us
    ppermute x4, waiting for transfers between devices: 11.1 us -> 0.54 us  [ends(): return lax.ppermute(x, 'skill', [(0, 1), (1, 0), (2, 3), (3, 2)])]
    ppermute x4, starting transfers between devices: 4.69 us -> 8.81 us  [ends(): return lax.ppermute(x, 'skill', [(0, 1), (1, 0), (2, 3), (3, 2)])]
    ppermute x2, waiting for transfers between devices: 6.17 us -> 8.83 us  [outward(): return lax.ppermute(x, 'skill', [(1, 0), (2, 3)])]
    pallas_call x2 -> x3, Pallas kernels: 11.8 us -> 13.9 us  [base_product(): pl.pallas_call(base_kernel, grid_spec=pltpu.PrefetchScalarGridSpec(num_sc...]
    ppermute x7 -> x8, starting transfers between devices: 5.61 us -> 7.19 us  [swap(): return lax.ppermute(x, axis, [(0, 1), (1, 0)])]
    pallas_call x16 -> x17, Pallas kernels: 26.8 us -> 26.8 us  [call(): pl.pallas_call(functools.partial(kernel, len(ins)), in_specs=specs + [ANY...]
  transfers between devices with their start and end apart: 21 -> 22, of which waited for: 9 -> 7; matrix products, arithmetic and copies ran while one was open for 0% -> 0% of each run, Pallas kernels for 38% -> 42%
where the time goes in v4:
time: 83.5 us; the launch traced here: 82.1 us
  Pallas kernels  40.7 us (49%)
  starting transfers between devices  24.9 us (30%)
  waiting for transfers between devices  14.1 us (17%)
  loops' own time  0.88 us (1%)
    pallas_call x17, Pallas kernels, call(): pl.pallas_call(functools.partial(kernel, len(ins)), in_specs=specs + [ANY...  26.8 us
    pallas_call x3, Pallas kernels, base_product(): pl.pallas_call(base_kernel, grid_spec=pltpu.PrefetchScalarGridSpec(num_sc...  13.9 us
    ppermute x2, waiting for transfers between devices, outward(): return lax.ppermute(x, 'skill', [(1, 0), (2, 3)])  8.83 us
    ppermute x4, starting transfers between devices, ends(): return lax.ppermute(x, 'skill', [(0, 1), (1, 0), (2, 3), (3, 2)])  8.81 us
    ppermute x8, starting transfers between devices, swap(): return lax.ppermute(x, axis, [(0, 1), (1, 0)])  7.19 us
    ppermute x3, starting transfers between devices, line_body(): lax.ppermute(own_t, 'skill', [(j, j ^ k) for j in range(n)])  5.62 us
    ppermute x2, starting transfers between devices, outward(): return lax.ppermute(x, 'skill', [(1, 0), (2, 3)])  2.57 us
  transfers between devices with their start and end apart: 22, of which 7 were waited for; matrix products, arithmetic and copies ran while one was open for 0% of the time, Pallas kernels for 42%

profile of v4, /device:TPU:0, one launch (start us, length us, event | category | flops | bytes accessed | tf_op | source)
XLA Modules:
  0.0 82.1 jit_solution(6121725933236239055)
XLA Ops:
  0.0 5.0 %collective-permute-start.72 = (s32[1,12]{1,0:T(1,128)}, s32[1,12]{1,0:T(1,128)S(1)}, u32[]{:S(2)}, u32[]{:S(2)}) collective-permute-start(s32[1,12]{1,0:T(1,128)} %bitcast.21), channel_id=1, source_target_pairs={{0,12},{4,8},{8,4},{12,0},{1,13},{5,9},{9,5},{13,1},{2,14},{6,10},... | collective-permute-start | bytes 152 | tf_op jit(solution)/shard_map/ppermute | solution.py:477
  5.0 0.0 collective-permute-start.71
  5.1 0.6 collective-permute-start.70
  5.6 2.5 %shard_map.73 = (bf16[32,16,256]{2,1,0:T(8,128)(2,1)S(1)}, bf16[512,2048]{1,0:T(8,128)(2,1)S(1)}) custom-call(f32[32,128]{1,0:T(8,128)} %alloc_ref.1, bf16[2048,256]{1,0:T(8,128)(2,1)} %bitcast.25), custom_call_target="tpu_custom_call" | custom-call | flops 536870912 | bytes 1048576 | tf_op jit(solution)/shard_map/pallas_call | solution.py:26
  8.1 0.0 collective-permute-done.72
  8.1 1.5 %collective-permute-done.71 = s32[1,12]{1,0:T(1,128)S(1)} collective-permute-done((s32[1,12]{1,0:T(1,128)}, s32[1,12]{1,0:T(1,128)S(1)}, u32[]{:S(2)}, u32[]{:S(2)}) %collective-permute-start.71) | collective-permute-done | bytes 80 | tf_op jit(solution)/shard_map/ppermute | solution.py:477
  9.6 0.0 collective-permute-done.70
  9.6 0.7 pad_add_fusion.refs_0_
  10.3 0.0 collective-permute-start.74
  10.3 0.1 pad_add_fusion.1
  10.4 1.5 %collective-permute-start.73 = (s32[4,12]{1,0:T(4,128)S(1)}, s32[4,12]{1,0:T(4,128)S(1)}, u32[]{:S(2)}, u32[]{:S(2)}) collective-permute-start(s32[4,12]{1,0:T(4,128)S(1)} %pad_add_fusion.refs_0_), channel_id=1, source_target_pairs={{0,16},{16,0},{1,17},{17,1},{2,18},{18,2},{3,19},{19,3},{4,20},{20... | collective-permute-start | bytes 584 | tf_op jit(solution)/shard_map/ppermute | solution.py:439
  11.9 4.1 %shard_map.75 = bf16[32,16,768]{2,1,0:T(8,128)(2,1)S(1)} custom-call(bf16[512,2048]{1,0:T(8,128)(2,1)S(1)} %get-tuple-element.283.refs_0_, bf16[2048,2048]{1,0:T(8,128)(2,1)} %bitcast.15, bf16[32,16,256]{2,1,0:T(8,128)(2,1)S(1)} %get-tuple-element.284.refs_2_), custom_call_target="tpu_custom_call" | custom-call | flops 1610612736 | bytes 3932160 | tf_op jit(solution)/shard_map/pallas_call | solution.py:26
  16.0 0.0 collective-permute-done.73.refs_1_
  16.0 0.8 shard_map.74
  17.4 0.0 collective-permute-done.74
  17.5 57.6 %conditional.1 = (bf16[16,1536]{1,0:T(8,128)(2,1)S(1)}, bf16[12,16,256]{2,1,0:T(8,128)(2,1)S(1)}, bf16[1536,256]{1,0:T(8,128)(2,1)}) conditional(s32[]{:T(128)} %bitcast.4, (s32[16,128]{1,0:T(8,128)S(1)}, bf16[32,16,768]{2,1,0:T(8,128)(2,1)S(1)}, bf16[32,16,256]{2,1,0:T(8,128)(2,1)S(1)}, ...), branch_computations={%region_0.0_spmd, %region_1.0_spmd, %region_2.0_spmd, %region_3.0_... | conditional | flops 9227468800 | bytes 82936392 | solution.py:551
  17.7 0.8 branch_1_fun.16
  18.5 2.1 %collective-permute-start.14 = (bf16[18,16,768]{2,1,0:T(8,128)(2,1)S(1)}, bf16[18,16,768]{2,1,0:T(8,128)(2,1)S(1)}, u32[]{:S(2)}, u32[]{:S(2)}) collective-permute-start(bf16[18,16,768]{2,1,0:T(8,128)(2,1)S(1)} %get-tuple-element.145), channel_id=1, source_target_pairs={{0,4},{4,0},{8,12},{12,8},{1,5},{5,1},{9,13},{13,9},{2,6},{6,2},{1... | collective-permute-start | bytes 1327112 | tf_op jit(solution)/shard_map/cond/branch_1_fun/ppermute | solution.py:443
  20.6 0.0 collective-permute-start.15
  20.6 4.1 %branch_1_fun.17 = (bf16[32,16,768]{2,1,0:T(8,128)(2,1)S(1)}, bf16[18,16,768]{2,1,0:T(8,128)(2,1)S(1)}) custom-call(s32[16,128]{1,0:T(8,128)S(1)} %get-tuple-element.138.tab_ref.refs_0_, bf16[512,2048]{1,0:T(8,128)(2,1)S(1)} %get-tuple-element.140.refs_1_, bf16[2048,2048]{1,0:T(8,128)(2,1)} %get-tuple-element.141.refs_2_), custom_call_target="tpu_custom_call" | custom-call | flops 1610612736 | bytes 3932160 | tf_op jit(solution)/shard_map/cond/branch_1_fun/pallas_call | solution.py:26
  24.7 2.6 %collective-permute-start.16 = (bf16[18,16,768]{2,1,0:T(8,128)(2,1)S(1)}, bf16[18,16,768]{2,1,0:T(8,128)(2,1)S(1)}, u32[]{:S(2)}, u32[]{:S(2)}) collective-permute-start(bf16[18,16,768]{2,1,0:T(8,128)(2,1)S(1)} %get-tuple-element.148.refs_0_), channel_id=1, source_target_pairs={{0,4},{4,0},{8,12},{12,8},{1,5},{5,1},{9,13},{13,9},{2,6},{6,2},{1... | collective-permute-start | bytes 1327112 | tf_op jit(solution)/shard_map/cond/branch_1_fun/ppermute | solution.py:443
  27.3 3.3 %branch_1_fun.18 = (bf16[512,256]{1,0:T(8,128)(2,1)S(1)}, bf16[512,256]{1,0:T(8,128)(2,1)S(1)}) custom-call(s32[2]{0:T(128)S(1)} %get-tuple-element.146.order_ref, bf16[1536,2048]{1,0:T(8,128)(2,1)S(1)} %get-tuple-element.139.tokens_ref, bf16[2048,1024]{1,0:T(8,128)(2,1)} %get-tuple-element.147.first_ref.second_ref, ...), custom_call_target="tpu_custom_call" | custom-call | flops 1073741824 | bytes 4718592 | tf_op jit(solution)/shard_map/cond/branch_1_fun/pallas_call | solution.py:362
  30.7 0.0 collective-permute-done.15.refs_3_.refs_6_.refs_5_
  30.7 0.0 collective-permute-done.14.refs_1_.refs_0_
  30.7 0.8 branch_1_fun.19
  31.5 0.1 collective-permute-start.17
  31.6 0.5 collective-permute-start.18
  32.1 2.9 %branch_1_fun.20 = (bf16[32,16,512]{2,1,0:T(8,128)(2,1)S(1)}, bf16[18,16,512]{2,1,0:T(8,128)(2,1)S(1)}) custom-call(s32[16,128]{1,0:T(8,128)S(1)} %get-tuple-element.138.tab_ref.refs_0_, bf16[512,2048]{1,0:T(8,128)(2,1)S(1)} %get-tuple-element.140.refs_1_, bf16[2048,2048]{1,0:T(8,128)(2,1)} %get-tuple-element.141.refs_2_, ...), custom_call_target="tpu_custom_call" | custom-call | flops 1073741824 | bytes 2621440 | tf_op jit(solution)/shard_map/cond/branch_1_fun/pallas_call | solution.py:26
  35.0 4.7 %branch_1_fun.21 = (bf16[1024,256]{1,0:T(8,128)(2,1)S(1)}, bf16[1024,256]{1,0:T(8,128)(2,1)S(1)}) custom-call(s32[2]{0:T(128)S(1)} %get-tuple-element.146.order_ref, bf16[1536,2048]{1,0:T(8,128)(2,1)S(1)} %get-tuple-element.139.tokens_ref, bf16[2048,1024]{1,0:T(8,128)(2,1)} %get-tuple-element.147.first_ref.second_ref, ...), custom_call_target="tpu_custom_call" | custom-call | flops 2147483648 | bytes 7340032 | tf_op jit(solution)/shard_map/cond/branch_1_fun/pallas_call | solution.py:362
  39.6 0.0 collective-permute-done.18.refs_7_.refs_1_
  39.6 0.0 collective-permute-done.17.refs_4_.refs_1_
  39.6 0.8 %branch_1_fun.22 = (bf16[16,16,768]{2,1,0:T(8,128)(2,1)S(1)}, bf16[22,16,512]{2,1,0:T(8,128)(2,1)S(1)}, bf16[1024,256]{1,0:T(8,128)(2,1)S(1)}) custom-call(s32[16,128]{1,0:T(8,128)S(1)} %get-tuple-element.138.tab_ref.refs_0_, bf16[32,16,768]{2,1,0:T(8,128)(2,1)S(1)} %get-tuple-element.154.refs_0_.refs_2_.own_ref, ...), custom_call_target="tpu_custom_call", output_to_operand_aliasing={{2}: (10, {})} | custom-call | bytes 2260992 | tf_op jit(solution)/shard_map/cond/branch_1_fun/pallas_call | solution.py:26
  40.5 0.1 collective-permute-start.22
  40.6 0.4 collective-permute-start.20
  41.1 4.1 %collective-permute-start.19 = (bf16[22,16,512]{2,1,0:T(8,128)(2,1)S(1)}, bf16[22,16,512]{2,1,0:T(8,128)(2,1)S(1)}, u32[]{:S(2)}, u32[]{:S(2)}) collective-permute-start(bf16[22,16,512]{2,1,0:T(8,128)(2,1)S(1)} %get-tuple-element.159), channel_id=1, source_target_pairs={{0,4},{4,0},{8,12},{12,8},{1,5},{5,1},{9,13},{13,9},{2,6},{6,2},{1... | collective-permute-start | bytes 1081352 | tf_op jit(solution)/shard_map/cond/branch_1_fun/ppermute | solution.py:443
  45.1 0.1 branch_1_fun.23.refs_0_
  45.2 1.6 %collective-permute-start.21 = (bf16[512,256]{1,0:T(8,128)(2,1)S(1)}, bf16[512,256]{1,0:T(8,128)(2,1)S(1)}, u32[]{:S(2)}, u32[]{:S(2)}) collective-permute-start(bf16[512,256]{1,0:T(8,128)(2,1)S(1)} %branch_1_fun.23.refs_0_), channel_id=1, source_target_pairs={{0,1},{1,0},{2,3},{3,2},{4,5},{5,4},{6,7},{7,6},{8,9},{9,8},{10,11... | collective-permute-start | bytes 786440 | tf_op jit(solution)/shard_map/cond/branch_1_fun/ppermute | solution.py:439
  46.8 5.9 %branch_1_fun.24 = (bf16[1536,256]{1,0:T(8,128)(2,1)S(1)}, bf16[1536,256]{1,0:T(8,128)(2,1)S(1)}) custom-call(s32[2]{0:T(128)S(1)} %get-tuple-element.161.order_ref, bf16[1536,2048]{1,0:T(8,128)(2,1)S(1)} %get-tuple-element.139.tokens_ref, bf16[2048,1024]{1,0:T(8,128)(2,1)} %get-tuple-element.147.first_ref.second_ref, ...), custom_call_target="tpu_custom_call" | custom-call | flops 3221225472 | bytes 9961472 | tf_op jit(solution)/shard_map/cond/branch_1_fun/pallas_call | solution.py:362
  52.7 0.0 collective-permute-done.22.refs_1_
  52.7 0.1 branch_1_fun.25.refs_7_
  52.8 0.5 collective-permute-done.21.refs_4_.refs_2_
  53.3 0.5 collective-permute-done.19.refs_1_.refs_2_.refs_6_.refs_0_
  53.8 0.9 %branch_1_fun.26 = (bf16[16,16,512]{2,1,0:T(8,128)(2,1)S(1)}, bf16[11,16,768]{2,1,0:T(8,128)(2,1)S(1)}, bf16[1536,256]{1,0:T(8,128)(2,1)S(1)}, bf16[1024,256]{1,0:T(8,128)(2,1)S(1)}) custom-call(s32[16,128]{1,0:T(8,128)S(1)} %get-tuple-element.138.tab_ref.refs_0_, ...), custom_call_target="tpu_custom_call", output_to_operand_aliasing={{2}: (7, {}), {3}: (8, {})} | custom-call | bytes 1597440 | tf_op jit(solution)/shard_map/cond/branch_1_fun/pallas_call | solution.py:26
  54.7 0.1 collective-permute-start.24
  54.8 1.6 %collective-permute-start.27 = (bf16[1024,256]{1,0:T(8,128)(2,1)S(1)}, bf16[1024,256]{1,0:T(8,128)(2,1)S(1)}, u32[]{:S(2)}, u32[]{:S(2)}) collective-permute-start(bf16[1024,256]{1,0:T(8,128)(2,1)S(1)} %get-tuple-element.169), channel_id=1, source_target_pairs={{0,1},{1,0},{2,3},{3,2},{4,5},{5,4},{6,7},{7,6},{8,9},{9,8},{10,11... | collective-permute-start | bytes 1572872 | tf_op jit(solution)/shard_map/cond/branch_1_fun/ppermute | solution.py:439
  56.3 0.2 collective-permute-start.23
  56.5 1.3 %collective-permute-start.26 = (bf16[11,16,768]{2,1,0:T(8,128)(2,1)S(1)}, bf16[11,16,768]{2,1,0:T(8,128)(2,1)S(1)}, u32[]{:S(2)}, u32[]{:S(2)}) collective-permute-start(bf16[11,16,768]{2,1,0:T(8,128)(2,1)S(1)} %get-tuple-element.168), channel_id=1, source_target_pairs={{4,0},{8,12},{5,1},{9,13},{6,2},{10,14},{7,3},{11,15},{20,16},{24,... | collective-permute-start | bytes 811016 | tf_op jit(solution)/shard_map/cond/branch_1_fun/ppermute | solution.py:451
  57.8 1.6 %branch_1_fun.27 = (f32[16,1536]{1,0:T(8,128)S(1)}, bf16[12,16,256]{2,1,0:T(8,128)(2,1)S(1)}) custom-call(s32[16,128]{1,0:T(8,128)S(1)} %get-tuple-element.138.tab_ref.refs_0_, bf16[1536,2048]{1,0:T(8,128)(2,1)S(1)} %get-tuple-element.139.tokens_ref, bf16[32,16,768]{2,1,0:T(8,128)(2,1)S(1)} %get-tuple-element.142.refs_0_.refs_3_.own_ref, ...), custom_call_target="tpu_custom_call" | custom-call | flops 37748736 | bytes 3932160 | tf_op jit(solution)/shard_map/cond/branch_1_fun/pallas_call | solution.py:26
  59.4 0.0 collective-permute-done.23.refs_1_
  59.4 0.0 collective-permute-done.24.refs_3_.refs_1_
  59.4 0.8 branch_1_fun.28.refs_4_
  60.2 1.3 %collective-permute-start.25 = (bf16[11,16,512]{2,1,0:T(8,128)(2,1)S(1)}, bf16[11,16,512]{2,1,0:T(8,128)(2,1)S(1)}, u32[]{:S(2)}, u32[]{:S(2)}) collective-permute-start(bf16[11,16,512]{2,1,0:T(8,128)(2,1)S(1)} %branch_1_fun.28.refs_4_), channel_id=1, source_target_pairs={{4,0},{8,12},{5,1},{9,13},{6,2},{10,14},{7,3},{11,15},{20,16},{24,... | collective-permute-start | bytes 540680 | tf_op jit(solution)/shard_map/cond/branch_1_fun/ppermute | solution.py:451
  61.5 6.0 %collective-permute-done.26.refs_2_ = bf16[11,16,768]{2,1,0:T(8,128)(2,1)S(1)} collective-permute-done((bf16[11,16,768]{2,1,0:T(8,128)(2,1)S(1)}, bf16[11,16,768]{2,1,0:T(8,128)(2,1)S(1)}, u32[]{:S(2)}, u32[]{:S(2)}) %collective-permute-start.26) | collective-permute-done | bytes 270368 | tf_op jit(solution)/shard_map/cond/branch_1_fun/ppermute | solution.py:451
  67.5 1.6 %branch_1_fun.29.refs_4_.refs_3_ = f32[16,1536]{1,0:T(8,128)S(1)} custom-call(s32[16,128]{1,0:T(8,128)S(1)} %get-tuple-element.138.tab_ref.refs_0_, bf16[1536,2048]{1,0:T(8,128)(2,1)S(1)} %get-tuple-element.139.tokens_ref, bf16[32,16,768]{2,1,0:T(8,128)(2,1)S(1)} %get-tuple-element.154.refs_0_.refs_2_.own_ref, ...), custom_call_target="tpu_custom_call" | custom-call | flops 37748736 | bytes 3932160 | tf_op jit(solution)/shard_map/cond/branch_1_fun/pallas_call | solution.py:26
  69.2 0.0 collective-permute-done.27.refs_3_
  69.2 1.2 %branch_1_fun.30.refs_4_ = bf16[1536,256]{1,0:T(8,128)(2,1)} custom-call(bf16[1536,256]{1,0:T(8,128)(2,1)S(1)} %get-tuple-element.162.refs_5_.refs_0_, bf16[1536,256]{1,0:T(8,128)(2,1)S(1)} %collective-permute-done.24.refs_3_.refs_1_, bf16[512,256]{1,0:T(8,128)(2,1)S(1)} %collective-permute-done.21.refs_4_.refs_2_, ...), custom_call_target="tpu_custom_call" | custom-call | bytes 3145728 | tf_op jit(solution)/shard_map/cond/branch_1_fun/pallas_call | solution.py:26
  70.4 2.8 %collective-permute-done.25.refs_2_ = bf16[11,16,512]{2,1,0:T(8,128)(2,1)S(1)} collective-permute-done((bf16[11,16,512]{2,1,0:T(8,128)(2,1)S(1)}, bf16[11,16,512]{2,1,0:T(8,128)(2,1)S(1)}, u32[]{:S(2)}, u32[]{:S(2)}) %collective-permute-start.25) | collective-permute-done | bytes 180256 | tf_op jit(solution)/shard_map/cond/branch_1_fun/ppermute | solution.py:451
  73.2 1.4 %branch_1_fun.31 = bf16[16,1536]{1,0:T(8,128)(2,1)S(1)} custom-call(s32[16,128]{1,0:T(8,128)S(1)} %get-tuple-element.138.tab_ref.refs_0_, bf16[1536,2048]{1,0:T(8,128)(2,1)S(1)} %get-tuple-element.139.tokens_ref, bf16[32,16,512]{2,1,0:T(8,128)(2,1)S(1)} %get-tuple-element.153.refs_0_.own_ref, ...), custom_call_target="tpu_custom_call" | custom-call | flops 25165824 | bytes 2621440 | tf_op jit(solution)/shard_map/cond/branch_1_fun/pallas_call | solution.py:26
  75.1 0.1 collective-permute-start.77
  75.1 0.6 collective-permute-start.76
  75.8 1.2 %collective-permute-start.75 = (bf16[16,1536]{1,0:T(8,128)(2,1)S(1)}, bf16[16,1536]{1,0:T(8,128)(2,1)S(1)}, u32[]{:S(2)}, u32[]{:S(2)}) collective-permute-start(bf16[16,1536]{1,0:T(8,128)(2,1)S(1)} %get-tuple-element.286.refs_0_), channel_id=1, source_target_pairs={{0,2},{2,0},{1,3},{3,1},{4,6},{6,4},{5,7},{7,5},{8,10},{10,8},{9,1... | collective-permute-start | bytes 147464 | tf_op jit(solution)/shard_map/ppermute | solution.py:439
  77.0 1.7 %collective-permute-done.77.refs_3_ = bf16[16,1536]{1,0:T(8,128)(2,1)S(1)} collective-permute-done((bf16[16,1536]{1,0:T(8,128)(2,1)S(1)}, bf16[16,1536]{1,0:T(8,128)(2,1)S(1)}, u32[]{:S(2)}, u32[]{:S(2)}) %collective-permute-start.77) | collective-permute-done | bytes 49184 | tf_op jit(solution)/shard_map/ppermute | solution.py:553
  78.6 1.1 %collective-permute-done.76.refs_2_ = bf16[16,1536]{1,0:T(8,128)(2,1)S(1)} collective-permute-done((bf16[16,1536]{1,0:T(8,128)(2,1)S(1)}, bf16[16,1536]{1,0:T(8,128)(2,1)S(1)}, u32[]{:S(2)}, u32[]{:S(2)}) %collective-permute-start.76) | collective-permute-done | bytes 49184 | tf_op jit(solution)/shard_map/ppermute | solution.py:439
  79.7 2.4 %shard_map.76 = bf16[1536,256]{1,0:T(8,128)(2,1)} custom-call(s32[16,128]{1,0:T(8,128)S(1)} %get-tuple-element.281.tab_ref, bf16[12,16,256]{2,1,0:T(8,128)(2,1)S(1)} %get-tuple-element.285.up_ref, bf16[16,1536]{1,0:T(8,128)(2,1)S(1)} %get-tuple-element.286.refs_0_, bf16[16,1536]{1,0:T(8,128)(2,1)S(1)} %collective-permute-done.75.refs_1_, ...), custom_call_target="tpu_custom_call" | custom-call | flops 12582912 | bytes 1572864 | tf_op jit(solution)/shard_map/pallas_call | solution.py:26
  (10 shorter events, 0.0 us)
Async XLA Ops:
  0.0 8.1 %collective-permute-start.72 = (s32[1,12]{1,0:T(1,128)}, s32[1,12]{1,0:T(1,128)S(1)}, u32[]{:S(2)}, u32[]{:S(2)}) collective-permute-start(s32[1,12]{1,0:T(1,128)} %bitcast.21), channel_id=1, source_target_pairs={{0,12},{4,8},{8,4},{12,0},{1,13},{5,9},{9,5},{13,1},{2,14},{6,10},... | collective-permute-start | bytes 152 | tf_op jit(solution)/shard_map/ppermute | solution.py:477
  5.0 4.6 %collective-permute-start.71 = (s32[1,12]{1,0:T(1,128)}, s32[1,12]{1,0:T(1,128)S(1)}, u32[]{:S(2)}, u32[]{:S(2)}) collective-permute-start(s32[1,12]{1,0:T(1,128)} %bitcast.22), channel_id=1, source_target_pairs={{0,8},{4,12},{8,0},{12,4},{1,9},{5,13},{9,1},{13,5},{2,10},{6,14},... | collective-permute-start | bytes 152 | tf_op jit(solution)/shard_map/ppermute | solution.py:477
  5.1 4.6 %collective-permute-start.70 = (s32[1,12]{1,0:T(1,128)}, s32[1,12]{1,0:T(1,128)S(1)}, u32[]{:S(2)}, u32[]{:S(2)}) collective-permute-start(s32[1,12]{1,0:T(1,128)} %bitcast.23), channel_id=1, source_target_pairs={{0,4},{4,0},{8,12},{12,8},{1,5},{5,1},{9,13},{13,9},{2,6},{6,2},{1... | collective-permute-start | bytes 152 | tf_op jit(solution)/shard_map/ppermute | solution.py:477
  5.6 10.4 %copy-start = (s32[12]{0:T(128)S(1)}, s32[12]{0:T(128)}, u32[]{:S(2)}) copy-start(s32[12]{0:T(128)} %param.18) | copy-start | bytes 148
  5.6 11.8 %slice-start = ((s8[6291456]{0:T(1024)(128)(4,1)}), s8[4194304]{0:T(1024)(128)(4,1)S(1)}, s32[]{:S(2)}) async-start(s8[6291456]{0:T(1024)(128)(4,1)} %bitcast.13), calls=%async_computation | async-start | bytes 8388608
  10.3 7.1 %collective-permute-start.74 = (bf16[32,16,256]{2,1,0:T(8,128)(2,1)S(1)}, bf16[32,16,256]{2,1,0:T(8,128)(2,1)S(1)}, u32[]{:S(2)}, u32[]{:S(2)}) collective-permute-start(bf16[32,16,256]{2,1,0:T(8,128)(2,1)S(1)} %get-tuple-element.284.refs_2_), channel_id=1, source_target_pairs={{0,4},{4,0},{8,12},{12,8},{1,5},{5,1},{9,13},{13,9},{2,6},{6,2},{1... | collective-permute-start | bytes 786440 | tf_op jit(solution)/shard_map/ppermute | solution.py:443
  10.4 5.6 %collective-permute-start.73 = (s32[4,12]{1,0:T(4,128)S(1)}, s32[4,12]{1,0:T(4,128)S(1)}, u32[]{:S(2)}, u32[]{:S(2)}) collective-permute-start(s32[4,12]{1,0:T(4,128)S(1)} %pad_add_fusion.refs_0_), channel_id=1, source_target_pairs={{0,16},{16,0},{1,17},{17,1},{2,18},{18,2},{3,19},{19,3},{4,20},{20... | collective-permute-start | bytes 584 | tf_op jit(solution)/shard_map/ppermute | solution.py:439
  11.9 5.5 %slice-start.1 = ((s8[6291456]{0:T(1024)(128)(4,1)}), s8[2097152]{0:T(1024)(128)(4,1)S(1)}, s32[]{:S(2)}) async-start(s8[6291456]{0:T(1024)(128)(4,1)} %bitcast.13), calls=%async_computation.1 | async-start | bytes 4194304
  18.5 12.2 %collective-permute-start.14 = (bf16[18,16,768]{2,1,0:T(8,128)(2,1)S(1)}, bf16[18,16,768]{2,1,0:T(8,128)(2,1)S(1)}, u32[]{:S(2)}, u32[]{:S(2)}) collective-permute-start(bf16[18,16,768]{2,1,0:T(8,128)(2,1)S(1)} %get-tuple-element.145), channel_id=1, source_target_pairs={{0,4},{4,0},{8,12},{12,8},{1,5},{5,1},{9,13},{13,9},{2,6},{6,2},{1... | collective-permute-start | bytes 1327112 | tf_op jit(solution)/shard_map/cond/branch_1_fun/ppermute | solution.py:443
  20.6 10.1 %collective-permute-start.15 = (bf16[16,16,256]{2,1,0:T(8,128)(2,1)S(1)}, bf16[16,16,256]{2,1,0:T(8,128)(2,1)S(1)}, u32[]{:S(2)}, u32[]{:S(2)}) collective-permute-start(bf16[16,16,256]{2,1,0:T(8,128)(2,1)S(1)} %get-tuple-element.150), channel_id=1, source_target_pairs={{4,8},{6,10},{0,2},{12,14},{8,4},{10,6},{2,0},{14,12},{5,9},{7,11}... | collective-permute-start | bytes 393224 | tf_op jit(solution)/shard_map/cond/branch_1_fun/ppermute | solution.py:456
  24.7 15.0 %collective-permute-start.16 = (bf16[18,16,768]{2,1,0:T(8,128)(2,1)S(1)}, bf16[18,16,768]{2,1,0:T(8,128)(2,1)S(1)}, u32[]{:S(2)}, u32[]{:S(2)}) collective-permute-start(bf16[18,16,768]{2,1,0:T(8,128)(2,1)S(1)} %get-tuple-element.148.refs_0_), channel_id=1, source_target_pairs={{0,4},{4,0},{8,12},{12,8},{1,5},{5,1},{9,13},{13,9},{2,6},{6,2},{1... | collective-permute-start | bytes 1327112 | tf_op jit(solution)/shard_map/cond/branch_1_fun/ppermute | solution.py:443
  31.5 8.1 %collective-permute-start.17 = (bf16[16,16,768]{2,1,0:T(8,128)(2,1)S(1)}, bf16[16,16,768]{2,1,0:T(8,128)(2,1)S(1)}, u32[]{:S(2)}, u32[]{:S(2)}) collective-permute-start(bf16[16,16,768]{2,1,0:T(8,128)(2,1)S(1)} %get-tuple-element.152.refs_3_), channel_id=1, source_target_pairs={{4,8},{6,10},{0,2},{12,14},{8,4},{10,6},{2,0},{14,12},{5,9},{7,11}... | collective-permute-start | bytes 1179656 | tf_op jit(solution)/shard_map/cond/branch_1_fun/ppermute | solution.py:456
  31.6 8.1 %collective-permute-start.18 = (bf16[512,256]{1,0:T(8,128)(2,1)S(1)}, bf16[512,256]{1,0:T(8,128)(2,1)S(1)}, u32[]{:S(2)}, u32[]{:S(2)}) collective-permute-start(bf16[512,256]{1,0:T(8,128)(2,1)S(1)} %get-tuple-element.156), channel_id=1, source_target_pairs={{0,2},{2,0},{1,3},{3,1},{4,6},{6,4},{5,7},{7,5},{8,10},{10,8},{9,1... | collective-permute-start | bytes 786440 | tf_op jit(solution)/shard_map/cond/branch_1_fun/ppermute | solution.py:439
  40.5 12.2 %collective-permute-start.22 = (bf16[1024,256]{1,0:T(8,128)(2,1)S(1)}, bf16[1024,256]{1,0:T(8,128)(2,1)S(1)}, u32[]{:S(2)}, u32[]{:S(2)}) collective-permute-start(bf16[1024,256]{1,0:T(8,128)(2,1)S(1)} %get-tuple-element.164), channel_id=1, source_target_pairs={{0,2},{2,0},{1,3},{3,1},{4,6},{6,4},{5,7},{7,5},{8,10},{10,8},{9,1... | collective-permute-start | bytes 1572872 | tf_op jit(solution)/shard_map/cond/branch_1_fun/ppermute | solution.py:439
  40.6 13.2 %collective-permute-start.20 = (bf16[16,16,768]{2,1,0:T(8,128)(2,1)S(1)}, bf16[16,16,768]{2,1,0:T(8,128)(2,1)S(1)}, u32[]{:S(2)}, u32[]{:S(2)}) collective-permute-start(bf16[16,16,768]{2,1,0:T(8,128)(2,1)S(1)} %get-tuple-element.160.refs_2_), channel_id=1, source_target_pairs={{4,8},{6,10},{0,2},{12,14},{8,4},{10,6},{2,0},{14,12},{5,9},{7,11}... | collective-permute-start | bytes 1179656 | tf_op jit(solution)/shard_map/cond/branch_1_fun/ppermute | solution.py:456
  41.1 12.7 %collective-permute-start.19 = (bf16[22,16,512]{2,1,0:T(8,128)(2,1)S(1)}, bf16[22,16,512]{2,1,0:T(8,128)(2,1)S(1)}, u32[]{:S(2)}, u32[]{:S(2)}) collective-permute-start(bf16[22,16,512]{2,1,0:T(8,128)(2,1)S(1)} %get-tuple-element.159), channel_id=1, source_target_pairs={{0,4},{4,0},{8,12},{12,8},{1,5},{5,1},{9,13},{13,9},{2,6},{6,2},{1... | collective-permute-start | bytes 1081352 | tf_op jit(solution)/shard_map/cond/branch_1_fun/ppermute | solution.py:443
  45.2 8.1 %collective-permute-start.21 = (bf16[512,256]{1,0:T(8,128)(2,1)S(1)}, bf16[512,256]{1,0:T(8,128)(2,1)S(1)}, u32[]{:S(2)}, u32[]{:S(2)}) collective-permute-start(bf16[512,256]{1,0:T(8,128)(2,1)S(1)} %branch_1_fun.23.refs_0_), channel_id=1, source_target_pairs={{0,1},{1,0},{2,3},{3,2},{4,5},{5,4},{6,7},{7,6},{8,9},{9,8},{10,11... | collective-permute-start | bytes 786440 | tf_op jit(solution)/shard_map/cond/branch_1_fun/ppermute | solution.py:439
  54.7 4.7 %collective-permute-start.24 = (bf16[1536,256]{1,0:T(8,128)(2,1)S(1)}, bf16[1536,256]{1,0:T(8,128)(2,1)S(1)}, u32[]{:S(2)}, u32[]{:S(2)}) collective-permute-start(bf16[1536,256]{1,0:T(8,128)(2,1)S(1)} %get-tuple-element.167), channel_id=1, source_target_pairs={{0,2},{2,0},{1,3},{3,1},{4,6},{6,4},{5,7},{7,5},{8,10},{10,8},{9,1... | collective-permute-start | bytes 2359304 | tf_op jit(solution)/shard_map/cond/branch_1_fun/ppermute | solution.py:439
  54.8 14.4 %collective-permute-start.27 = (bf16[1024,256]{1,0:T(8,128)(2,1)S(1)}, bf16[1024,256]{1,0:T(8,128)(2,1)S(1)}, u32[]{:S(2)}, u32[]{:S(2)}) collective-permute-start(bf16[1024,256]{1,0:T(8,128)(2,1)S(1)} %get-tuple-element.169), channel_id=1, source_target_pairs={{0,1},{1,0},{2,3},{3,2},{4,5},{5,4},{6,7},{7,6},{8,9},{9,8},{10,11... | collective-permute-start | bytes 1572872 | tf_op jit(solution)/shard_map/cond/branch_1_fun/ppermute | solution.py:439
  56.3 3.1 %collective-permute-start.23 = (bf16[16,16,512]{2,1,0:T(8,128)(2,1)S(1)}, bf16[16,16,512]{2,1,0:T(8,128)(2,1)S(1)}, u32[]{:S(2)}, u32[]{:S(2)}) collective-permute-start(bf16[16,16,512]{2,1,0:T(8,128)(2,1)S(1)} %get-tuple-element.165.refs_7_), channel_id=1, source_target_pairs={{4,8},{6,10},{0,2},{12,14},{8,4},{10,6},{2,0},{14,12},{5,9},{7,11}... | collective-permute-start | bytes 786440 | tf_op jit(solution)/shard_map/cond/branch_1_fun/ppermute | solution.py:456
  56.5 11.0 %collective-permute-start.26 = (bf16[11,16,768]{2,1,0:T(8,128)(2,1)S(1)}, bf16[11,16,768]{2,1,0:T(8,128)(2,1)S(1)}, u32[]{:S(2)}, u32[]{:S(2)}) collective-permute-start(bf16[11,16,768]{2,1,0:T(8,128)(2,1)S(1)} %get-tuple-element.168), channel_id=1, source_target_pairs={{4,0},{8,12},{5,1},{9,13},{6,2},{10,14},{7,3},{11,15},{20,16},{24,... | collective-permute-start | bytes 811016 | tf_op jit(solution)/shard_map/cond/branch_1_fun/ppermute | solution.py:451
  60.2 13.0 %collective-permute-start.25 = (bf16[11,16,512]{2,1,0:T(8,128)(2,1)S(1)}, bf16[11,16,512]{2,1,0:T(8,128)(2,1)S(1)}, u32[]{:S(2)}, u32[]{:S(2)}) collective-permute-start(bf16[11,16,512]{2,1,0:T(8,128)(2,1)S(1)} %branch_1_fun.28.refs_4_), channel_id=1, source_target_pairs={{4,0},{8,12},{5,1},{9,13},{6,2},{10,14},{7,3},{11,15},{20,16},{24,... | collective-permute-start | bytes 540680 | tf_op jit(solution)/shard_map/cond/branch_1_fun/ppermute | solution.py:451
  75.1 3.6 %collective-permute-start.77 = (bf16[16,1536]{1,0:T(8,128)(2,1)S(1)}, bf16[16,1536]{1,0:T(8,128)(2,1)S(1)}, u32[]{:S(2)}, u32[]{:S(2)}) collective-permute-start(bf16[16,1536]{1,0:T(8,128)(2,1)S(1)} %get-tuple-element.286.refs_0_), channel_id=1, source_target_pairs={{0,3},{1,2},{2,1},{3,0},{4,7},{5,6},{6,5},{7,4},{8,11},{9,10},{10,... | collective-permute-start | bytes 147464 | tf_op jit(solution)/shard_map/ppermute | solution.py:553
  75.1 4.6 %collective-permute-start.76 = (bf16[16,1536]{1,0:T(8,128)(2,1)S(1)}, bf16[16,1536]{1,0:T(8,128)(2,1)S(1)}, u32[]{:S(2)}, u32[]{:S(2)}) collective-permute-start(bf16[16,1536]{1,0:T(8,128)(2,1)S(1)} %get-tuple-element.286.refs_0_), channel_id=1, source_target_pairs={{0,1},{1,0},{2,3},{3,2},{4,5},{5,4},{6,7},{7,6},{8,9},{9,8},{10,11... | collective-permute-start | bytes 147464 | tf_op jit(solution)/shard_map/ppermute | solution.py:439
  75.8 4.0 %collective-permute-start.75 = (bf16[16,1536]{1,0:T(8,128)(2,1)S(1)}, bf16[16,1536]{1,0:T(8,128)(2,1)S(1)}, u32[]{:S(2)}, u32[]{:S(2)}) collective-permute-start(bf16[16,1536]{1,0:T(8,128)(2,1)S(1)} %get-tuple-element.286.refs_0_), channel_id=1, source_target_pairs={{0,2},{2,0},{1,3},{3,1},{4,6},{6,4},{5,7},{7,5},{8,10},{10,8},{9,1... | collective-permute-start | bytes 147464 | tf_op jit(solution)/shard_map/ppermute | solution.py:439
